TPU v7x, 32 devices: a whole 2x2x4 slice. The times are simulated.
32 devices in a mesh: row: 4 (over y, x), col: 8 (over z, core).
Axes of the slice: x: 2, y: 2, z: 4, core: 2. Of those that a mesh axis runs over, the one named last changes fastest.
Arguments:
- state: float32 [3, 10, 131072], P(None, None, ('row', 'col')), may hold values from -6 to 6
- depth: float32 [131072], P(('row', 'col')), may hold values from 1 to 18
- metric: float32 [4, 131072], P(None, ('row', 'col')), may hold values from -4 to 4, as said below
- partner: int32 [131072], P(('row', 'col')), may hold values from -63 to 63, as said below
- refine: int32 [131072], P(('row', 'col')), may hold values from 0 to 1, as said below
- diff_ops: float32 [2, 10, 10], replicated, may hold values from -2 to 2
- lift: float32 [10, 12], replicated, may hold values from -1.75 to 1.75
- prolong: float32 [2, 10, 10], replicated, may hold values from -2 to 2
Outputs:
- refined: float32 [3, 10, 196608], P(None, None, ('row', 'col'))
Inputs may be any that keep to these rules, and one draw needn't show every extreme that they name: `metric`: (r_x, r_y) and (s_x, s_y) are orthogonal and of equal length, between 1 and 4. Where partner[i] is not 0, j = i + partner[i] is a triangle with partner[j] = -partner[i]; an offset of size 63 occurs in every draw. `refine`: split the curve into sections of 4096 consecutive triangles. The refinements before section k number k * 2048 plus an offset between -1024 and 1024, and both ends of that range occur in every draw; all refinements together number 131072 / 2.
All inputs are finite; a program needn't handle non-finite values.
Results may differ from a plain program's by a relative error of at most 0.000076.
Values sent between devices are 32-bit elements; how exact they have to be, the bound alone decides.
No kernel may reach another device: no remote copies, remote signals or barrier semaphores. Data moves between devices by JAX's collectives and lax.ppermute only.
A program may use at most 64 MiB of HBM per device.

v0:
```python
import functools

import jax
import jax.numpy as jnp
from jax import lax
from jax.experimental import pallas as pl
from jax.experimental.pallas import tpu as pltpu
from jax.sharding import PartitionSpec as P

GRAVITY = 9.81
COURANT = 0.5
HIGH = lax.Precision.HIGHEST
LANES = 128
AXES = ("row", "col")
FACES = ((0, 1, 2, 3), (3, 6, 8, 9), (9, 7, 4, 0))
PACK = 40
WIDE = 32
PAD = 8

VMEM = pl.BlockSpec(memory_space=pltpu.VMEM)
HBM = pl.BlockSpec(memory_space=pltpu.HBM)
PARAMS = pltpu.CompilerParams(vmem_limit_bytes=48 * 1024 * 1024)


class Sizes:
    def __init__(self, cells):
        self.cells = cells
        self.blocks = cells // LANES
        self.margin = cells // 4 // LANES
        self.halo = self.margin + 1
        self.rows = -(-(self.blocks + 2 * self.halo) // 8) * 8
        self.tall = self.rows + 2 * PAD
        self.slots = 3 * self.blocks // 2
        self.keep = self.halo - self.margin


def fetch_all(pairs, sems):
    copies = [pltpu.make_async_copy(src, dst, sems.at[num]) for num, (src, dst) in enumerate(pairs)]
    for copy in copies:
        copy.start()
    return copies


def split_metric(metric_ref, spread, blocks):
    for block in range(blocks):
        spread[8 * block : 8 * block + 4, :] = metric_ref[:, LANES * block : LANES * (block + 1)]
    return [spread[pl.ds(comp, blocks, stride=8), :] for comp in range(4)]


def pack_kernel(
    sizes, state_hbm, depth_hbm, metric_hbm, partner_hbm, refine_hbm, stats_ref, head_ref, tail_ref,
    state_head, state_tail, depth_ref, metric_ref, partner_ref, refine_ref, spread, sems,
):
    blocks, halo = sizes.blocks, sizes.halo
    wide = LANES * halo
    copies = fetch_all(
        (
            (depth_hbm, depth_ref),
            (metric_hbm, metric_ref),
            (refine_hbm, refine_ref),
            (partner_hbm, partner_ref),
            (state_hbm.at[:, :, 0:wide], state_head),
            (state_hbm.at[:, :, sizes.cells - wide : sizes.cells], state_tail),
        ),
        sems,
    )
    for copy in copies:
        copy.wait()
    rx, ry, sx, sy = split_metric(metric_ref, spread, blocks)
    depth = depth_ref[...]
    refine = refine_ref[...].astype(jnp.float32)
    faces = ((sx, sy), (rx + sx, ry + sy), (rx, ry))
    lengths = [jnp.sqrt(vx * vx + vy * vy) for vx, vy in faces]
    rate = jnp.sqrt(GRAVITY * depth) * jnp.maximum(jnp.maximum(lengths[0], lengths[1]), lengths[2])
    top = jnp.max(jnp.max(rate, axis=0, keepdims=True), axis=1, keepdims=True)
    extra = jnp.sum(jnp.sum(refine, axis=0, keepdims=True), axis=1, keepdims=True)
    shape = stats_ref.shape
    lane = lax.broadcasted_iota(jnp.int32, shape, 1)
    stats_ref[...] = jnp.where(
        lane < LANES // 2, jnp.broadcast_to(top, shape), jnp.broadcast_to(extra, shape)
    )
    partner = partner_ref[...].astype(jnp.float32)
    for ref, source, start in ((head_ref, state_head, 0), (tail_ref, state_tail, blocks - halo)):
        pack_state(source, ref, halo)
        for num, dense in enumerate((depth, rx, ry, sx, sy, partner, refine)):
            ref[pl.ds(4 * num + 3, halo, stride=PACK), :] = dense[start : start + halo]


def pack_state(source, target, blocks):
    for block in range(blocks):
        for node in range(10):
            at = PACK * block + 4 * node
            target[at : at + 3, :] = source[node, :, LANES * block : LANES * (block + 1)]


def pair_index(partner):
    lane = lax.broadcasted_iota(jnp.int32, partner.shape, 1)
    target = lane + partner.astype(jnp.int32)
    return target & (LANES - 1), (target >= 0) & (target < LANES)


def lane_gather(values, index):
    return jnp.take_along_axis(values, index, axis=1, mode="promise_in_bounds")


def outer_values(load, index, inside):
    shape = index.shape
    lane = lax.broadcasted_iota(jnp.int32, shape, 1)

    def prev(item):
        return pltpu.roll(jnp.where(lane == LANES - 1, load(item, -1), load(item, 0)), 1, 1)

    def after(item):
        return pltpu.roll(jnp.where(lane == 0, load(item, 1), load(item, 0)), LANES - 1, 1)

    def across(item):
        other = jnp.where(lane < LANES // 2, load(item, 1), load(item, -1))
        return jnp.where(inside, lane_gather(load(item, 0), index), lane_gather(other, index))

    return prev, after, across


def wall_masks(sizes, start, place, count, partner):
    shape = partner.shape
    lane = lax.broadcasted_iota(jnp.int32, shape, 1)
    row = lax.broadcasted_iota(jnp.int32, shape, 0) + start
    first = (lane == 0) & (row == sizes.halo) & (place == 0)
    last = (lane == LANES - 1) & (row == sizes.halo + sizes.blocks - 1) & (place == count - 1)
    return first, last, partner == 0


def tendency(load, geo, walls, index, inside, diff_ref, lift_ref):
    speed_sq, rx, ry, sx, sy = geo[:5]
    outer_sq, waves, ghosts = geo[5:8], geo[8:11], geo[11:14]
    own = [[load(10 * field + node, 0) for node in range(10)] for field in range(3)]
    eta, mom_x, mom_y = own
    flow_r = [-(rx * mom_x[b] + ry * mom_y[b]) for b in range(10)]
    flow_s = [-(sx * mom_x[b] + sy * mom_y[b]) for b in range(10)]
    half_r = (0.5 * rx, 0.5 * ry)
    half_s = (0.5 * sx, 0.5 * sy)
    vectors = (
        (-half_s[0], -half_s[1]),
        (half_r[0] + half_s[0], half_r[1] + half_s[1]),
        (-half_r[0], -half_r[1]),
    )
    fetch = outer_values(load, index, inside)
    jumps = ([], [], [])
    for face in range(3):
        vec_x, vec_y = vectors[face]
        theirs = FACES[(1, 0, 2)[face]]
        wall = walls[face]
        for j in range(4):
            node, match = FACES[face][j], theirs[3 - j]
            in_eta, in_x, in_y = eta[node], mom_x[node], mom_y[node]
            ext_eta, ext_x, ext_y = [fetch[face](10 * field + match) for field in range(3)]
            bounce = (in_x * vec_x + in_y * vec_y) * ghosts[face]
            d_eta = jnp.where(wall, 0.0, in_eta - ext_eta)
            d_x = jnp.where(wall, bounce * vec_x, in_x - ext_x)
            d_y = jnp.where(wall, bounce * vec_y, in_y - ext_y)
            head = jnp.where(wall, 0.0, speed_sq * in_eta - outer_sq[face] * ext_eta)
            jumps[0].append(d_x * vec_x + d_y * vec_y - waves[face] * d_eta)
            jumps[1].append(head * vec_x - waves[face] * d_x)
            jumps[2].append(head * vec_y - waves[face] * d_y)
    pull = (-speed_sq * rx, -speed_sq * ry)
    push = (-speed_sq * sx, -speed_sq * sy)
    out = [[None] * 10 for _ in range(3)]
    for a in range(10):
        total = along_r = along_s = None
        for b in range(10):
            d_r, d_s = diff_ref[a, 0, b], diff_ref[a, 1, b]
            term = d_r * flow_r[b] + d_s * flow_s[b]
            total = term if b == 0 else total + term
            along_r = d_r * eta[b] if b == 0 else along_r + d_r * eta[b]
            along_s = d_s * eta[b] if b == 0 else along_s + d_s * eta[b]
        sums = [total, pull[0] * along_r + push[0] * along_s, pull[1] * along_r + push[1] * along_s]
        for q in range(12):
            weight = lift_ref[a, q]
            for field in range(3):
                sums[field] = sums[field] + weight * jumps[field][q]
        for field in range(3):
            out[field][a] = sums[field]
    return [out[field][a] for field in range(3) for a in range(10)]


def first_kernel(
    sizes, state_hbm, depth_hbm, metric_hbm, partner_hbm, refine_hbm, before_ref, after_ref, diff_hbm, lift_hbm,
    cur, rate_ref, geo_ref,
    state_ref, depth_ref, metric_ref, partner_ref, refine_ref, diff_ref, lift_ref,
    spread, wide, aux, sems,
):
    blocks, halo = sizes.blocks, sizes.halo
    top, bottom = PAD + halo, PAD + halo + blocks
    place = lax.axis_index(AXES)
    count = lax.axis_size(AXES)
    copies = fetch_all(
        (
            (metric_hbm, metric_ref),
            (state_hbm, state_ref),
            (depth_hbm, depth_ref),
            (partner_hbm, partner_ref),
            (refine_hbm, refine_ref),
            (diff_hbm, diff_ref),
            (lift_hbm, lift_ref),
        ),
        sems,
    )
    for copy in copies:
        copy.wait()
    metric = split_metric(metric_ref, spread, blocks)
    dense = [depth_ref[...], *metric, partner_ref[...].astype(jnp.float32), refine_ref[...].astype(jnp.float32)]
    pack_state(state_ref, wide, blocks)
    for num in range(7):
        at = 4 * num + 3
        aux[num, top - halo : top, :] = before_ref[pl.ds(at, halo, stride=PACK), :]
        aux[num, top:bottom, :] = dense[num]
        aux[num, bottom : bottom + halo, :] = after_ref[pl.ds(at, halo, stride=PACK), :]
    for field in range(3):
        for node in range(10):
            item = 10 * field + node
            at = 4 * node + field
            cur[item, top - halo : top, :] = before_ref[pl.ds(at, halo, stride=PACK), :]
            cur[item, top:bottom, :] = wide[pl.ds(at, blocks, stride=PACK), :]
            cur[item, bottom : bottom + halo, :] = after_ref[pl.ds(at, halo, stride=PACK), :]

    def step(group, carry):
        base = PAD + 8 * group

        def load_aux(item, shift):
            return aux[item, pl.ds(base + shift, 8), :]

        def load(item, shift):
            return cur[item, pl.ds(base + shift, 8), :]

        depth, rx, ry, sx, sy, partner, refine = [load_aux(num, 0) for num in range(7)]
        index, inside = pair_index(partner)
        fetch = outer_values(load_aux, index, inside)
        walls = wall_masks(sizes, 8 * group, place, count, partner)
        speed_sq = GRAVITY * depth
        outer_sq = [jnp.where(walls[k], speed_sq, GRAVITY * fetch[k](0)) for k in range(3)]
        faces = ((sx, sy), (rx + sx, ry + sy), (rx, ry))
        squares = [vx * vx + vy * vy for vx, vy in faces]
        waves = [
            0.5 * jnp.sqrt(squares[k]) * jnp.sqrt(jnp.maximum(speed_sq, outer_sq[k])) for k in range(3)
        ]
        ghosts = [8.0 / squares[k] for k in range(3)]
        geo = [speed_sq, rx, ry, sx, sy, *outer_sq, *waves, *ghosts]
        rates = tendency(load, geo, walls, index, inside, diff_ref, lift_ref)
        at = pl.ds(pl.multiple_of(8 * group, 8), 8)
        for num, value in enumerate([*geo, partner, refine]):
            geo_ref[num, at, :] = value
        for item in range(30):
            rate_ref[item, at, :] = rates[item]
        return carry

    lax.fori_loop(0, sizes.rows // 8, step, 0)


def child_matrix(prolong_ref):
    f32 = jnp.float32
    node_r = lax.broadcasted_iota(jnp.int32, (PACK, 10), 0) // 4
    spread_r = (node_r == lax.broadcasted_iota(jnp.int32, (PACK, 10), 1)).astype(f32)
    item_c = lax.broadcasted_iota(jnp.int32, (10, WIDE), 1)
    spread_c = (item_c % 10 == lax.broadcasted_iota(jnp.int32, (10, WIDE), 0)).astype(f32)
    row = lax.broadcasted_iota(jnp.int32, (PACK, WIDE), 0)
    col = lax.broadcasted_iota(jnp.int32, (PACK, WIDE), 1)
    same = row % 4 == col // 10
    parts = []
    for child in range(2):
        left = jnp.dot(spread_r, prolong_ref[:, child, :], precision=HIGH, preferred_element_type=f32)
        full = jnp.dot(left, spread_c, precision=HIGH, preferred_element_type=f32)
        parts.append(jnp.where(same, full, 0.0))
    parts.append((same & (row // 4 == col % 10)).astype(f32))
    whole = jnp.concatenate(parts, axis=0)
    rounded = whole.astype(jnp.bfloat16)
    rest = (whole - rounded.astype(f32)).astype(jnp.bfloat16)
    return jnp.concatenate([rounded, rounded, rounded, rest], axis=1)


def second_kernel(
    sizes, cur, rate_ref, geo_ref, stats_ref, diff_hbm, lift_hbm, prolong_hbm, out_hbm,
    diff_ref, lift_ref, prolong_ref, out_ref,
    first, ends_ref, place_v, place_s, wide, weights, gathered, index_ref, sems, out_sems, sem,
):
    slots, keep, rows = sizes.slots, sizes.keep, sizes.rows
    place = lax.axis_index(AXES)
    count = lax.axis_size(AXES)
    copies = fetch_all(
        ((prolong_hbm, prolong_ref), (diff_hbm, diff_ref), (lift_hbm, lift_ref)), sems
    )
    for item in (30, 31):
        wide[pl.ds(item, slots + 1, stride=WIDE), :] = jnp.zeros((slots + 1, LANES), jnp.float32)
    for copy in copies:
        copy.wait()
    weights[...] = child_matrix(prolong_ref)
    stats = stats_ref[...]
    lane_n = lax.broadcasted_iota(jnp.int32, stats.shape, 1)
    dev_n = lax.broadcasted_iota(jnp.int32, stats.shape, 0)
    rate = jnp.where(lane_n < LANES // 2, stats, 0.0)
    top = jnp.max(jnp.max(rate, axis=0, keepdims=True), axis=1, keepdims=True)
    gone = jnp.where((lane_n == LANES - 1) & (dev_n < place), stats, 0.0)
    earlier = jnp.sum(jnp.sum(gone, axis=0, keepdims=True), axis=1, keepdims=True)
    step = COURANT / top
    refine = geo_ref[15, keep : keep + slots, :]
    counts = (1.0 + refine).astype(jnp.bfloat16)
    row_i = lax.broadcasted_iota(jnp.int32, (LANES, LANES), 0)
    col_i = lax.broadcasted_iota(jnp.int32, (LANES, LANES), 1)
    upper = (row_i <= col_i).astype(jnp.bfloat16)
    within = jnp.dot(counts, upper, preferred_element_type=jnp.float32)
    whole = jnp.dot(counts, jnp.ones((LANES, LANES), jnp.bfloat16), preferred_element_type=jnp.float32)
    row_s = lax.broadcasted_iota(jnp.int32, (slots, slots), 0)
    col_s = lax.broadcasted_iota(jnp.int32, (slots, slots), 1)
    lower = (col_s < row_s).astype(jnp.bfloat16)
    before = jnp.dot(lower, whole.astype(jnp.bfloat16), preferred_element_type=jnp.float32)
    own = before[sizes.margin : sizes.margin + 1, :]
    start = earlier - (place * (sizes.cells // 2)).astype(jnp.float32)
    ends = within + before + (start - own)
    ends_ref[:slots, :] = 2.0 * ends + refine
    ends_ref[slots:, :] = jnp.full((8, LANES), 1e9, jnp.float32)
    full = before + whole + (start - own)
    first_slot = LANES * lax.broadcasted_iota(jnp.int32, (slots, LANES), 1).astype(jnp.float32)
    lead = jnp.sum((full <= first_slot).astype(jnp.float32), axis=0, keepdims=True)
    lead = jnp.clip(lead.astype(jnp.int32), 0, slots - 1)
    place_v[...] = jnp.broadcast_to(lead, (8, LANES))
    copy = pltpu.make_async_copy(place_v, place_s, sem)
    copy.start()

    for item in range(30):
        first[item, PAD : PAD + rows, :] = cur[item, PAD : PAD + rows, :] + step * rate_ref[item]

    def stage(group, carry):
        base = PAD + keep + 8 * group
        at = pl.ds(8 * group + keep, 8)

        def load(item, shift):
            return first[item, pl.ds(base + shift, 8), :]

        geo = [geo_ref[num, at, :] for num in range(14)]
        partner = geo_ref[14, at, :]
        index, inside = pair_index(partner)
        walls = wall_masks(sizes, 8 * group + keep, place, count, partner)
        rates = tendency(load, geo, walls, index, inside, diff_ref, lift_ref)
        lead_row = 8 * WIDE * group
        for field in range(3):
            for node in range(10):
                item = 10 * field + node
                old = cur[item, pl.ds(base, 8), :]
                new = 0.5 * old + 0.5 * (load(item, 0) + step * rates[item])
                wide[pl.ds(lead_row + item, 8, stride=WIDE), :] = new
        return carry

    lax.fori_loop(0, slots // 8, stage, 0)

    copy.wait()
    for slot in range(slots):
        lead_at = place_s[0, slot]
        index_ref[0, slot : slot + 1, :] = ends_ref[pl.ds(lead_at, 1), :]
        index_ref[1, slot : slot + 1, :] = ends_ref[pl.ds(lead_at + 1, 1), :]
    near, far = index_ref[0], index_ref[1]
    slot_no = LANES * lax.broadcasted_iota(jnp.int32, (slots, LANES), 0) + lax.broadcasted_iota(
        jnp.int32, (slots, LANES), 1
    )
    goal = (2 * slot_no + 1).astype(jnp.float32)
    beyond = jnp.broadcast_to(near[:, LANES - 1 :], (slots, LANES)) <= goal

    def pick(index):
        return jnp.where(beyond, lane_gather(far, index), lane_gather(near, index))

    found = jnp.zeros((slots, LANES), jnp.int32)
    size = LANES // 2
    while size:
        passed = pick(found + (size - 1)) <= goal
        found = jnp.where(passed, found + size, found)
        size //= 2
    mine = pick(found).astype(jnp.int32)
    split = mine & 1
    begin = (mine >> 1) - 1 - split
    kind = split * (1 + slot_no - begin)
    index_ref[0] = found.astype(jnp.float32)
    index_ref[1] = kind.astype(jnp.float32)
    index_ref[2] = beyond.astype(jnp.float32)
    for slot in range(slots):
        lead_at = place_s[0, slot] * WIDE
        lane_idx = jnp.broadcast_to(index_ref[0, slot : slot + 1, :], (WIDE, LANES)).astype(jnp.int32)
        passed = jnp.broadcast_to(index_ref[2, slot : slot + 1, :], (WIDE, LANES)) > 0.5
        one = wide[pl.ds(pl.multiple_of(lead_at, WIDE), WIDE), :]
        two = wide[pl.ds(pl.multiple_of(lead_at + WIDE, WIDE), WIDE), :]
        gathered[:, LANES * slot : LANES * (slot + 1)] = jnp.where(
            passed, lane_gather(two, lane_idx), lane_gather(one, lane_idx)
        )
    matrix = weights[...]
    chunk = 8 * LANES
    results = []
    for part in range(slots // 8):
        span = slice(chunk * part, chunk * (part + 1))
        values = gathered[:, span]
        high = values.astype(jnp.bfloat16)
        rest = values - high.astype(jnp.float32)
        low = rest.astype(jnp.bfloat16)
        last = (rest - low.astype(jnp.float32)).astype(jnp.bfloat16)
        stack = jnp.concatenate([high, low, last, high], axis=0)
        children = jnp.dot(matrix, stack, preferred_element_type=jnp.float32)
        for sub in range(8):
            slot = 8 * part + sub
            cut = slice(LANES * sub, LANES * (sub + 1))
            tag = jnp.broadcast_to(index_ref[1, slot : slot + 1, :], (PACK, LANES))
            value = jnp.where(
                tag < 0.5,
                children[2 * PACK :, cut],
                jnp.where(tag < 1.5, children[:PACK, cut], children[PACK : 2 * PACK, cut]),
            )
            for node in range(10):
                out_ref[node, :, LANES * slot : LANES * (slot + 1)] = value[4 * node : 4 * node + 3]
        result = pltpu.make_async_copy(out_ref.at[:, :, span], out_hbm.at[:, :, span], out_sems.at[part])
        result.start()
        results.append(result)
    for result in results:
        result.wait()


def shards(state, depth, metric, partner, refine, diff_ops, lift, prolong):
    sizes = Sizes(state.shape[2])
    count = lax.axis_size(AXES)
    blocks, rows, slots, halo = sizes.blocks, sizes.rows, sizes.slots, sizes.halo
    depth, partner, refine = [x.reshape(blocks, LANES) for x in (depth, partner, refine)]
    state, diff_ops, prolong = [jnp.transpose(x, (1, 0, 2)) for x in (state, diff_ops, prolong)]
    state, depth, metric, partner, refine, diff_ops, lift, prolong = [
        pltpu.with_memory_space_constraint(x, pltpu.HBM)
        for x in (state, depth, metric, partner, refine, diff_ops, lift, prolong)
    ]
    f32, i32 = jnp.float32, jnp.int32
    packed = jax.ShapeDtypeStruct((PACK * halo, LANES), f32)
    dense = [
        pltpu.VMEM((blocks, LANES), f32),
        pltpu.VMEM(metric.shape, f32),
        pltpu.VMEM((blocks, LANES), i32),
        pltpu.VMEM((blocks, LANES), i32),
    ]
    stats, head, tail = pl.pallas_call(
        functools.partial(pack_kernel, sizes),
        name="pack",
        out_shape=(jax.ShapeDtypeStruct((count, LANES), f32), packed, packed),
        in_specs=[HBM] * 5,
        out_specs=(VMEM,) * 3,
        scratch_shapes=[
            pltpu.VMEM((10, 3, LANES * halo), f32),
            pltpu.VMEM((10, 3, LANES * halo), f32),
            *dense,
            pltpu.VMEM((8 * blocks, LANES), f32),
            pltpu.SemaphoreType.DMA((6,)),
        ],
        compiler_params=PARAMS,
    )(state, depth, metric, partner, refine)
    before = lax.ppermute(tail, AXES, [(i, i + 1) for i in range(count - 1)])
    after = lax.ppermute(head, AXES, [(i + 1, i) for i in range(count - 1)])
    stats = lax.all_to_all(stats, AXES, 0, 0, tiled=True)
    before, after, stats = [
        pltpu.with_memory_space_constraint(x, pltpu.VMEM) for x in (before, after, stats)
    ]
    operators = [pltpu.SMEM(diff_ops.shape, f32), pltpu.SMEM(lift.shape, f32)]
    cur, rates, geo = pl.pallas_call(
        functools.partial(first_kernel, sizes),
        name="first_stage",
        out_shape=(
            jax.ShapeDtypeStruct((30, sizes.tall, LANES), f32),
            jax.ShapeDtypeStruct((30, rows, LANES), f32),
            jax.ShapeDtypeStruct((16, rows, LANES), f32),
        ),
        in_specs=[HBM] * 5 + [VMEM] * 2 + [HBM] * 2,
        out_specs=(VMEM,) * 3,
        scratch_shapes=[
            pltpu.VMEM(state.shape, f32),
            *dense,
            *operators,
            pltpu.VMEM((8 * blocks, LANES), f32),
            pltpu.VMEM((PACK * blocks, LANES), f32),
            pltpu.VMEM((7, sizes.tall, LANES), f32),
            pltpu.SemaphoreType.DMA((7,)),
        ],
        compiler_params=PARAMS,
    )(state, depth, metric, partner, refine, before, after, diff_ops, lift)
    refined = pl.pallas_call(
        functools.partial(second_kernel, sizes),
        name="second_stage_refine",
        out_shape=jax.ShapeDtypeStruct((10, 3, LANES * slots), f32),
        in_specs=[VMEM] * 4 + [HBM] * 3,
        out_specs=HBM,
        scratch_shapes=[
            *operators,
            pltpu.VMEM(prolong.shape, f32),
            pltpu.VMEM((10, 3, LANES * slots), f32),
            pltpu.VMEM((30, sizes.tall, LANES), f32),
            pltpu.VMEM((slots + 8, LANES), f32),
            pltpu.VMEM((8, LANES), i32),
            pltpu.SMEM((8, LANES), i32),
            pltpu.VMEM((WIDE * (slots + 1), LANES), f32),
            pltpu.VMEM((3 * PACK, 4 * WIDE), jnp.bfloat16),
            pltpu.VMEM((WIDE, LANES * slots), f32),
            pltpu.VMEM((3, slots, LANES), f32),
            pltpu.SemaphoreType.DMA((3,)),
            pltpu.SemaphoreType.DMA((slots // 8,)),
            pltpu.SemaphoreType.DMA,
        ],
        compiler_params=PARAMS,
    )(cur, rates, geo, stats, diff_ops, lift, prolong)
    return jnp.transpose(refined, (1, 0, 2))


def solution(mesh):
    return jax.shard_map(
        shards,
        mesh=mesh,
        in_specs=(
            P(None, None, AXES),
            P(AXES),
            P(None, AXES),
            P(AXES),
            P(AXES),
            P(),
            P(),
            P(),
        ),
        out_specs=P(None, None, AXES),
        check_vma=False,
    )
```

profile of v0, /device:TPU:0, one launch (start us, length us, event | category | flops | bytes accessed | tf_op | source)
XLA Modules:
  0.0 28.6 jit_solution(485479535091487976)
XLA Ops:
  0.0 1.9 %pack.1 = (f32[32,128]{1,0:T(8,128)}, f32[360,128]{1,0:T(8,128)S(1)}, f32[360,128]{1,0:T(8,128)S(1)}) custom-call(f32[10,3,4096]{2,1,0:T(4,128)} %bitcast.12, f32[32,128]{1,0:T(8,128)} %bitcast.14, f32[4,4096]{1,0:T(4,128)} %metric_hbm.3, s32[32,128]{1,0:T(8,128)} %bitcast.16, s32[32,128]{1,0:T(8,128)} %bitcast.18), custom_call_target="tpu_custom_call" | custom-call | tf_op jit(solution)/shard_map/pack/pallas_call | solution.py:438
  1.9 2.4 %collective-permute-start = (f32[360,128]{1,0:T(8,128)S(1)}, f32[360,128]{1,0:T(8,128)S(1)}, u32[]{:S(2)}, u32[]{:S(2)}) collective-permute-start(f32[360,128]{1,0:T(8,128)S(1)} %get-tuple-element.11), channel_id=1, source_target_pairs={{0,1},{1,2},{2,3},{3,4},{4,5},{5,6},{6,7},{7,8},{8,9},{9,10},{10,1... | collective-permute-start | bytes 552968 | tf_op jit(solution)/shard_map/ppermute | solution.py:453
  4.3 1.3 %collective-permute-start.1 = (f32[360,128]{1,0:T(8,128)S(1)}, f32[360,128]{1,0:T(8,128)S(1)}, u32[]{:S(2)}, u32[]{:S(2)}) collective-permute-start(f32[360,128]{1,0:T(8,128)S(1)} %get-tuple-element.12), channel_id=1, source_target_pairs={{1,0},{2,1},{3,2},{4,3},{5,4},{6,5},{7,6},{8,7},{9,8},{10,9},{11,1... | collective-permute-start | bytes 552968 | tf_op jit(solution)/shard_map/ppermute | solution.py:454
  5.6 9.2 %all-to-all-start = ((f32[32,1,128]{2,1,0:T(1,128)}), f32[32,1,128]{2,1,0:T(1,128)S(1)}, u32[]{:S(2)}, u32[]{:S(2)}) async-start(f32[32,1,128]{2,1,0:T(1,128)} %bitcast.6), calls=%async_computation | async-start | bytes 32768 | tf_op jit(solution)/shard_map/all_to_all | solution.py:455
  14.8 0.0 collective-permute-done.before_ref
  14.8 0.0 collective-permute-done.1.after_ref
  14.8 3.9 %first_stage.1 = (f32[30,72,128]{2,1,0:T(8,128)S(1)}, f32[30,56,128]{2,1,0:T(8,128)S(1)}, f32[16,56,128]{2,1,0:T(8,128)S(1)}) custom-call(f32[10,3,4096]{2,1,0:T(4,128)} %bitcast.13, f32[32,128]{1,0:T(8,128)} %bitcast.15, f32[4,4096]{1,0:T(4,128)} %metric_hbm.3, s32[32,128]{1,0:T(8,128)} %bitcast.17, s32[32,128]{1,0:T(8,128)} %bitcast.19, ...), custom_call_target="tpu_custom_call" | custom-call | tf_op jit(solution)/shard_map/first_stage/pallas_call | solution.py:460
  18.7 3.1 %all-to-all-done = f32[32,1,128]{2,1,0:T(1,128)S(1)} async-done(((f32[32,1,128]{2,1,0:T(1,128)}), f32[32,1,128]{2,1,0:T(1,128)S(1)}, u32[]{:S(2)}, u32[]{:S(2)}) %all-to-all-start) | async-done | bytes 16416 | tf_op jit(solution)/shard_map/all_to_all | solution.py:455
  21.9 6.7 %second_stage_refine.1 = f32[10,3,6144]{2,1,0:T(4,128)} custom-call(f32[30,72,128]{2,1,0:T(8,128)S(1)} %get-tuple-element.13.cur, f32[30,56,128]{2,1,0:T(8,128)S(1)} %get-tuple-element.14.rate_ref, f32[16,56,128]{2,1,0:T(8,128)S(1)} %get-tuple-element.15.geo_ref, f32[32,128]{1,0:T(8,128)S(1)} %bitcast.11, f32[10,2,10]{2,1,0:T(2,128)} %bitcast.21, ...), custom_call_target="tpu_custom_call" | custom-call | tf_op jit(solution)/shard_map/second_stage_refine/pallas_call | solution.py:481
Async XLA Ops:
  1.9 12.9 %collective-permute-start = (f32[360,128]{1,0:T(8,128)S(1)}, f32[360,128]{1,0:T(8,128)S(1)}, u32[]{:S(2)}, u32[]{:S(2)}) collective-permute-start(f32[360,128]{1,0:T(8,128)S(1)} %get-tuple-element.11), channel_id=1, source_target_pairs={{0,1},{1,2},{2,3},{3,4},{4,5},{5,6},{6,7},{7,8},{8,9},{9,10},{10,1... | collective-permute-start | bytes 552968 | tf_op jit(solution)/shard_map/ppermute | solution.py:453
  4.3 10.5 %collective-permute-start.1 = (f32[360,128]{1,0:T(8,128)S(1)}, f32[360,128]{1,0:T(8,128)S(1)}, u32[]{:S(2)}, u32[]{:S(2)}) collective-permute-start(f32[360,128]{1,0:T(8,128)S(1)} %get-tuple-element.12), channel_id=1, source_target_pairs={{1,0},{2,1},{3,2},{4,3},{5,4},{6,5},{7,6},{8,7},{9,8},{10,9},{11,1... | collective-permute-start | bytes 552968 | tf_op jit(solution)/shard_map/ppermute | solution.py:454
  5.6 16.3 %all-to-all-start = ((f32[32,1,128]{2,1,0:T(1,128)}), f32[32,1,128]{2,1,0:T(1,128)S(1)}, u32[]{:S(2)}, u32[]{:S(2)}) async-start(f32[32,1,128]{2,1,0:T(1,128)} %bitcast.6), calls=%async_computation | async-start | bytes 32768 | tf_op jit(solution)/shard_map/all_to_all | solution.py:455
where the time goes:
time: 28.9 us; the launch traced here: 28.6 us
  starting transfers between devices  12.9 us (45%)
  Pallas kernels  12.5 us (43%)
  waiting for transfers between devices  3.13 us (11%)
    all_to_all x1, starting transfers between devices, shards(): stats = lax.all_to_all(stats, AXES, 0, 0, tiled=True)  9.21 us
    pallas_call x1, Pallas kernels, shards(): pl.pallas_call(functools.partial(second_kernel, sizes), name='second_stag...  6.7 us
    pallas_call x1, Pallas kernels, shards(): pl.pallas_call(functools.partial(first_kernel, sizes), name='first_stage'...  3.92 us
    all_to_all x1, waiting for transfers between devices, shards(): stats = lax.all_to_all(stats, AXES, 0, 0, tiled=True)  3.12 us
    ppermute x1, starting transfers between devices, shards(): before = lax.ppermute(tail, AXES, [(i, i + 1) for i in range(count - 1)])  2.37 us
    pallas_call x1, Pallas kernels, shards(): pl.pallas_call(functools.partial(pack_kernel, sizes), name='pack', out_sh...  1.88 us
    ppermute x1, starting transfers between devices, shards(): after = lax.ppermute(head, AXES, [(i + 1, i) for i in range(count - 1)])  1.29 us
  transfers between devices with their start and end apart: 3, of which 1 were waited for; matrix products, arithmetic and copies ran while one was open for 0% of the time, Pallas kernels for 14%

commit v1 on v0

--- a/solution.py
+++ b/solution.py
@@ -48,19 +48,22 @@
 
 
 def pack_kernel(
-    sizes, state_hbm, depth_hbm, metric_hbm, partner_hbm, refine_hbm, stats_ref, head_ref, tail_ref,
-    state_head, state_tail, depth_ref, metric_ref, partner_ref, refine_ref, spread, sems,
+    sizes, state_hbm, depth_hbm, metric_hbm, partner_hbm, refine_hbm, stats_ref, even_ref, odd_ref,
+    state_even, state_odd, depth_ref, metric_ref, partner_ref, refine_ref, spread, sems,
 ):
     blocks, halo = sizes.blocks, sizes.halo
     wide = LANES * halo
+    late = blocks - halo
+    even = (lax.axis_index(AXES) + 1) % 2 * late
+    odd = late - even
     copies = fetch_all(
         (
             (depth_hbm, depth_ref),
             (metric_hbm, metric_ref),
             (refine_hbm, refine_ref),
             (partner_hbm, partner_ref),
-            (state_hbm.at[:, :, 0:wide], state_head),
-            (state_hbm.at[:, :, sizes.cells - wide : sizes.cells], state_tail),
+            (state_hbm.at[:, :, pl.ds(pl.multiple_of(LANES * even, LANES), wide)], state_even),
+            (state_hbm.at[:, :, pl.ds(pl.multiple_of(LANES * odd, LANES), wide)], state_odd),
         ),
         sems,
     )
@@ -79,11 +82,14 @@
     stats_ref[...] = jnp.where(
         lane < LANES // 2, jnp.broadcast_to(top, shape), jnp.broadcast_to(extra, shape)
     )
-    partner = partner_ref[...].astype(jnp.float32)
-    for ref, source, start in ((head_ref, state_head, 0), (tail_ref, state_tail, blocks - halo)):
+    for ref, source, start in ((even_ref, state_even, even), (odd_ref, state_odd, odd)):
         pack_state(source, ref, halo)
-        for num, dense in enumerate((depth, rx, ry, sx, sy, partner, refine)):
-            ref[pl.ds(4 * num + 3, halo, stride=PACK), :] = dense[start : start + halo]
+        at = pl.ds(start, halo)
+        dense = [depth_ref[at, :]]
+        dense += [spread[pl.ds(8 * start + comp, halo, stride=8), :] for comp in range(4)]
+        dense += [partner_ref[at, :].astype(jnp.float32), refine_ref[at, :].astype(jnp.float32)]
+        for num, value in enumerate(dense):
+            ref[pl.ds(4 * num + 3, halo, stride=PACK), :] = value
 
 
 def pack_state(source, target, blocks):
@@ -183,7 +189,7 @@
 
 
 def first_kernel(
-    sizes, state_hbm, depth_hbm, metric_hbm, partner_hbm, refine_hbm, before_ref, after_ref, diff_hbm, lift_hbm,
+    sizes, state_hbm, depth_hbm, metric_hbm, partner_hbm, refine_hbm, even_ref, odd_ref, diff_hbm, lift_hbm,
     cur, rate_ref, geo_ref,
     state_ref, depth_ref, metric_ref, partner_ref, refine_ref, diff_ref, lift_ref,
     spread, wide, aux, sems,
@@ -209,18 +215,22 @@
     metric = split_metric(metric_ref, spread, blocks)
     dense = [depth_ref[...], *metric, partner_ref[...].astype(jnp.float32), refine_ref[...].astype(jnp.float32)]
     pack_state(state_ref, wide, blocks)
+    even = place % 2 == 0
+
+    def set_halo(target, num, row):
+        by_even = even_ref[pl.ds(row, halo, stride=PACK), :]
+        by_odd = odd_ref[pl.ds(row, halo, stride=PACK), :]
+        target[num, top - halo : top, :] = jnp.where(even, by_odd, by_even)
+        target[num, bottom : bottom + halo, :] = jnp.where(even, by_even, by_odd)
+
     for num in range(7):
-        at = 4 * num + 3
-        aux[num, top - halo : top, :] = before_ref[pl.ds(at, halo, stride=PACK), :]
+        set_halo(aux, num, 4 * num + 3)
         aux[num, top:bottom, :] = dense[num]
-        aux[num, bottom : bottom + halo, :] = after_ref[pl.ds(at, halo, stride=PACK), :]
     for field in range(3):
         for node in range(10):
             item = 10 * field + node
-            at = 4 * node + field
-            cur[item, top - halo : top, :] = before_ref[pl.ds(at, halo, stride=PACK), :]
-            cur[item, top:bottom, :] = wide[pl.ds(at, blocks, stride=PACK), :]
-            cur[item, bottom : bottom + halo, :] = after_ref[pl.ds(at, halo, stride=PACK), :]
+            set_halo(cur, item, 4 * node + field)
+            cur[item, top:bottom, :] = wide[pl.ds(4 * node + field, blocks, stride=PACK), :]
 
     def step(group, carry):
         base = PAD + 8 * group
@@ -277,27 +287,28 @@
 
 
 def second_kernel(
-    sizes, cur, rate_ref, geo_ref, stats_ref, diff_hbm, lift_hbm, prolong_hbm, out_hbm,
-    diff_ref, lift_ref, prolong_ref, out_ref,
+    sizes, cur, rate_ref, geo_ref, stats_hbm, diff_hbm, lift_hbm, prolong_hbm, out_hbm,
+    stats_ref, diff_ref, lift_ref, prolong_ref, out_ref,
     first, ends_ref, place_v, place_s, wide, weights, gathered, index_ref, sems, out_sems, sem,
 ):
     slots, keep, rows = sizes.slots, sizes.keep, sizes.rows
     place = lax.axis_index(AXES)
     count = lax.axis_size(AXES)
     copies = fetch_all(
-        ((prolong_hbm, prolong_ref), (diff_hbm, diff_ref), (lift_hbm, lift_ref)), sems
+        ((prolong_hbm, prolong_ref), (stats_hbm, stats_ref), (diff_hbm, diff_ref), (lift_hbm, lift_ref)), sems
     )
     for item in (30, 31):
         wide[pl.ds(item, slots + 1, stride=WIDE), :] = jnp.zeros((slots + 1, LANES), jnp.float32)
-    for copy in copies:
+    copies[0].wait()
+    weights[...] = child_matrix(prolong_ref)
+    for copy in copies[1:]:
         copy.wait()
-    weights[...] = child_matrix(prolong_ref)
     stats = stats_ref[...]
     lane_n = lax.broadcasted_iota(jnp.int32, stats.shape, 1)
-    dev_n = lax.broadcasted_iota(jnp.int32, stats.shape, 0)
+    row_n = lax.broadcasted_iota(jnp.int32, stats.shape, 0)
     rate = jnp.where(lane_n < LANES // 2, stats, 0.0)
     top = jnp.max(jnp.max(rate, axis=0, keepdims=True), axis=1, keepdims=True)
-    gone = jnp.where((lane_n == LANES - 1) & (dev_n < place), stats, 0.0)
+    gone = jnp.where((lane_n == LANES - 1) & (row_n % 8 == 0) & (row_n < 8 * place), stats, 0.0)
     earlier = jnp.sum(jnp.sum(gone, axis=0, keepdims=True), axis=1, keepdims=True)
     step = COURANT / top
     refine = geo_ref[15, keep : keep + slots, :]
@@ -417,6 +428,11 @@
         result.wait()
 
 
+def swaps(start, count):
+    pairs = [(i, i + 1) for i in range(start, count - 1, 2)]
+    return pairs + [(j, i) for i, j in pairs]
+
+
 def shards(state, depth, metric, partner, refine, diff_ops, lift, prolong):
     sizes = Sizes(state.shape[2])
     count = lax.axis_size(AXES)
@@ -435,10 +451,10 @@
         pltpu.VMEM((blocks, LANES), i32),
         pltpu.VMEM((blocks, LANES), i32),
     ]
-    stats, head, tail = pl.pallas_call(
+    stats, even, odd = pl.pallas_call(
         functools.partial(pack_kernel, sizes),
         name="pack",
-        out_shape=(jax.ShapeDtypeStruct((count, LANES), f32), packed, packed),
+        out_shape=(jax.ShapeDtypeStruct((8, LANES), f32), packed, packed),
         in_specs=[HBM] * 5,
         out_specs=(VMEM,) * 3,
         scratch_shapes=[
@@ -450,12 +466,11 @@
         ],
         compiler_params=PARAMS,
     )(state, depth, metric, partner, refine)
-    before = lax.ppermute(tail, AXES, [(i, i + 1) for i in range(count - 1)])
-    after = lax.ppermute(head, AXES, [(i + 1, i) for i in range(count - 1)])
-    stats = lax.all_to_all(stats, AXES, 0, 0, tiled=True)
-    before, after, stats = [
-        pltpu.with_memory_space_constraint(x, pltpu.VMEM) for x in (before, after, stats)
-    ]
+    stats = lax.all_gather(stats, AXES, tiled=True)
+    even = lax.ppermute(even, AXES, swaps(0, count))
+    odd = lax.ppermute(odd, AXES, swaps(1, count))
+    even, odd = [pltpu.with_memory_space_constraint(x, pltpu.VMEM) for x in (even, odd)]
+    stats = pltpu.with_memory_space_constraint(stats, pltpu.HBM)
     operators = [pltpu.SMEM(diff_ops.shape, f32), pltpu.SMEM(lift.shape, f32)]
     cur, rates, geo = pl.pallas_call(
         functools.partial(first_kernel, sizes),
@@ -477,14 +492,15 @@
             pltpu.SemaphoreType.DMA((7,)),
         ],
         compiler_params=PARAMS,
-    )(state, depth, metric, partner, refine, before, after, diff_ops, lift)
+    )(state, depth, metric, partner, refine, even, odd, diff_ops, lift)
     refined = pl.pallas_call(
         functools.partial(second_kernel, sizes),
         name="second_stage_refine",
         out_shape=jax.ShapeDtypeStruct((10, 3, LANES * slots), f32),
-        in_specs=[VMEM] * 4 + [HBM] * 3,
+        in_specs=[VMEM] * 3 + [HBM] * 4,
         out_specs=HBM,
         scratch_shapes=[
+            pltpu.VMEM(stats.shape, f32),
             *operators,
             pltpu.VMEM(prolong.shape, f32),
             pltpu.VMEM((10, 3, LANES * slots), f32),
@@ -496,7 +512,7 @@
             pltpu.VMEM((3 * PACK, 4 * WIDE), jnp.bfloat16),
             pltpu.VMEM((WIDE, LANES * slots), f32),
             pltpu.VMEM((3, slots, LANES), f32),
-            pltpu.SemaphoreType.DMA((3,)),
+            pltpu.SemaphoreType.DMA((4,)),
             pltpu.SemaphoreType.DMA((slots // 8,)),
             pltpu.SemaphoreType.DMA,
         ],

time: 28.9 us -> 61.2 us (2.12)
  blocking collectives: 0 us -> 47.8 us
  starting transfers between devices: 12.9 us -> 1.18 us
  waiting for transfers between devices: 3.13 us -> 0.01 us
    all_gather x0 -> x1, blocking collectives: none -> 47.8 us  [shards(): stats = lax.all_gather(stats, AXES, tiled=True)]
    all_to_all x1 -> x0, starting transfers between devices: 9.21 us -> none  [shards(): stats = lax.all_to_all(stats, AXES, 0, 0, tiled=True)]
    all_to_all x1 -> x0, waiting for transfers between devices: 3.12 us -> none  [shards(): stats = lax.all_to_all(stats, AXES, 0, 0, tiled=True)]
    ppermute x2, starting transfers between devices: 3.66 us -> 1.18 us  [the longest x1 0.66 us: shards(): odd = lax.ppermute(odd, AXES, swaps(1, count))]
  transfers between devices with their start and end apart: 3 -> 2, of which waited for: 1 -> 0; matrix products, arithmetic and copies ran while one was open for 0% -> 0% of each run, Pallas kernels for 14% -> 0%
where the time goes in v1:
time: 61.2 us; the launch traced here: 60.8 us
  blocking collectives  47.8 us (78%)
  Pallas kernels  11.9 us (19%)
  starting transfers between devices  1.18 us (2%)
    all_gather x1, blocking collectives, shards(): stats = lax.all_gather(stats, AXES, tiled=True)  47.8 us
    pallas_call x1, Pallas kernels, shards(): pl.pallas_call(functools.partial(second_kernel, sizes), name='second_stag...  6.66 us
    pallas_call x1, Pallas kernels, shards(): pl.pallas_call(functools.partial(first_kernel, sizes), name='first_stage'...  3.93 us
    pallas_call x1, Pallas kernels, shards(): pl.pallas_call(functools.partial(pack_kernel, sizes), name='pack', out_sh...  1.28 us
  transfers between devices with their start and end apart: 2, of which 0 were waited for; matrix products, arithmetic and copies ran while one was open for 0% of the time, Pallas kernels for 0%

profile of v1, /device:TPU:0, one launch (start us, length us, event | category | flops | bytes accessed | tf_op | source)
XLA Modules:
  0.0 60.8 jit_solution(977116592388834415)
XLA Ops:
  0.0 1.3 %pack.1 = (f32[8,128]{1,0:T(8,128)S(1)}, f32[360,128]{1,0:T(8,128)S(1)}, f32[360,128]{1,0:T(8,128)S(1)}) custom-call(f32[10,3,4096]{2,1,0:T(4,128)} %bitcast.7, f32[32,128]{1,0:T(8,128)} %bitcast.9, f32[4,4096]{1,0:T(4,128)} %metric_hbm.3, s32[32,128]{1,0:T(8,128)} %bitcast.11, s32[32,128]{1,0:T(8,128)} %bitcast.13), custom_call_target="tpu_custom_call" | custom-call | tf_op jit(solution)/shard_map/pack/pallas_call | solution.py:454
  1.3 0.5 collective-permute-start
  1.8 0.7 %collective-permute-start.1 = (f32[360,128]{1,0:T(8,128)S(1)}, f32[360,128]{1,0:T(8,128)S(1)}, u32[]{:S(2)}, u32[]{:S(2)}) collective-permute-start(f32[360,128]{1,0:T(8,128)S(1)} %get-tuple-element.12), channel_id=1, source_target_pairs={{1,2},{3,4},{5,6},{7,8},{9,10},{11,12},{13,14},{15,16},{17,18},{19... | collective-permute-start | bytes 552968 | tf_op jit(solution)/shard_map/ppermute | solution.py:471
  2.5 47.8 %all_gather.3.stats_hbm = f32[256,128]{1,0:T(8,128)} all-gather(f32[8,128]{1,0:T(8,128)S(1)} %get-tuple-element.16), channel_id=1, replica_groups=mesh['row'=4,'col'=8] {'row','col'}, dimensions={0}, use_global_device_ids=true | all-gather | bytes 135168 | tf_op jit(solution)/shard_map/all_gather | solution.py:469
  50.2 0.0 collective-permute-done.even_ref
  50.2 0.0 collective-permute-done.1.odd_ref
  50.2 3.9 %first_stage.1 = (f32[30,72,128]{2,1,0:T(8,128)S(1)}, f32[30,56,128]{2,1,0:T(8,128)S(1)}, f32[16,56,128]{2,1,0:T(8,128)S(1)}) custom-call(f32[10,3,4096]{2,1,0:T(4,128)} %bitcast.8, f32[32,128]{1,0:T(8,128)} %bitcast.10, f32[4,4096]{1,0:T(4,128)} %metric_hbm.3, s32[32,128]{1,0:T(8,128)} %bitcast.12, s32[32,128]{1,0:T(8,128)} %bitcast.14, ...), custom_call_target="tpu_custom_call" | custom-call | tf_op jit(solution)/shard_map/first_stage/pallas_call | solution.py:475
  54.2 6.7 %second_stage_refine.1 = f32[10,3,6144]{2,1,0:T(4,128)} custom-call(f32[30,72,128]{2,1,0:T(8,128)S(1)} %get-tuple-element.13.cur, f32[30,56,128]{2,1,0:T(8,128)S(1)} %get-tuple-element.14.rate_ref, f32[16,56,128]{2,1,0:T(8,128)S(1)} %get-tuple-element.15.geo_ref, f32[256,128]{1,0:T(8,128)} %all_gather.3.stats_hbm, f32[10,2,10]{2,1,0:T(2,128)} %bitcast.16, ...), custom_call_target="tpu_custom_call" | custom-call | tf_op jit(solution)/shard_map/second_stage_refine/pallas_call | solution.py:496
Async XLA Ops:
  1.3 48.9 %collective-permute-start = (f32[360,128]{1,0:T(8,128)S(1)}, f32[360,128]{1,0:T(8,128)S(1)}, u32[]{:S(2)}, u32[]{:S(2)}) collective-permute-start(f32[360,128]{1,0:T(8,128)S(1)} %get-tuple-element.11), channel_id=1, source_target_pairs={{0,1},{2,3},{4,5},{6,7},{8,9},{10,11},{12,13},{14,15},{16,17},{18,... | collective-permute-start | bytes 552968 | tf_op jit(solution)/shard_map/ppermute | solution.py:470
  1.8 48.4 %collective-permute-start.1 = (f32[360,128]{1,0:T(8,128)S(1)}, f32[360,128]{1,0:T(8,128)S(1)}, u32[]{:S(2)}, u32[]{:S(2)}) collective-permute-start(f32[360,128]{1,0:T(8,128)S(1)} %get-tuple-element.12), channel_id=1, source_target_pairs={{1,2},{3,4},{5,6},{7,8},{9,10},{11,12},{13,14},{15,16},{17,18},{19... | collective-permute-start | bytes 552968 | tf_op jit(solution)/shard_map/ppermute | solution.py:471

commit v2 on v1

--- a/solution.py
+++ b/solution.py
@@ -48,8 +48,8 @@
 
 
 def pack_kernel(
-    sizes, state_hbm, depth_hbm, metric_hbm, partner_hbm, refine_hbm, stats_ref, even_ref, odd_ref,
-    state_even, state_odd, depth_ref, metric_ref, partner_ref, refine_ref, spread, sems,
+    sizes, state_hbm, depth_hbm, metric_hbm, partner_hbm, refine_hbm, stats_hbm, even_ref, odd_ref,
+    stats_ref, state_even, state_odd, depth_ref, metric_ref, partner_ref, refine_ref, spread, sems, sem,
 ):
     blocks, halo = sizes.blocks, sizes.halo
     wide = LANES * halo
@@ -67,7 +67,7 @@
         ),
         sems,
     )
-    for copy in copies:
+    for copy in copies[:3]:
         copy.wait()
     rx, ry, sx, sy = split_metric(metric_ref, spread, blocks)
     depth = depth_ref[...]
@@ -82,6 +82,10 @@
     stats_ref[...] = jnp.where(
         lane < LANES // 2, jnp.broadcast_to(top, shape), jnp.broadcast_to(extra, shape)
     )
+    sent = pltpu.make_async_copy(stats_ref, stats_hbm, sem)
+    sent.start()
+    for copy in copies[3:]:
+        copy.wait()
     for ref, source, start in ((even_ref, state_even, even), (odd_ref, state_odd, odd)):
         pack_state(source, ref, halo)
         at = pl.ds(start, halo)
@@ -90,6 +94,7 @@
         dense += [partner_ref[at, :].astype(jnp.float32), refine_ref[at, :].astype(jnp.float32)]
         for num, value in enumerate(dense):
             ref[pl.ds(4 * num + 3, halo, stride=PACK), :] = value
+    sent.wait()
 
 
 def pack_state(source, target, blocks):
@@ -188,83 +193,6 @@
     return [out[field][a] for field in range(3) for a in range(10)]
 
 
-def first_kernel(
-    sizes, state_hbm, depth_hbm, metric_hbm, partner_hbm, refine_hbm, even_ref, odd_ref, diff_hbm, lift_hbm,
-    cur, rate_ref, geo_ref,
-    state_ref, depth_ref, metric_ref, partner_ref, refine_ref, diff_ref, lift_ref,
-    spread, wide, aux, sems,
-):
-    blocks, halo = sizes.blocks, sizes.halo
-    top, bottom = PAD + halo, PAD + halo + blocks
-    place = lax.axis_index(AXES)
-    count = lax.axis_size(AXES)
-    copies = fetch_all(
-        (
-            (metric_hbm, metric_ref),
-            (state_hbm, state_ref),
-            (depth_hbm, depth_ref),
-            (partner_hbm, partner_ref),
-            (refine_hbm, refine_ref),
-            (diff_hbm, diff_ref),
-            (lift_hbm, lift_ref),
-        ),
-        sems,
-    )
-    for copy in copies:
-        copy.wait()
-    metric = split_metric(metric_ref, spread, blocks)
-    dense = [depth_ref[...], *metric, partner_ref[...].astype(jnp.float32), refine_ref[...].astype(jnp.float32)]
-    pack_state(state_ref, wide, blocks)
-    even = place % 2 == 0
-
-    def set_halo(target, num, row):
-        by_even = even_ref[pl.ds(row, halo, stride=PACK), :]
-        by_odd = odd_ref[pl.ds(row, halo, stride=PACK), :]
-        target[num, top - halo : top, :] = jnp.where(even, by_odd, by_even)
-        target[num, bottom : bottom + halo, :] = jnp.where(even, by_even, by_odd)
-
-    for num in range(7):
-        set_halo(aux, num, 4 * num + 3)
-        aux[num, top:bottom, :] = dense[num]
-    for field in range(3):
-        for node in range(10):
-            item = 10 * field + node
-            set_halo(cur, item, 4 * node + field)
-            cur[item, top:bottom, :] = wide[pl.ds(4 * node + field, blocks, stride=PACK), :]
-
-    def step(group, carry):
-        base = PAD + 8 * group
-
-        def load_aux(item, shift):
-            return aux[item, pl.ds(base + shift, 8), :]
-
-        def load(item, shift):
-            return cur[item, pl.ds(base + shift, 8), :]
-
-        depth, rx, ry, sx, sy, partner, refine = [load_aux(num, 0) for num in range(7)]
-        index, inside = pair_index(partner)
-        fetch = outer_values(load_aux, index, inside)
-        walls = wall_masks(sizes, 8 * group, place, count, partner)
-        speed_sq = GRAVITY * depth
-        outer_sq = [jnp.where(walls[k], speed_sq, GRAVITY * fetch[k](0)) for k in range(3)]
-        faces = ((sx, sy), (rx + sx, ry + sy), (rx, ry))
-        squares = [vx * vx + vy * vy for vx, vy in faces]
-        waves = [
-            0.5 * jnp.sqrt(squares[k]) * jnp.sqrt(jnp.maximum(speed_sq, outer_sq[k])) for k in range(3)
-        ]
-        ghosts = [8.0 / squares[k] for k in range(3)]
-        geo = [speed_sq, rx, ry, sx, sy, *outer_sq, *waves, *ghosts]
-        rates = tendency(load, geo, walls, index, inside, diff_ref, lift_ref)
-        at = pl.ds(pl.multiple_of(8 * group, 8), 8)
-        for num, value in enumerate([*geo, partner, refine]):
-            geo_ref[num, at, :] = value
-        for item in range(30):
-            rate_ref[item, at, :] = rates[item]
-        return carry
-
-    lax.fori_loop(0, sizes.rows // 8, step, 0)
-
-
 def child_matrix(prolong_ref):
     f32 = jnp.float32
     node_r = lax.broadcasted_iota(jnp.int32, (PACK, 10), 0) // 4
@@ -286,59 +214,172 @@
     return jnp.concatenate([rounded, rounded, rounded, rest], axis=1)
 
 
+def sum_children(sizes, refine, ends_ref):
+    slots, f32 = sizes.slots, jnp.float32
+    counts = (1.0 + refine).astype(jnp.bfloat16)
+    row_i = lax.broadcasted_iota(jnp.int32, (LANES, LANES), 0)
+    col_i = lax.broadcasted_iota(jnp.int32, (LANES, LANES), 1)
+    upper = (row_i <= col_i).astype(jnp.bfloat16)
+    within = jnp.dot(counts, upper, preferred_element_type=f32)
+    whole = jnp.dot(counts, jnp.ones((LANES, LANES), jnp.bfloat16), preferred_element_type=f32)
+    row_s = lax.broadcasted_iota(jnp.int32, (slots, slots), 0)
+    col_s = lax.broadcasted_iota(jnp.int32, (slots, slots), 1)
+    lower = (col_s < row_s).astype(jnp.bfloat16)
+    before = jnp.dot(lower, whole.astype(jnp.bfloat16), preferred_element_type=f32)
+    before = before - before[sizes.margin : sizes.margin + 1, :]
+    ends_ref[0] = 2.0 * (within + before) + refine
+    ends_ref[1] = before + whole
+
+
+def first_kernel(
+    sizes, state_hbm, depth_hbm, metric_hbm, partner_hbm, refine_hbm, even_ref, odd_ref, diff_hbm, lift_hbm, prolong_hbm,
+    cur, rate_ref, geo_ref, weights, ends_ref,
+    state_ref, depth_ref, metric_ref, partner_ref, refine_ref, diff_ref, lift_ref, prolong_ref,
+    spread, wide, aux, sems,
+):
+    blocks, halo = sizes.blocks, sizes.halo
+    top, bottom = PAD + halo, PAD + halo + blocks
+    place = lax.axis_index(AXES)
+    count = lax.axis_size(AXES)
+    copies = fetch_all(
+        (
+            (metric_hbm, metric_ref),
+            (state_hbm, state_ref),
+            (depth_hbm, depth_ref),
+            (partner_hbm, partner_ref),
+            (refine_hbm, refine_ref),
+            (diff_hbm, diff_ref),
+            (lift_hbm, lift_ref),
+            (prolong_hbm, prolong_ref),
+        ),
+        sems,
+    )
+    for copy in copies:
+        copy.wait()
+    metric = split_metric(metric_ref, spread, blocks)
+    dense = [depth_ref[...], *metric, partner_ref[...].astype(jnp.float32), refine_ref[...].astype(jnp.float32)]
+    pack_state(state_ref, wide, blocks)
+    even = place % 2 == 0
+
+    def set_halo(target, num, row):
+        by_even = even_ref[pl.ds(row, halo, stride=PACK), :]
+        by_odd = odd_ref[pl.ds(row, halo, stride=PACK), :]
+        target[num, top - halo : top, :] = jnp.where(even, by_odd, by_even)
+        target[num, bottom : bottom + halo, :] = jnp.where(even, by_even, by_odd)
+
+    for num in range(7):
+        set_halo(aux, num, 4 * num + 3)
+        aux[num, top:bottom, :] = dense[num]
+    for field in range(3):
+        for node in range(10):
+            item = 10 * field + node
+            set_halo(cur, item, 4 * node + field)
+            cur[item, top:bottom, :] = wide[pl.ds(4 * node + field, blocks, stride=PACK), :]
+
+    weights[...] = child_matrix(prolong_ref)
+    begin = PAD + sizes.keep
+    sum_children(sizes, aux[6, begin : begin + sizes.slots, :], ends_ref)
+
+    def step(group, carry):
+        base = PAD + 8 * group
+
+        def load_aux(item, shift):
+            return aux[item, pl.ds(base + shift, 8), :]
+
+        def load(item, shift):
+            return cur[item, pl.ds(base + shift, 8), :]
+
+        depth, rx, ry, sx, sy, partner = [load_aux(num, 0) for num in range(6)]
+        index, inside = pair_index(partner)
+        fetch = outer_values(load_aux, index, inside)
+        walls = wall_masks(sizes, 8 * group, place, count, partner)
+        speed_sq = GRAVITY * depth
+        outer_sq = [jnp.where(walls[k], speed_sq, GRAVITY * fetch[k](0)) for k in range(3)]
+        faces = ((sx, sy), (rx + sx, ry + sy), (rx, ry))
+        squares = [vx * vx + vy * vy for vx, vy in faces]
+        waves = [
+            0.5 * jnp.sqrt(squares[k]) * jnp.sqrt(jnp.maximum(speed_sq, outer_sq[k])) for k in range(3)
+        ]
+        ghosts = [8.0 / squares[k] for k in range(3)]
+        geo = [speed_sq, rx, ry, sx, sy, *outer_sq, *waves, *ghosts]
+        rates = tendency(load, geo, walls, index, inside, diff_ref, lift_ref)
+        at = pl.ds(pl.multiple_of(8 * group, 8), 8)
+        for num, value in enumerate([*geo, partner]):
+            geo_ref[num, at, :] = value
+        for item in range(30):
+            rate_ref[item, at, :] = rates[item]
+        return carry
+
+    lax.fori_loop(0, sizes.rows // 8, step, 0)
+
+
 def second_kernel(
-    sizes, cur, rate_ref, geo_ref, stats_hbm, diff_hbm, lift_hbm, prolong_hbm, out_hbm,
-    stats_ref, diff_ref, lift_ref, prolong_ref, out_ref,
-    first, ends_ref, place_v, place_s, wide, weights, gathered, index_ref, sems, out_sems, sem,
+    sizes, cur, rate_ref, geo_ref, weights, base_ref, stats_ref, diff_hbm, lift_hbm, out_hbm,
+    diff_ref, lift_ref, out_ref, first, ends_ref, place_v, place_s, wide, pair_ref, gathered, index_ref,
+    sems, out_sems, sem,
 ):
     slots, keep, rows = sizes.slots, sizes.keep, sizes.rows
     place = lax.axis_index(AXES)
     count = lax.axis_size(AXES)
-    copies = fetch_all(
-        ((prolong_hbm, prolong_ref), (stats_hbm, stats_ref), (diff_hbm, diff_ref), (lift_hbm, lift_ref)), sems
-    )
-    for item in (30, 31):
-        wide[pl.ds(item, slots + 1, stride=WIDE), :] = jnp.zeros((slots + 1, LANES), jnp.float32)
-    copies[0].wait()
-    weights[...] = child_matrix(prolong_ref)
-    for copy in copies[1:]:
-        copy.wait()
+    copies = fetch_all(((diff_hbm, diff_ref), (lift_hbm, lift_ref)), sems)
     stats = stats_ref[...]
-    lane_n = lax.broadcasted_iota(jnp.int32, stats.shape, 1)
+    half = LANES // 2
     row_n = lax.broadcasted_iota(jnp.int32, stats.shape, 0)
-    rate = jnp.where(lane_n < LANES // 2, stats, 0.0)
-    top = jnp.max(jnp.max(rate, axis=0, keepdims=True), axis=1, keepdims=True)
-    gone = jnp.where((lane_n == LANES - 1) & (row_n % 8 == 0) & (row_n < 8 * place), stats, 0.0)
-    earlier = jnp.sum(jnp.sum(gone, axis=0, keepdims=True), axis=1, keepdims=True)
+    top = jnp.max(stats, axis=0, keepdims=True)
+    earlier = jnp.sum(jnp.where(row_n < place, stats, 0.0), axis=0, keepdims=True)
+    left = lax.broadcasted_iota(jnp.int32, (1, LANES), 1) < half
+    top = jnp.where(left, top, pltpu.roll(top, half, 1))
+    earlier = jnp.where(left, pltpu.roll(earlier, half, 1), earlier)
     step = COURANT / top
-    refine = geo_ref[15, keep : keep + slots, :]
-    counts = (1.0 + refine).astype(jnp.bfloat16)
-    row_i = lax.broadcasted_iota(jnp.int32, (LANES, LANES), 0)
-    col_i = lax.broadcasted_iota(jnp.int32, (LANES, LANES), 1)
-    upper = (row_i <= col_i).astype(jnp.bfloat16)
-    within = jnp.dot(counts, upper, preferred_element_type=jnp.float32)
-    whole = jnp.dot(counts, jnp.ones((LANES, LANES), jnp.bfloat16), preferred_element_type=jnp.float32)
-    row_s = lax.broadcasted_iota(jnp.int32, (slots, slots), 0)
-    col_s = lax.broadcasted_iota(jnp.int32, (slots, slots), 1)
-    lower = (col_s < row_s).astype(jnp.bfloat16)
-    before = jnp.dot(lower, whole.astype(jnp.bfloat16), preferred_element_type=jnp.float32)
-    own = before[sizes.margin : sizes.margin + 1, :]
     start = earlier - (place * (sizes.cells // 2)).astype(jnp.float32)
-    ends = within + before + (start - own)
-    ends_ref[:slots, :] = 2.0 * ends + refine
+    ends_ref[:slots, :] = base_ref[0] + 2.0 * start
     ends_ref[slots:, :] = jnp.full((8, LANES), 1e9, jnp.float32)
-    full = before + whole + (start - own)
     first_slot = LANES * lax.broadcasted_iota(jnp.int32, (slots, LANES), 1).astype(jnp.float32)
-    lead = jnp.sum((full <= first_slot).astype(jnp.float32), axis=0, keepdims=True)
+    lead = jnp.sum((base_ref[1] + start <= first_slot).astype(jnp.float32), axis=0, keepdims=True)
     lead = jnp.clip(lead.astype(jnp.int32), 0, slots - 1)
     place_v[...] = jnp.broadcast_to(lead, (8, LANES))
     copy = pltpu.make_async_copy(place_v, place_s, sem)
     copy.start()
+    for item in (30, 31):
+        wide[pl.ds(item, slots + 1, stride=WIDE), :] = jnp.zeros((slots + 1, LANES), jnp.float32)
 
     for item in range(30):
         first[item, PAD : PAD + rows, :] = cur[item, PAD : PAD + rows, :] + step * rate_ref[item]
 
+    copy.wait()
+    for fetched in copies:
+        fetched.wait()
+
+    def search(group):
+        for sub in range(8):
+            lead_at = place_s[0, 8 * group + sub]
+            pair_ref[0, sub : sub + 1, :] = ends_ref[pl.ds(lead_at, 1), :]
+            pair_ref[1, sub : sub + 1, :] = ends_ref[pl.ds(lead_at + 1, 1), :]
+        near, far = pair_ref[0], pair_ref[1]
+        row = lax.broadcasted_iota(jnp.int32, (8, LANES), 0) + 8 * group
+        slot_no = LANES * row + lax.broadcasted_iota(jnp.int32, (8, LANES), 1)
+        goal = (2 * slot_no + 1).astype(jnp.float32)
+        beyond = jnp.broadcast_to(near[:, LANES - 1 :], (8, LANES)) <= goal
+
+        def pick(index):
+            return jnp.where(beyond, lane_gather(far, index), lane_gather(near, index))
+
+        found = jnp.zeros((8, LANES), jnp.int32)
+        size = LANES // 2
+        while size:
+            passed = pick(found + (size - 1)) <= goal
+            found = jnp.where(passed, found + size, found)
+            size //= 2
+        mine = pick(found).astype(jnp.int32)
+        split = mine & 1
+        begin = (mine >> 1) - 1 - split
+        at = pl.ds(pl.multiple_of(8 * group, 8), 8)
+        index_ref[0, at, :] = found.astype(jnp.float32)
+        index_ref[1, at, :] = (split * (1 + slot_no - begin)).astype(jnp.float32)
+        index_ref[2, at, :] = beyond.astype(jnp.float32)
+
     def stage(group, carry):
+        search(group)
         base = PAD + keep + 8 * group
         at = pl.ds(8 * group + keep, 8)
 
@@ -361,34 +402,6 @@
 
     lax.fori_loop(0, slots // 8, stage, 0)
 
-    copy.wait()
-    for slot in range(slots):
-        lead_at = place_s[0, slot]
-        index_ref[0, slot : slot + 1, :] = ends_ref[pl.ds(lead_at, 1), :]
-        index_ref[1, slot : slot + 1, :] = ends_ref[pl.ds(lead_at + 1, 1), :]
-    near, far = index_ref[0], index_ref[1]
-    slot_no = LANES * lax.broadcasted_iota(jnp.int32, (slots, LANES), 0) + lax.broadcasted_iota(
-        jnp.int32, (slots, LANES), 1
-    )
-    goal = (2 * slot_no + 1).astype(jnp.float32)
-    beyond = jnp.broadcast_to(near[:, LANES - 1 :], (slots, LANES)) <= goal
-
-    def pick(index):
-        return jnp.where(beyond, lane_gather(far, index), lane_gather(near, index))
-
-    found = jnp.zeros((slots, LANES), jnp.int32)
-    size = LANES // 2
-    while size:
-        passed = pick(found + (size - 1)) <= goal
-        found = jnp.where(passed, found + size, found)
-        size //= 2
-    mine = pick(found).astype(jnp.int32)
-    split = mine & 1
-    begin = (mine >> 1) - 1 - split
-    kind = split * (1 + slot_no - begin)
-    index_ref[0] = found.astype(jnp.float32)
-    index_ref[1] = kind.astype(jnp.float32)
-    index_ref[2] = beyond.astype(jnp.float32)
     for slot in range(slots):
         lead_at = place_s[0, slot] * WIDE
         lane_idx = jnp.broadcast_to(index_ref[0, slot : slot + 1, :], (WIDE, LANES)).astype(jnp.int32)
@@ -454,70 +467,72 @@
     stats, even, odd = pl.pallas_call(
         functools.partial(pack_kernel, sizes),
         name="pack",
-        out_shape=(jax.ShapeDtypeStruct((8, LANES), f32), packed, packed),
+        out_shape=(jax.ShapeDtypeStruct((count, LANES), f32), packed, packed),
         in_specs=[HBM] * 5,
-        out_specs=(VMEM,) * 3,
+        out_specs=(HBM, VMEM, VMEM),
         scratch_shapes=[
+            pltpu.VMEM((count, LANES), f32),
             pltpu.VMEM((10, 3, LANES * halo), f32),
             pltpu.VMEM((10, 3, LANES * halo), f32),
             *dense,
             pltpu.VMEM((8 * blocks, LANES), f32),
             pltpu.SemaphoreType.DMA((6,)),
+            pltpu.SemaphoreType.DMA,
         ],
         compiler_params=PARAMS,
     )(state, depth, metric, partner, refine)
-    stats = lax.all_gather(stats, AXES, tiled=True)
     even = lax.ppermute(even, AXES, swaps(0, count))
     odd = lax.ppermute(odd, AXES, swaps(1, count))
-    even, odd = [pltpu.with_memory_space_constraint(x, pltpu.VMEM) for x in (even, odd)]
-    stats = pltpu.with_memory_space_constraint(stats, pltpu.HBM)
+    stats = lax.all_to_all(stats, AXES, 0, 0, tiled=True)
+    even, odd, stats = [pltpu.with_memory_space_constraint(x, pltpu.VMEM) for x in (even, odd, stats)]
     operators = [pltpu.SMEM(diff_ops.shape, f32), pltpu.SMEM(lift.shape, f32)]
-    cur, rates, geo = pl.pallas_call(
+    cur, rates, geo, weights, ends = pl.pallas_call(
         functools.partial(first_kernel, sizes),
         name="first_stage",
         out_shape=(
             jax.ShapeDtypeStruct((30, sizes.tall, LANES), f32),
             jax.ShapeDtypeStruct((30, rows, LANES), f32),
-            jax.ShapeDtypeStruct((16, rows, LANES), f32),
+            jax.ShapeDtypeStruct((15, rows, LANES), f32),
+            jax.ShapeDtypeStruct((3 * PACK, 4 * WIDE), jnp.bfloat16),
+            jax.ShapeDtypeStruct((2, slots, LANES), f32),
         ),
-        in_specs=[HBM] * 5 + [VMEM] * 2 + [HBM] * 2,
-        out_specs=(VMEM,) * 3,
+        in_specs=[HBM] * 5 + [VMEM] * 2 + [HBM] * 3,
+        out_specs=(VMEM,) * 5,
         scratch_shapes=[
             pltpu.VMEM(state.shape, f32),
             *dense,
             *operators,
+            pltpu.VMEM(prolong.shape, f32),
             pltpu.VMEM((8 * blocks, LANES), f32),
             pltpu.VMEM((PACK * blocks, LANES), f32),
             pltpu.VMEM((7, sizes.tall, LANES), f32),
-            pltpu.SemaphoreType.DMA((7,)),
+            pltpu.SemaphoreType.DMA((8,)),
         ],
         compiler_params=PARAMS,
-    )(state, depth, metric, partner, refine, even, odd, diff_ops, lift)
+    )(state, depth, metric, partner, refine, even, odd, diff_ops, lift, prolong)
     refined = pl.pallas_call(
         functools.partial(second_kernel, sizes),
         name="second_stage_refine",
         out_shape=jax.ShapeDtypeStruct((10, 3, LANES * slots), f32),
-        in_specs=[VMEM] * 3 + [HBM] * 4,
+        in_specs=[VMEM] * 6 + [HBM] * 2,
         out_specs=HBM,
         scratch_shapes=[
-            pltpu.VMEM(stats.shape, f32),
             *operators,
-            pltpu.VMEM(prolong.shape, f32),
             pltpu.VMEM((10, 3, LANES * slots), f32),
             pltpu.VMEM((30, sizes.tall, LANES), f32),
             pltpu.VMEM((slots + 8, LANES), f32),
             pltpu.VMEM((8, LANES), i32),
             pltpu.SMEM((8, LANES), i32),
             pltpu.VMEM((WIDE * (slots + 1), LANES), f32),
-            pltpu.VMEM((3 * PACK, 4 * WIDE), jnp.bfloat16),
+            pltpu.VMEM((2, 8, LANES), f32),
             pltpu.VMEM((WIDE, LANES * slots), f32),
             pltpu.VMEM((3, slots, LANES), f32),
-            pltpu.SemaphoreType.DMA((4,)),
+            pltpu.SemaphoreType.DMA((2,)),
             pltpu.SemaphoreType.DMA((slots // 8,)),
             pltpu.SemaphoreType.DMA,
         ],
         compiler_params=PARAMS,
-    )(cur, rates, geo, stats, diff_ops, lift, prolong)
+    )(cur, rates, geo, weights, ends, stats, diff_ops, lift)
     return jnp.transpose(refined, (1, 0, 2))
 
 

time: 61.2 us -> 26.3 us (0.43)
  blocking collectives: 47.8 us -> 0 us
  starting transfers between devices: 1.18 us -> 9.91 us
  waiting for transfers between devices: 0.01 us -> 2.56 us
  Pallas kernels: 11.9 us -> 13.4 us
    all_gather x1 -> x0, blocking collectives: 47.8 us -> none  [shards(): stats = lax.all_gather(stats, AXES, tiled=True)]
    all_to_all x0 -> x1, starting transfers between devices: none -> 8.74 us  [shards(): stats = lax.all_to_all(stats, AXES, 0, 0, tiled=True)]
    all_to_all x0 -> x1, waiting for transfers between devices: none -> 2.56 us  [shards(): stats = lax.all_to_all(stats, AXES, 0, 0, tiled=True)]
    pallas_call x1, Pallas kernels: 6.66 us -> 7.29 us  [shards(): pl.pallas_call(functools.partial(second_kernel, sizes), name='second_stag...]
  transfers between devices with their start and end apart: 2 -> 3, of which waited for: 0 -> 1; matrix products, arithmetic and copies ran while one was open for 0% -> 0% of each run, Pallas kernels for 0% -> 17%
where the time goes in v2:
time: 26.3 us; the launch traced here: 25.9 us
  Pallas kernels  13.4 us (51%)
  starting transfers between devices  9.91 us (38%)
  waiting for transfers between devices  2.56 us (10%)
    all_to_all x1, starting transfers between devices, shards(): stats = lax.all_to_all(stats, AXES, 0, 0, tiled=True)  8.74 us
    pallas_call x1, Pallas kernels, shards(): pl.pallas_call(functools.partial(second_kernel, sizes), name='second_stag...  7.29 us
    pallas_call x1, Pallas kernels, shards(): pl.pallas_call(functools.partial(first_kernel, sizes), name='first_stage'...  4.48 us
    all_to_all x1, waiting for transfers between devices, shards(): stats = lax.all_to_all(stats, AXES, 0, 0, tiled=True)  2.56 us
    pallas_call x1, Pallas kernels, shards(): pl.pallas_call(functools.partial(pack_kernel, sizes), name='pack', out_sh...  1.65 us
    ppermute x1, starting transfers between devices, shards(): odd = lax.ppermute(odd, AXES, swaps(1, count))  0.66 us
  transfers between devices with their start and end apart: 3, of which 1 were waited for; matrix products, arithmetic and copies ran while one was open for 0% of the time, Pallas kernels for 17%

profile of v2, /device:TPU:0, one launch (start us, length us, event | category | flops | bytes accessed | tf_op | source)
XLA Modules:
  0.0 25.9 jit_solution(1161711071917191410)
XLA Ops:
  0.0 1.7 %pack.1 = (f32[32,128]{1,0:T(8,128)}, f32[360,128]{1,0:T(8,128)S(1)}, f32[360,128]{1,0:T(8,128)S(1)}) custom-call(f32[10,3,4096]{2,1,0:T(4,128)} %bitcast.12, f32[32,128]{1,0:T(8,128)} %bitcast.14, f32[4,4096]{1,0:T(4,128)} %metric_hbm.3, s32[32,128]{1,0:T(8,128)} %bitcast.16, s32[32,128]{1,0:T(8,128)} %bitcast.18), custom_call_target="tpu_custom_call" | custom-call | tf_op jit(solution)/shard_map/pack/pallas_call | solution.py:467
  1.7 0.5 %collective-permute-start = (f32[360,128]{1,0:T(8,128)S(1)}, f32[360,128]{1,0:T(8,128)S(1)}, u32[]{:S(2)}, u32[]{:S(2)}) collective-permute-start(f32[360,128]{1,0:T(8,128)S(1)} %get-tuple-element.13), channel_id=1, source_target_pairs={{0,1},{2,3},{4,5},{6,7},{8,9},{10,11},{12,13},{14,15},{16,17},{18,... | collective-permute-start | bytes 552968 | tf_op jit(solution)/shard_map/ppermute | solution.py:484
  2.2 0.7 %collective-permute-start.1 = (f32[360,128]{1,0:T(8,128)S(1)}, f32[360,128]{1,0:T(8,128)S(1)}, u32[]{:S(2)}, u32[]{:S(2)}) collective-permute-start(f32[360,128]{1,0:T(8,128)S(1)} %get-tuple-element.14), channel_id=1, source_target_pairs={{1,2},{3,4},{5,6},{7,8},{9,10},{11,12},{13,14},{15,16},{17,18},{19... | collective-permute-start | bytes 552968 | tf_op jit(solution)/shard_map/ppermute | solution.py:485
  2.8 8.7 %all-to-all-start = ((f32[32,1,128]{2,1,0:T(1,128)}), f32[32,1,128]{2,1,0:T(1,128)S(1)}, u32[]{:S(2)}, u32[]{:S(2)}) async-start(f32[32,1,128]{2,1,0:T(1,128)} %bitcast.7), calls=%async_computation | async-start | bytes 32768 | tf_op jit(solution)/shard_map/all_to_all | solution.py:486
  11.6 0.0 collective-permute-done.even_ref
  11.6 0.0 collective-permute-done.1.odd_ref
  11.6 4.5 %first_stage.1 = (f32[30,72,128]{2,1,0:T(8,128)S(1)}, f32[30,56,128]{2,1,0:T(8,128)S(1)}, f32[15,56,128]{2,1,0:T(8,128)S(1)}, bf16[120,128]{1,0:T(8,128)(2,1)S(1)}, f32[2,48,128]{2,1,0:T(8,128)S(1)}) custom-call(f32[10,3,4096]{2,1,0:T(4,128)} %bitcast.13, f32[32,128]{1,0:T(8,128)} %bitcast.15, f32[4,4096]{1,0:T(4,128)} %metric_hbm.3, s32[32,128]{1,0:T(8,128)} %bitcast.17, ...), custom_call_target="tpu_custom_call" | custom-call | tf_op jit(solution)/shard_map/first_stage/pallas_call | solution.py:489
  16.1 2.6 %all-to-all-done = f32[32,1,128]{2,1,0:T(1,128)S(1)} async-done(((f32[32,1,128]{2,1,0:T(1,128)}), f32[32,1,128]{2,1,0:T(1,128)S(1)}, u32[]{:S(2)}, u32[]{:S(2)}) %all-to-all-start) | async-done | bytes 16416 | tf_op jit(solution)/shard_map/all_to_all | solution.py:486
  18.7 7.3 %second_stage_refine.1 = f32[10,3,6144]{2,1,0:T(4,128)} custom-call(f32[30,72,128]{2,1,0:T(8,128)S(1)} %get-tuple-element.15.cur, f32[30,56,128]{2,1,0:T(8,128)S(1)} %get-tuple-element.16.rate_ref, f32[15,56,128]{2,1,0:T(8,128)S(1)} %get-tuple-element.17.geo_ref, bf16[120,128]{1,0:T(8,128)(2,1)S(1)} %get-tuple-element.18.weights, ...), custom_call_target="tpu_custom_call" | custom-call | tf_op jit(solution)/shard_map/second_stage_refine/pallas_call | solution.py:513
Async XLA Ops:
  1.7 9.9 %collective-permute-start = (f32[360,128]{1,0:T(8,128)S(1)}, f32[360,128]{1,0:T(8,128)S(1)}, u32[]{:S(2)}, u32[]{:S(2)}) collective-permute-start(f32[360,128]{1,0:T(8,128)S(1)} %get-tuple-element.13), channel_id=1, source_target_pairs={{0,1},{2,3},{4,5},{6,7},{8,9},{10,11},{12,13},{14,15},{16,17},{18,... | collective-permute-start | bytes 552968 | tf_op jit(solution)/shard_map/ppermute | solution.py:484
  2.2 9.4 %collective-permute-start.1 = (f32[360,128]{1,0:T(8,128)S(1)}, f32[360,128]{1,0:T(8,128)S(1)}, u32[]{:S(2)}, u32[]{:S(2)}) collective-permute-start(f32[360,128]{1,0:T(8,128)S(1)} %get-tuple-element.14), channel_id=1, source_target_pairs={{1,2},{3,4},{5,6},{7,8},{9,10},{11,12},{13,14},{15,16},{17,18},{19... | collective-permute-start | bytes 552968 | tf_op jit(solution)/shard_map/ppermute | solution.py:485
  2.8 15.8 %all-to-all-start = ((f32[32,1,128]{2,1,0:T(1,128)}), f32[32,1,128]{2,1,0:T(1,128)S(1)}, u32[]{:S(2)}, u32[]{:S(2)}) async-start(f32[32,1,128]{2,1,0:T(1,128)} %bitcast.7), calls=%async_computation | async-start | bytes 32768 | tf_op jit(solution)/shard_map/all_to_all | solution.py:486

commit v3 on v2

--- a/solution.py
+++ b/solution.py
@@ -232,9 +232,9 @@
 
 
 def first_kernel(
-    sizes, state_hbm, depth_hbm, metric_hbm, partner_hbm, refine_hbm, even_ref, odd_ref, diff_hbm, lift_hbm, prolong_hbm,
-    cur, rate_ref, geo_ref, weights, ends_ref,
-    state_ref, depth_ref, metric_ref, partner_ref, refine_ref, diff_ref, lift_ref, prolong_ref,
+    sizes, state_hbm, depth_hbm, metric_hbm, partner_hbm, refine_hbm, odd_ref, even_ref, diff_hbm, lift_hbm, prolong_hbm,
+    cur, rate_ref, twice_ref, weights, ends_ref,
+    geo_ref, state_ref, depth_ref, metric_ref, partner_ref, refine_ref, diff_ref, lift_ref, prolong_ref,
     spread, wide, aux, sems,
 ):
     blocks, halo = sizes.blocks, sizes.halo
@@ -307,21 +307,36 @@
         for num, value in enumerate([*geo, partner]):
             geo_ref[num, at, :] = value
         for item in range(30):
-            rate_ref[item, at, :] = rates[item]
+            rate_ref[item, pl.ds(base, 8), :] = rates[item]
         return carry
 
     lax.fori_loop(0, sizes.rows // 8, step, 0)
 
-
-def second_kernel(
-    sizes, cur, rate_ref, geo_ref, weights, base_ref, stats_ref, diff_hbm, lift_hbm, out_hbm,
-    diff_ref, lift_ref, out_ref, first, ends_ref, place_v, place_s, wide, pair_ref, gathered, index_ref,
-    sems, out_sems, sem,
+    def again(group, carry):
+        row = 8 * group + sizes.keep
+        at = pl.ds(row, 8)
+
+        def load(item, shift):
+            return rate_ref[item, pl.ds(PAD + row + shift, 8), :]
+
+        geo = [geo_ref[num, at, :] for num in range(14)]
+        partner = geo_ref[14, at, :]
+        index, inside = pair_index(partner)
+        walls = wall_masks(sizes, row, place, count, partner)
+        rates = tendency(load, geo, walls, index, inside, diff_ref, lift_ref)
+        for item in range(30):
+            twice_ref[item, pl.ds(pl.multiple_of(8 * group, 8), 8), :] = rates[item]
+        return carry
+
+    lax.fori_loop(0, sizes.slots // 8, again, 0)
+
+
+def refine_kernel(
+    sizes, cur, rate_ref, twice_ref, weights, base_ref, stats_ref, out_hbm,
+    out_ref, ends_ref, place_v, place_s, wide, gathered, index_ref, out_sems, sem,
 ):
-    slots, keep, rows = sizes.slots, sizes.keep, sizes.rows
+    slots, keep = sizes.slots, sizes.keep
     place = lax.axis_index(AXES)
-    count = lax.axis_size(AXES)
-    copies = fetch_all(((diff_hbm, diff_ref), (lift_hbm, lift_ref)), sems)
     stats = stats_ref[...]
     half = LANES // 2
     row_n = lax.broadcasted_iota(jnp.int32, stats.shape, 0)
@@ -331,6 +346,7 @@
     top = jnp.where(left, top, pltpu.roll(top, half, 1))
     earlier = jnp.where(left, pltpu.roll(earlier, half, 1), earlier)
     step = COURANT / top
+    half_square = 0.5 * step * step
     start = earlier - (place * (sizes.cells // 2)).astype(jnp.float32)
     ends_ref[:slots, :] = base_ref[0] + 2.0 * start
     ends_ref[slots:, :] = jnp.full((8, LANES), 1e9, jnp.float32)
@@ -340,77 +356,49 @@
     place_v[...] = jnp.broadcast_to(lead, (8, LANES))
     copy = pltpu.make_async_copy(place_v, place_s, sem)
     copy.start()
+    for item in range(30):
+        now = slice(PAD + keep, PAD + keep + slots)
+        value = cur[item, now, :] + step * rate_ref[item, now, :] + half_square * twice_ref[item]
+        wide[pl.ds(item, slots, stride=WIDE), :] = value
     for item in (30, 31):
         wide[pl.ds(item, slots + 1, stride=WIDE), :] = jnp.zeros((slots + 1, LANES), jnp.float32)
-
-    for item in range(30):
-        first[item, PAD : PAD + rows, :] = cur[item, PAD : PAD + rows, :] + step * rate_ref[item]
-
     copy.wait()
-    for fetched in copies:
-        fetched.wait()
-
-    def search(group):
-        for sub in range(8):
-            lead_at = place_s[0, 8 * group + sub]
-            pair_ref[0, sub : sub + 1, :] = ends_ref[pl.ds(lead_at, 1), :]
-            pair_ref[1, sub : sub + 1, :] = ends_ref[pl.ds(lead_at + 1, 1), :]
-        near, far = pair_ref[0], pair_ref[1]
-        row = lax.broadcasted_iota(jnp.int32, (8, LANES), 0) + 8 * group
-        slot_no = LANES * row + lax.broadcasted_iota(jnp.int32, (8, LANES), 1)
-        goal = (2 * slot_no + 1).astype(jnp.float32)
-        beyond = jnp.broadcast_to(near[:, LANES - 1 :], (8, LANES)) <= goal
-
-        def pick(index):
-            return jnp.where(beyond, lane_gather(far, index), lane_gather(near, index))
-
-        found = jnp.zeros((8, LANES), jnp.int32)
-        size = LANES // 2
-        while size:
-            passed = pick(found + (size - 1)) <= goal
-            found = jnp.where(passed, found + size, found)
-            size //= 2
-        mine = pick(found).astype(jnp.int32)
-        split = mine & 1
-        begin = (mine >> 1) - 1 - split
-        at = pl.ds(pl.multiple_of(8 * group, 8), 8)
-        index_ref[0, at, :] = found.astype(jnp.float32)
-        index_ref[1, at, :] = (split * (1 + slot_no - begin)).astype(jnp.float32)
-        index_ref[2, at, :] = beyond.astype(jnp.float32)
-
-    def stage(group, carry):
-        search(group)
-        base = PAD + keep + 8 * group
-        at = pl.ds(8 * group + keep, 8)
-
-        def load(item, shift):
-            return first[item, pl.ds(base + shift, 8), :]
-
-        geo = [geo_ref[num, at, :] for num in range(14)]
-        partner = geo_ref[14, at, :]
-        index, inside = pair_index(partner)
-        walls = wall_masks(sizes, 8 * group + keep, place, count, partner)
-        rates = tendency(load, geo, walls, index, inside, diff_ref, lift_ref)
-        lead_row = 8 * WIDE * group
-        for field in range(3):
-            for node in range(10):
-                item = 10 * field + node
-                old = cur[item, pl.ds(base, 8), :]
-                new = 0.5 * old + 0.5 * (load(item, 0) + step * rates[item])
-                wide[pl.ds(lead_row + item, 8, stride=WIDE), :] = new
-        return carry
-
-    lax.fori_loop(0, slots // 8, stage, 0)
-
+    for slot in range(slots):
+        lead_at = place_s[0, slot]
+        index_ref[0, slot : slot + 1, :] = ends_ref[pl.ds(lead_at, 1), :]
+        index_ref[1, slot : slot + 1, :] = ends_ref[pl.ds(lead_at + 1, 1), :]
+    near, far = index_ref[0], index_ref[1]
+    lane = lax.broadcasted_iota(jnp.int32, (slots, LANES), 1)
+    slot_no = LANES * lax.broadcasted_iota(jnp.int32, (slots, LANES), 0) + lane
+    goal = (2 * slot_no + 1).astype(jnp.float32)
+    beyond = jnp.broadcast_to(near[:, LANES - 1 :], (slots, LANES)) <= goal
+
+    def pick(index):
+        return jnp.where(beyond, lane_gather(far, index), lane_gather(near, index))
+
+    found = jnp.zeros((slots, LANES), jnp.int32)
+    size = LANES // 2
+    while size:
+        passed = pick(found + (size - 1)) <= goal
+        found = jnp.where(passed, found + size, found)
+        size //= 2
+    mine = pick(found).astype(jnp.int32)
+    split = mine & 1
+    begin = (mine >> 1) - 1 - split
+    kind = split * (1 + slot_no - begin)
+    index_ref[0] = found.astype(jnp.float32)
+    index_ref[1] = kind.astype(jnp.float32)
+    index_ref[2] = (lane < jnp.broadcast_to(found[:, 0:1], (slots, LANES))).astype(jnp.float32)
     for slot in range(slots):
         lead_at = place_s[0, slot] * WIDE
-        lane_idx = jnp.broadcast_to(index_ref[0, slot : slot + 1, :], (WIDE, LANES)).astype(jnp.int32)
-        passed = jnp.broadcast_to(index_ref[2, slot : slot + 1, :], (WIDE, LANES)) > 0.5
-        one = wide[pl.ds(pl.multiple_of(lead_at, WIDE), WIDE), :]
-        two = wide[pl.ds(pl.multiple_of(lead_at + WIDE, WIDE), WIDE), :]
-        gathered[:, LANES * slot : LANES * (slot + 1)] = jnp.where(
-            passed, lane_gather(two, lane_idx), lane_gather(one, lane_idx)
-        )
+        lane_idx = jnp.broadcast_to(index_ref[0, slot : slot + 1, :], (8, LANES)).astype(jnp.int32)
+        ahead = jnp.broadcast_to(index_ref[2, slot : slot + 1, :], (8, LANES)) > 0.5
+        for part in range(0, WIDE, 8):
+            one = wide[pl.ds(pl.multiple_of(lead_at + part, 8), 8), :]
+            two = wide[pl.ds(pl.multiple_of(lead_at + WIDE + part, 8), 8), :]
+            gathered[part : part + 8, LANES * slot : LANES * (slot + 1)] = lane_gather(
+                jnp.where(ahead, two, one), lane_idx
+            )
     matrix = weights[...]
     chunk = 8 * LANES
     results = []
@@ -481,27 +469,28 @@
         ],
         compiler_params=PARAMS,
     )(state, depth, metric, partner, refine)
+    odd = lax.ppermute(odd, AXES, swaps(1, count))
     even = lax.ppermute(even, AXES, swaps(0, count))
-    odd = lax.ppermute(odd, AXES, swaps(1, count))
     stats = lax.all_to_all(stats, AXES, 0, 0, tiled=True)
     even, odd, stats = [pltpu.with_memory_space_constraint(x, pltpu.VMEM) for x in (even, odd, stats)]
-    operators = [pltpu.SMEM(diff_ops.shape, f32), pltpu.SMEM(lift.shape, f32)]
-    cur, rates, geo, weights, ends = pl.pallas_call(
+    cur, rates, twice, weights, ends = pl.pallas_call(
         functools.partial(first_kernel, sizes),
-        name="first_stage",
+        name="rates_twice",
         out_shape=(
             jax.ShapeDtypeStruct((30, sizes.tall, LANES), f32),
-            jax.ShapeDtypeStruct((30, rows, LANES), f32),
-            jax.ShapeDtypeStruct((15, rows, LANES), f32),
+            jax.ShapeDtypeStruct((30, sizes.tall, LANES), f32),
+            jax.ShapeDtypeStruct((30, slots, LANES), f32),
             jax.ShapeDtypeStruct((3 * PACK, 4 * WIDE), jnp.bfloat16),
             jax.ShapeDtypeStruct((2, slots, LANES), f32),
         ),
         in_specs=[HBM] * 5 + [VMEM] * 2 + [HBM] * 3,
         out_specs=(VMEM,) * 5,
         scratch_shapes=[
+            pltpu.VMEM((15, rows, LANES), f32),
             pltpu.VMEM(state.shape, f32),
             *dense,
-            *operators,
+            pltpu.SMEM(diff_ops.shape, f32),
+            pltpu.SMEM(lift.shape, f32),
             pltpu.VMEM(prolong.shape, f32),
             pltpu.VMEM((8 * blocks, LANES), f32),
             pltpu.VMEM((PACK * blocks, LANES), f32),
@@ -509,30 +498,26 @@
             pltpu.SemaphoreType.DMA((8,)),
         ],
         compiler_params=PARAMS,
-    )(state, depth, metric, partner, refine, even, odd, diff_ops, lift, prolong)
+    )(state, depth, metric, partner, refine, odd, even, diff_ops, lift, prolong)
     refined = pl.pallas_call(
-        functools.partial(second_kernel, sizes),
-        name="second_stage_refine",
+        functools.partial(refine_kernel, sizes),
+        name="sum_and_refine",
         out_shape=jax.ShapeDtypeStruct((10, 3, LANES * slots), f32),
-        in_specs=[VMEM] * 6 + [HBM] * 2,
+        in_specs=[VMEM] * 6,
         out_specs=HBM,
         scratch_shapes=[
-            *operators,
             pltpu.VMEM((10, 3, LANES * slots), f32),
-            pltpu.VMEM((30, sizes.tall, LANES), f32),
             pltpu.VMEM((slots + 8, LANES), f32),
             pltpu.VMEM((8, LANES), i32),
             pltpu.SMEM((8, LANES), i32),
             pltpu.VMEM((WIDE * (slots + 1), LANES), f32),
-            pltpu.VMEM((2, 8, LANES), f32),
             pltpu.VMEM((WIDE, LANES * slots), f32),
             pltpu.VMEM((3, slots, LANES), f32),
-            pltpu.SemaphoreType.DMA((2,)),
             pltpu.SemaphoreType.DMA((slots // 8,)),
             pltpu.SemaphoreType.DMA,
         ],
         compiler_params=PARAMS,
-    )(cur, rates, geo, weights, ends, stats, diff_ops, lift)
+    )(cur, rates, twice, weights, ends, stats)
     return jnp.transpose(refined, (1, 0, 2))
 
 

time: 26.3 us -> 23.9 us (0.909)
  the two profiles are of different devices: /device:TPU:0 before, /device:TPU:4 now
where the time goes in v3:
time: 23.9 us; the launch traced here: 23.6 us
  Pallas kernels  11.7 us (49%)
  starting transfers between devices  8.74 us (37%)
  waiting for transfers between devices  3.11 us (13%)
    pallas_call x1, Pallas kernels, shards(): pl.pallas_call(functools.partial(first_kernel, sizes), name='rates_twice'...  6.45 us
    ppermute x1, starting transfers between devices, shards(): odd = lax.ppermute(odd, AXES, swaps(1, count))  5.82 us
    pallas_call x1, Pallas kernels, shards(): pl.pallas_call(functools.partial(refine_kernel, sizes), name='sum_and_ref...  3.58 us
    ppermute x1, waiting for transfers between devices, shards(): odd = lax.ppermute(odd, AXES, swaps(1, count))  3.11 us
    all_to_all x1, starting transfers between devices, shards(): stats = lax.all_to_all(stats, AXES, 0, 0, tiled=True)  2.85 us
    pallas_call x1, Pallas kernels, shards(): pl.pallas_call(functools.partial(pack_kernel, sizes), name='pack', out_sh...  1.65 us
  transfers between devices with their start and end apart: 3, of which 1 were waited for; matrix products, arithmetic and copies ran while one was open for 0% of the time, Pallas kernels for 27%

profile of v3, /device:TPU:4, one launch (start us, length us, event | category | flops | bytes accessed | tf_op | source)
XLA Modules:
  0.0 23.6 jit_solution(17978895008943354181)
XLA Ops:
  0.0 1.7 %pack.1 = (f32[32,128]{1,0:T(8,128)}, f32[360,128]{1,0:T(8,128)S(1)}, f32[360,128]{1,0:T(8,128)S(1)}) custom-call(f32[10,3,4096]{2,1,0:T(4,128)} %bitcast.12, f32[32,128]{1,0:T(8,128)} %bitcast.14, f32[4,4096]{1,0:T(4,128)} %metric_hbm.3, s32[32,128]{1,0:T(8,128)} %bitcast.16, s32[32,128]{1,0:T(8,128)} %bitcast.18), custom_call_target="tpu_custom_call" | custom-call | tf_op jit(solution)/shard_map/pack/pallas_call | solution.py:455
  1.7 5.8 %collective-permute-start = (f32[360,128]{1,0:T(8,128)S(1)}, f32[360,128]{1,0:T(8,128)S(1)}, u32[]{:S(2)}, u32[]{:S(2)}) collective-permute-start(f32[360,128]{1,0:T(8,128)S(1)} %get-tuple-element.13), channel_id=1, source_target_pairs={{1,2},{3,4},{5,6},{7,8},{9,10},{11,12},{13,14},{15,16},{17,18},{19... | collective-permute-start | bytes 552968 | tf_op jit(solution)/shard_map/ppermute | solution.py:472
  7.5 0.1 collective-permute-start.1
  7.6 2.9 %all-to-all-start = ((f32[32,1,128]{2,1,0:T(1,128)}), f32[32,1,128]{2,1,0:T(1,128)S(1)}, u32[]{:S(2)}, u32[]{:S(2)}) async-start(f32[32,1,128]{2,1,0:T(1,128)} %bitcast.7), calls=%async_computation | async-start | bytes 32768 | tf_op jit(solution)/shard_map/all_to_all | solution.py:474
  10.4 3.1 %collective-permute-done.odd_ref = f32[360,128]{1,0:T(8,128)S(1)} collective-permute-done((f32[360,128]{1,0:T(8,128)S(1)}, f32[360,128]{1,0:T(8,128)S(1)}, u32[]{:S(2)}, u32[]{:S(2)}) %collective-permute-start) | collective-permute-done | bytes 184352 | tf_op jit(solution)/shard_map/ppermute | solution.py:472
  13.5 0.0 collective-permute-done.1.even_ref
  13.5 6.5 %rates_twice.1 = (f32[30,72,128]{2,1,0:T(8,128)S(1)}, f32[30,72,128]{2,1,0:T(8,128)S(1)}, f32[30,48,128]{2,1,0:T(8,128)S(1)}, bf16[120,128]{1,0:T(8,128)(2,1)S(1)}, f32[2,48,128]{2,1,0:T(8,128)S(1)}) custom-call(f32[10,3,4096]{2,1,0:T(4,128)} %bitcast.13, f32[32,128]{1,0:T(8,128)} %bitcast.15, f32[4,4096]{1,0:T(4,128)} %metric_hbm.3, s32[32,128]{1,0:T(8,128)} %bitcast.17, ...), custom_call_target="tpu_custom_call" | custom-call | tf_op jit(solution)/shard_map/rates_twice/pallas_call | solution.py:476
  20.0 0.0 all-to-all-done
  20.0 3.6 %sum_and_refine.1 = f32[10,3,6144]{2,1,0:T(4,128)} custom-call(f32[30,72,128]{2,1,0:T(8,128)S(1)} %get-tuple-element.15.cur, f32[30,72,128]{2,1,0:T(8,128)S(1)} %get-tuple-element.16.rate_ref, f32[30,48,128]{2,1,0:T(8,128)S(1)} %get-tuple-element.17.twice_ref, bf16[120,128]{1,0:T(8,128)(2,1)S(1)} %get-tuple-element.18.weights, ...), custom_call_target="tpu_custom_call" | custom-call | tf_op jit(solution)/shard_map/sum_and_refine/pallas_call | solution.py:502
Async XLA Ops:
  1.7 11.9 %collective-permute-start = (f32[360,128]{1,0:T(8,128)S(1)}, f32[360,128]{1,0:T(8,128)S(1)}, u32[]{:S(2)}, u32[]{:S(2)}) collective-permute-start(f32[360,128]{1,0:T(8,128)S(1)} %get-tuple-element.13), channel_id=1, source_target_pairs={{1,2},{3,4},{5,6},{7,8},{9,10},{11,12},{13,14},{15,16},{17,18},{19... | collective-permute-start | bytes 552968 | tf_op jit(solution)/shard_map/ppermute | solution.py:472
  7.5 6.1 %collective-permute-start.1 = (f32[360,128]{1,0:T(8,128)S(1)}, f32[360,128]{1,0:T(8,128)S(1)}, u32[]{:S(2)}, u32[]{:S(2)}) collective-permute-start(f32[360,128]{1,0:T(8,128)S(1)} %get-tuple-element.14), channel_id=1, source_target_pairs={{0,1},{2,3},{4,5},{6,7},{8,9},{10,11},{12,13},{14,15},{16,17},{18,... | collective-permute-start | bytes 552968 | tf_op jit(solution)/shard_map/ppermute | solution.py:473
  7.6 12.4 %all-to-all-start = ((f32[32,1,128]{2,1,0:T(1,128)}), f32[32,1,128]{2,1,0:T(1,128)S(1)}, u32[]{:S(2)}, u32[]{:S(2)}) async-start(f32[32,1,128]{2,1,0:T(1,128)} %bitcast.7), calls=%async_computation | async-start | bytes 32768 | tf_op jit(solution)/shard_map/all_to_all | solution.py:474

commit v4 on v3

--- a/solution.py
+++ b/solution.py
@@ -14,6 +14,7 @@
 AXES = ("row", "col")
 FACES = ((0, 1, 2, 3), (3, 6, 8, 9), (9, 7, 4, 0))
 PACK = 40
+SENT = 37
 WIDE = 32
 PAD = 8
 
@@ -28,10 +29,11 @@
         self.blocks = cells // LANES
         self.margin = cells // 4 // LANES
         self.halo = self.margin + 1
-        self.rows = -(-(self.blocks + 2 * self.halo) // 8) * 8
-        self.tall = self.rows + 2 * PAD
+        self.tall = self.blocks + 2 * PAD
+        self.side = self.halo + 3
+        self.strip = -(-2 * self.side // 8) * 8
+        self.strip_tall = self.strip + 2 * PAD
         self.slots = 3 * self.blocks // 2
-        self.keep = self.halo - self.margin
 
 
 def fetch_all(pairs, sems):
@@ -87,20 +89,20 @@
     for copy in copies[3:]:
         copy.wait()
     for ref, source, start in ((even_ref, state_even, even), (odd_ref, state_odd, odd)):
-        pack_state(source, ref, halo)
+        pack_state(source, ref, halo, SENT, 3)
         at = pl.ds(start, halo)
         dense = [depth_ref[at, :]]
         dense += [spread[pl.ds(8 * start + comp, halo, stride=8), :] for comp in range(4)]
         dense += [partner_ref[at, :].astype(jnp.float32), refine_ref[at, :].astype(jnp.float32)]
         for num, value in enumerate(dense):
-            ref[pl.ds(4 * num + 3, halo, stride=PACK), :] = value
+            ref[pl.ds(30 + num, halo, stride=SENT), :] = value
     sent.wait()
 
 
-def pack_state(source, target, blocks):
+def pack_state(source, target, blocks, height, width):
     for block in range(blocks):
         for node in range(10):
-            at = PACK * block + 4 * node
+            at = height * block + width * node
             target[at : at + 3, :] = source[node, :, LANES * block : LANES * (block + 1)]
 
 
@@ -131,12 +133,12 @@
     return prev, after, across
 
 
-def wall_masks(sizes, start, place, count, partner):
+def wall_masks(start, first_row, last_row, place, count, partner):
     shape = partner.shape
     lane = lax.broadcasted_iota(jnp.int32, shape, 1)
     row = lax.broadcasted_iota(jnp.int32, shape, 0) + start
-    first = (lane == 0) & (row == sizes.halo) & (place == 0)
-    last = (lane == LANES - 1) & (row == sizes.halo + sizes.blocks - 1) & (place == count - 1)
+    first = (lane == 0) & (row == first_row) & (place == 0)
+    last = (lane == LANES - 1) & (row == last_row) & (place == count - 1)
     return first, last, partner == 0
 
 
@@ -231,16 +233,72 @@
     ends_ref[1] = before + whole
 
 
-def first_kernel(
-    sizes, state_hbm, depth_hbm, metric_hbm, partner_hbm, refine_hbm, odd_ref, even_ref, diff_hbm, lift_hbm, prolong_hbm,
-    cur, rate_ref, twice_ref, weights, ends_ref,
+def rates_of_state(groups, ends, cur, aux, diff_ref, lift_ref, geo_ref, rate_ref):
+    place, count = lax.axis_index(AXES), lax.axis_size(AXES)
+
+    def step(group, carry):
+        base = PAD + 8 * group
+
+        def load_aux(item, shift):
+            return aux[item, pl.ds(base + shift, 8), :]
+
+        def load(item, shift):
+            return cur[item, pl.ds(base + shift, 8), :]
+
+        depth, rx, ry, sx, sy, partner = [load_aux(num, 0) for num in range(6)]
+        index, inside = pair_index(partner)
+        fetch = outer_values(load_aux, index, inside)
+        walls = wall_masks(8 * group, *ends, place, count, partner)
+        speed_sq = GRAVITY * depth
+        outer_sq = [jnp.where(walls[k], speed_sq, GRAVITY * fetch[k](0)) for k in range(3)]
+        faces = ((sx, sy), (rx + sx, ry + sy), (rx, ry))
+        squares = [vx * vx + vy * vy for vx, vy in faces]
+        waves = [
+            0.5 * jnp.sqrt(squares[k]) * jnp.sqrt(jnp.maximum(speed_sq, outer_sq[k])) for k in range(3)
+        ]
+        ghosts = [8.0 / squares[k] for k in range(3)]
+        geo = [speed_sq, rx, ry, sx, sy, *outer_sq, *waves, *ghosts]
+        rates = tendency(load, geo, walls, index, inside, diff_ref, lift_ref)
+        at = pl.ds(pl.multiple_of(8 * group, 8), 8)
+        for num, value in enumerate([*geo, partner]):
+            geo_ref[num, at, :] = value
+        for item in range(30):
+            rate_ref[item, pl.ds(pl.multiple_of(base, 8), 8), :] = rates[item]
+        return carry
+
+    lax.fori_loop(0, groups, step, 0)
+
+
+def rates_of_rates(groups, ends, rate_ref, diff_ref, lift_ref, geo_ref, twice_ref):
+    place, count = lax.axis_index(AXES), lax.axis_size(AXES)
+
+    def step(group, carry):
+        base = PAD + 8 * group
+        at = pl.ds(pl.multiple_of(8 * group, 8), 8)
+
+        def load(item, shift):
+            return rate_ref[item, pl.ds(base + shift, 8), :]
+
+        geo = [geo_ref[num, at, :] for num in range(14)]
+        partner = geo_ref[14, at, :]
+        index, inside = pair_index(partner)
+        walls = wall_masks(8 * group, *ends, place, count, partner)
+        rates = tendency(load, geo, walls, index, inside, diff_ref, lift_ref)
+        for item in range(30):
+            twice_ref[item, at, :] = rates[item]
+        return carry
+
+    lax.fori_loop(0, groups, step, 0)
+
+
+def own_kernel(
+    sizes, state_hbm, depth_hbm, metric_hbm, partner_hbm, refine_hbm, diff_hbm, lift_hbm, prolong_hbm,
+    cur, aux, rate_ref, twice_ref, weights,
     geo_ref, state_ref, depth_ref, metric_ref, partner_ref, refine_ref, diff_ref, lift_ref, prolong_ref,
-    spread, wide, aux, sems,
+    spread, wide, sems,
 ):
-    blocks, halo = sizes.blocks, sizes.halo
-    top, bottom = PAD + halo, PAD + halo + blocks
-    place = lax.axis_index(AXES)
-    count = lax.axis_size(AXES)
+    blocks = sizes.blocks
+    now = slice(PAD, PAD + blocks)
     copies = fetch_all(
         (
             (metric_hbm, metric_ref),
@@ -258,84 +316,58 @@
         copy.wait()
     metric = split_metric(metric_ref, spread, blocks)
     dense = [depth_ref[...], *metric, partner_ref[...].astype(jnp.float32), refine_ref[...].astype(jnp.float32)]
-    pack_state(state_ref, wide, blocks)
-    even = place % 2 == 0
-
-    def set_halo(target, num, row):
-        by_even = even_ref[pl.ds(row, halo, stride=PACK), :]
-        by_odd = odd_ref[pl.ds(row, halo, stride=PACK), :]
-        target[num, top - halo : top, :] = jnp.where(even, by_odd, by_even)
-        target[num, bottom : bottom + halo, :] = jnp.where(even, by_even, by_odd)
-
     for num in range(7):
-        set_halo(aux, num, 4 * num + 3)
-        aux[num, top:bottom, :] = dense[num]
+        aux[num, now, :] = dense[num]
+    pack_state(state_ref, wide, blocks, PACK, 4)
     for field in range(3):
         for node in range(10):
-            item = 10 * field + node
-            set_halo(cur, item, 4 * node + field)
-            cur[item, top:bottom, :] = wide[pl.ds(4 * node + field, blocks, stride=PACK), :]
-
+            cur[10 * field + node, now, :] = wide[pl.ds(4 * node + field, blocks, stride=PACK), :]
     weights[...] = child_matrix(prolong_ref)
-    begin = PAD + sizes.keep
-    sum_children(sizes, aux[6, begin : begin + sizes.slots, :], ends_ref)
-
-    def step(group, carry):
-        base = PAD + 8 * group
-
-        def load_aux(item, shift):
-            return aux[item, pl.ds(base + shift, 8), :]
-
-        def load(item, shift):
-            return cur[item, pl.ds(base + shift, 8), :]
-
-        depth, rx, ry, sx, sy, partner = [load_aux(num, 0) for num in range(6)]
-        index, inside = pair_index(partner)
-        fetch = outer_values(load_aux, index, inside)
-        walls = wall_masks(sizes, 8 * group, place, count, partner)
-        speed_sq = GRAVITY * depth
-        outer_sq = [jnp.where(walls[k], speed_sq, GRAVITY * fetch[k](0)) for k in range(3)]
-        faces = ((sx, sy), (rx + sx, ry + sy), (rx, ry))
-        squares = [vx * vx + vy * vy for vx, vy in faces]
-        waves = [
-            0.5 * jnp.sqrt(squares[k]) * jnp.sqrt(jnp.maximum(speed_sq, outer_sq[k])) for k in range(3)
-        ]
-        ghosts = [8.0 / squares[k] for k in range(3)]
-        geo = [speed_sq, rx, ry, sx, sy, *outer_sq, *waves, *ghosts]
-        rates = tendency(load, geo, walls, index, inside, diff_ref, lift_ref)
-        at = pl.ds(pl.multiple_of(8 * group, 8), 8)
-        for num, value in enumerate([*geo, partner]):
-            geo_ref[num, at, :] = value
-        for item in range(30):
-            rate_ref[item, pl.ds(base, 8), :] = rates[item]
-        return carry
-
-    lax.fori_loop(0, sizes.rows // 8, step, 0)
-
-    def again(group, carry):
-        row = 8 * group + sizes.keep
-        at = pl.ds(row, 8)
-
-        def load(item, shift):
-            return rate_ref[item, pl.ds(PAD + row + shift, 8), :]
-
-        geo = [geo_ref[num, at, :] for num in range(14)]
-        partner = geo_ref[14, at, :]
-        index, inside = pair_index(partner)
-        walls = wall_masks(sizes, row, place, count, partner)
-        rates = tendency(load, geo, walls, index, inside, diff_ref, lift_ref)
-        for item in range(30):
-            twice_ref[item, pl.ds(pl.multiple_of(8 * group, 8), 8), :] = rates[item]
-        return carry
-
-    lax.fori_loop(0, sizes.slots // 8, again, 0)
+    ends = (0, blocks - 1)
+    rates_of_state(blocks // 8, ends, cur, aux, diff_ref, lift_ref, geo_ref, rate_ref)
+    rates_of_rates(blocks // 8, ends, rate_ref, diff_ref, lift_ref, geo_ref, twice_ref)
+
+
+def strip_kernel(
+    sizes, cur_own, aux_own, rate_own, odd_ref, even_ref, diff_hbm, lift_hbm,
+    cur, rate_ref, twice_ref, ends_ref, aux, geo_ref, diff_ref, lift_ref, refine_ref, sems,
+):
+    blocks, halo, side, margin = sizes.blocks, sizes.halo, sizes.side, sizes.margin
+    copies = fetch_all(((diff_hbm, diff_ref), (lift_hbm, lift_ref)), sems)
+    even = lax.axis_index(AXES) % 2 == 0
+
+    def fill(target, source, num, row):
+        by_even = even_ref[pl.ds(row, halo, stride=SENT), :]
+        by_odd = odd_ref[pl.ds(row, halo, stride=SENT), :]
+        target[num, PAD : PAD + halo, :] = jnp.where(even, by_odd, by_even)
+        target[num, PAD + halo : PAD + side, :] = source[num, PAD : PAD + 3, :]
+        target[num, PAD + side : PAD + side + 3, :] = source[num, PAD + blocks - 3 : PAD + blocks, :]
+        target[num, PAD + side + 3 : PAD + 2 * side, :] = jnp.where(even, by_even, by_odd)
+
+    for num in range(7):
+        fill(aux, aux_own, num, 30 + num)
+    for field in range(3):
+        for node in range(10):
+            fill(cur, cur_own, 10 * field + node, 3 * node + field)
+    refine_ref[:margin, :] = aux[6, PAD + 1 : PAD + 1 + margin, :]
+    refine_ref[margin : margin + blocks, :] = aux_own[6, PAD : PAD + blocks, :]
+    refine_ref[margin + blocks :, :] = aux[6, PAD + side + 3 : PAD + side + 3 + margin, :]
+    sum_children(sizes, refine_ref[...], ends_ref)
+    for copy in copies:
+        copy.wait()
+    ends = (halo, side + 2)
+    rates_of_state(sizes.strip // 8, ends, cur, aux, diff_ref, lift_ref, geo_ref, rate_ref)
+    for item in range(30):
+        for row, block in ((side - 1, 2), (side, blocks - 3)):
+            rate_ref[item, PAD + row : PAD + row + 1, :] = rate_own[item, PAD + block : PAD + block + 1, :]
+    rates_of_rates(sizes.strip // 8, ends, rate_ref, diff_ref, lift_ref, geo_ref, twice_ref)
 
 
 def refine_kernel(
-    sizes, cur, rate_ref, twice_ref, weights, base_ref, stats_ref, out_hbm,
+    sizes, cur_own, rate_own, twice_own, cur, rate_ref, twice_ref, weights, base_ref, stats_ref, out_hbm,
     out_ref, ends_ref, place_v, place_s, wide, gathered, index_ref, out_sems, sem,
 ):
-    slots, keep = sizes.slots, sizes.keep
+    slots, blocks, side, outer = sizes.slots, sizes.blocks, sizes.side, sizes.margin + 2
     place = lax.axis_index(AXES)
     stats = stats_ref[...]
     half = LANES // 2
@@ -357,9 +389,15 @@
     copy = pltpu.make_async_copy(place_v, place_s, sem)
     copy.start()
     for item in range(30):
-        now = slice(PAD + keep, PAD + keep + slots)
-        value = cur[item, now, :] + step * rate_ref[item, now, :] + half_square * twice_ref[item]
-        wide[pl.ds(item, slots, stride=WIDE), :] = value
+        for to, rows, start_row, refs in (
+            (0, outer, 1, (cur, rate_ref, twice_ref)),
+            (outer, blocks - 4, 2, (cur_own, rate_own, twice_own)),
+            (slots - outer, outer, side + 1, (cur, rate_ref, twice_ref)),
+        ):
+            now = slice(PAD + start_row, PAD + start_row + rows)
+            once = refs[0][item, now, :] + step * refs[1][item, now, :]
+            value = once + half_square * refs[2][item, start_row : start_row + rows, :]
+            wide[pl.ds(WIDE * to + item, rows, stride=WIDE), :] = value
     for item in (30, 31):
         wide[pl.ds(item, slots + 1, stride=WIDE), :] = jnp.zeros((slots + 1, LANES), jnp.float32)
     copy.wait()
@@ -437,7 +475,7 @@
 def shards(state, depth, metric, partner, refine, diff_ops, lift, prolong):
     sizes = Sizes(state.shape[2])
     count = lax.axis_size(AXES)
-    blocks, rows, slots, halo = sizes.blocks, sizes.rows, sizes.slots, sizes.halo
+    blocks, slots, halo = sizes.blocks, sizes.slots, sizes.halo
     depth, partner, refine = [x.reshape(blocks, LANES) for x in (depth, partner, refine)]
     state, diff_ops, prolong = [jnp.transpose(x, (1, 0, 2)) for x in (state, diff_ops, prolong)]
     state, depth, metric, partner, refine, diff_ops, lift, prolong = [
@@ -445,13 +483,14 @@
         for x in (state, depth, metric, partner, refine, diff_ops, lift, prolong)
     ]
     f32, i32 = jnp.float32, jnp.int32
-    packed = jax.ShapeDtypeStruct((PACK * halo, LANES), f32)
+    packed = jax.ShapeDtypeStruct((SENT * halo, LANES), f32)
     dense = [
         pltpu.VMEM((blocks, LANES), f32),
         pltpu.VMEM(metric.shape, f32),
         pltpu.VMEM((blocks, LANES), i32),
         pltpu.VMEM((blocks, LANES), i32),
     ]
+    operators = [pltpu.SMEM(diff_ops.shape, f32), pltpu.SMEM(lift.shape, f32)]
     stats, even, odd = pl.pallas_call(
         functools.partial(pack_kernel, sizes),
         name="pack",
@@ -473,37 +512,57 @@
     even = lax.ppermute(even, AXES, swaps(0, count))
     stats = lax.all_to_all(stats, AXES, 0, 0, tiled=True)
     even, odd, stats = [pltpu.with_memory_space_constraint(x, pltpu.VMEM) for x in (even, odd, stats)]
-    cur, rates, twice, weights, ends = pl.pallas_call(
-        functools.partial(first_kernel, sizes),
-        name="rates_twice",
+    cur, aux, rates, twice, weights = pl.pallas_call(
+        functools.partial(own_kernel, sizes),
+        name="own_rates",
+        cost_estimate=pl.CostEstimate(flops=1 << 24, transcendentals=1 << 16, bytes_accessed=1 << 24),
         out_shape=(
             jax.ShapeDtypeStruct((30, sizes.tall, LANES), f32),
+            jax.ShapeDtypeStruct((7, sizes.tall, LANES), f32),
             jax.ShapeDtypeStruct((30, sizes.tall, LANES), f32),
-            jax.ShapeDtypeStruct((30, slots, LANES), f32),
+            jax.ShapeDtypeStruct((30, blocks, LANES), f32),
             jax.ShapeDtypeStruct((3 * PACK, 4 * WIDE), jnp.bfloat16),
-            jax.ShapeDtypeStruct((2, slots, LANES), f32),
         ),
-        in_specs=[HBM] * 5 + [VMEM] * 2 + [HBM] * 3,
+        in_specs=[HBM] * 8,
         out_specs=(VMEM,) * 5,
         scratch_shapes=[
-            pltpu.VMEM((15, rows, LANES), f32),
+            pltpu.VMEM((15, blocks, LANES), f32),
             pltpu.VMEM(state.shape, f32),
             *dense,
-            pltpu.SMEM(diff_ops.shape, f32),
-            pltpu.SMEM(lift.shape, f32),
+            *operators,
             pltpu.VMEM(prolong.shape, f32),
             pltpu.VMEM((8 * blocks, LANES), f32),
             pltpu.VMEM((PACK * blocks, LANES), f32),
-            pltpu.VMEM((7, sizes.tall, LANES), f32),
             pltpu.SemaphoreType.DMA((8,)),
         ],
         compiler_params=PARAMS,
-    )(state, depth, metric, partner, refine, odd, even, diff_ops, lift, prolong)
+    )(state, depth, metric, partner, refine, diff_ops, lift, prolong)
+    strip_cur, strip_rates, strip_twice, ends = pl.pallas_call(
+        functools.partial(strip_kernel, sizes),
+        name="strip_rates",
+        cost_estimate=pl.CostEstimate(flops=1024, transcendentals=0, bytes_accessed=1024),
+        out_shape=(
+            jax.ShapeDtypeStruct((30, sizes.strip_tall, LANES), f32),
+            jax.ShapeDtypeStruct((30, sizes.strip_tall, LANES), f32),
+            jax.ShapeDtypeStruct((30, sizes.strip, LANES), f32),
+            jax.ShapeDtypeStruct((2, slots, LANES), f32),
+        ),
+        in_specs=[VMEM] * 5 + [HBM] * 2,
+        out_specs=(VMEM,) * 4,
+        scratch_shapes=[
+            pltpu.VMEM((7, sizes.strip_tall, LANES), f32),
+            pltpu.VMEM((15, sizes.strip, LANES), f32),
+            *operators,
+            pltpu.VMEM((slots, LANES), f32),
+            pltpu.SemaphoreType.DMA((2,)),
+        ],
+        compiler_params=PARAMS,
+    )(cur, aux, rates, odd, even, diff_ops, lift)
     refined = pl.pallas_call(
         functools.partial(refine_kernel, sizes),
         name="sum_and_refine",
         out_shape=jax.ShapeDtypeStruct((10, 3, LANES * slots), f32),
-        in_specs=[VMEM] * 6,
+        in_specs=[VMEM] * 9,
         out_specs=HBM,
         scratch_shapes=[
             pltpu.VMEM((10, 3, LANES * slots), f32),
@@ -517,7 +576,7 @@
             pltpu.SemaphoreType.DMA,
         ],
         compiler_params=PARAMS,
-    )(cur, rates, twice, weights, ends, stats)
+    )(cur, rates, twice, strip_cur, strip_rates, strip_twice, weights, ends, stats)
     return jnp.transpose(refined, (1, 0, 2))
 
 

time: 23.9 us -> 27.8 us (1.16)
  the two profiles are of different devices: /device:TPU:4 before, /device:TPU:0 now
where the time goes in v4:
time: 27.8 us; the launch traced here: 27.4 us
  Pallas kernels  12.9 us (46%)
  starting transfers between devices  9.95 us (36%)
  local copies, waits for them, and re-layouts  4.47 us (16%)
    all_to_all x1, starting transfers between devices, shards(): stats = lax.all_to_all(stats, AXES, 0, 0, tiled=True)  4.84 us
    pallas_call x1, Pallas kernels, shards(): pl.pallas_call(functools.partial(own_kernel, sizes), name='own_rates', co...  4.67 us
    unnamed x12, local copies, waits for them, and re-layouts  4.47 us
    ppermute x1, starting transfers between devices, shards(): even = lax.ppermute(even, AXES, swaps(0, count))  4.44 us
    pallas_call x1, Pallas kernels, shards(): pl.pallas_call(functools.partial(refine_kernel, sizes), name='sum_and_ref...  3.6 us
    pallas_call x1, Pallas kernels, shards(): pl.pallas_call(functools.partial(strip_kernel, sizes), name='strip_rates'...  2.96 us
    pallas_call x1, Pallas kernels, shards(): pl.pallas_call(functools.partial(pack_kernel, sizes), name='pack', out_sh...  1.65 us
    ppermute x1, starting transfers between devices, shards(): odd = lax.ppermute(odd, AXES, swaps(1, count))  0.67 us
  transfers between devices with their start and end apart: 3, of which 0 were waited for; matrix products, arithmetic and copies ran while one was open for 0% of the time, Pallas kernels for 28%

profile of v4, /device:TPU:0, one launch (start us, length us, event | category | flops | bytes accessed | tf_op | source)
XLA Modules:
  0.0 27.4 jit_solution(10506246776398268673)
XLA Ops:
  0.0 1.6 %pack.1 = (f32[32,128]{1,0:T(8,128)}, f32[333,128]{1,0:T(8,128)S(1)}, f32[333,128]{1,0:T(8,128)S(1)}) custom-call(f32[10,3,4096]{2,1,0:T(4,128)} %bitcast.12, f32[32,128]{1,0:T(8,128)} %bitcast.14, f32[4,4096]{1,0:T(4,128)} %metric_hbm.3, s32[32,128]{1,0:T(8,128)} %bitcast.16, s32[32,128]{1,0:T(8,128)} %bitcast.18), custom_call_target="tpu_custom_call" | custom-call | tf_op jit(solution)/shard_map/pack/pallas_call | solution.py:494
  1.7 0.7 %collective-permute-start = (f32[333,128]{1,0:T(8,128)S(1)}, f32[333,128]{1,0:T(8,128)S(1)}, u32[]{:S(2)}, u32[]{:S(2)}) collective-permute-start(f32[333,128]{1,0:T(8,128)S(1)} %get-tuple-element.21), channel_id=1, source_target_pairs={{1,2},{3,4},{5,6},{7,8},{9,10},{11,12},{13,14},{15,16},{17,18},{19... | collective-permute-start | bytes 511496 | tf_op jit(solution)/shard_map/ppermute | solution.py:511
  2.3 4.4 %collective-permute-start.1 = (f32[333,128]{1,0:T(8,128)S(1)}, f32[333,128]{1,0:T(8,128)S(1)}, u32[]{:S(2)}, u32[]{:S(2)}) collective-permute-start(f32[333,128]{1,0:T(8,128)S(1)} %get-tuple-element.22), channel_id=1, source_target_pairs={{0,1},{2,3},{4,5},{6,7},{8,9},{10,11},{12,13},{14,15},{16,17},{18,... | collective-permute-start | bytes 511496 | tf_op jit(solution)/shard_map/ppermute | solution.py:512
  6.8 4.8 %all-to-all-start = ((f32[32,1,128]{2,1,0:T(1,128)}), f32[32,1,128]{2,1,0:T(1,128)S(1)}, u32[]{:S(2)}, u32[]{:S(2)}) async-start(f32[32,1,128]{2,1,0:T(1,128)} %bitcast.7), calls=%async_computation | async-start | bytes 32768 | tf_op jit(solution)/shard_map/all_to_all | solution.py:513
  11.6 4.7 %own_rates.1 = (f32[30,48,128]{2,1,0:T(8,128)S(1)}, f32[7,48,128]{2,1,0:T(8,128)S(1)}, f32[30,48,128]{2,1,0:T(8,128)S(1)}, f32[30,32,128]{2,1,0:T(8,128)S(1)}, bf16[120,128]{1,0:T(8,128)(2,1)S(1)}) custom-call(f32[10,3,4096]{2,1,0:T(4,128)} %bitcast.13, f32[32,128]{1,0:T(8,128)} %bitcast.15, f32[4,4096]{1,0:T(4,128)} %metric_hbm.3, s32[32,128]{1,0:T(8,128)} %bitcast.17, ...), custom_call_target="tpu_custom_call" | custom-call | flops 16777216 | bytes 16777216 | tf_op jit(solution)/shard_map/own_rates/pallas_call | solution.py:515
  16.3 0.0 copy-start.4
  16.3 0.6 %copy-done.4 = bf16[120,128]{1,0:T(8,128)(2,1)} copy-done((bf16[120,128]{1,0:T(8,128)(2,1)}, bf16[120,128]{1,0:T(8,128)(2,1)S(1)}, u32[]{:S(2)}) %copy-start.4) | copy-done | bytes 30744
  16.9 0.0 collective-permute-done.odd_ref
  16.9 0.0 collective-permute-done.1.even_ref
  16.9 3.0 %strip_rates.1 = (f32[30,40,128]{2,1,0:T(8,128)S(1)}, f32[30,40,128]{2,1,0:T(8,128)S(1)}, f32[30,24,128]{2,1,0:T(8,128)S(1)}, f32[2,48,128]{2,1,0:T(8,128)S(1)}) custom-call(f32[30,48,128]{2,1,0:T(8,128)S(1)} %get-tuple-element.17.cur_own, f32[7,48,128]{2,1,0:T(8,128)S(1)} %get-tuple-element.20.aux_own, f32[30,48,128]{2,1,0:T(8,128)S(1)} %get-tuple-element.18.rate_own, ...), custom_call_target="tpu_custom_call" | custom-call | flops 1024 | bytes 1024 | tf_op jit(solution)/shard_map/strip_rates/pallas_call | solution.py:540
  19.9 0.0 copy-start
  19.9 0.7 %copy-done = f32[30,24,128]{2,1,0:T(8,128)} copy-done((f32[30,24,128]{2,1,0:T(8,128)}, f32[30,24,128]{2,1,0:T(8,128)S(1)}, u32[]{:S(2)}) %copy-start) | copy-done | bytes 368664
  20.6 0.0 copy-start.2
  20.6 0.6 %copy-done.2 = f32[2,48,128]{2,1,0:T(8,128)} copy-done((f32[2,48,128]{2,1,0:T(8,128)}, f32[2,48,128]{2,1,0:T(8,128)S(1)}, u32[]{:S(2)}) %copy-start.2) | copy-done | bytes 49176
  21.2 0.0 all-to-all-done
  21.2 0.0 copy-start.1
  21.2 1.0 %copy-done.1 = f32[30,24,128]{2,1,0:T(8,128)S(1)} copy-done((f32[30,24,128]{2,1,0:T(8,128)S(1)}, f32[30,24,128]{2,1,0:T(8,128)}, u32[]{:S(2)}) %copy-start.1) | copy-done | bytes 368664
  22.2 0.0 copy-start.3
  22.2 0.8 %copy-done.3 = f32[2,48,128]{2,1,0:T(8,128)S(1)} copy-done((f32[2,48,128]{2,1,0:T(8,128)S(1)}, f32[2,48,128]{2,1,0:T(8,128)}, u32[]{:S(2)}) %copy-start.3) | copy-done | bytes 49176
  23.0 0.0 copy-start.5
  23.0 0.8 %copy-done.5 = bf16[120,128]{1,0:T(8,128)(2,1)S(1)} copy-done((bf16[120,128]{1,0:T(8,128)(2,1)S(1)}, bf16[120,128]{1,0:T(8,128)(2,1)}, u32[]{:S(2)}) %copy-start.5) | copy-done | bytes 30744
  23.8 3.6 %sum_and_refine.1 = f32[10,3,6144]{2,1,0:T(4,128)} custom-call(f32[30,48,128]{2,1,0:T(8,128)S(1)} %get-tuple-element.17.cur_own, f32[30,48,128]{2,1,0:T(8,128)S(1)} %get-tuple-element.18.rate_own, f32[30,32,128]{2,1,0:T(8,128)S(1)} %get-tuple-element.19.twice_own, f32[30,40,128]{2,1,0:T(8,128)S(1)} %get-tuple-element.23.cur, ...), custom_call_target="tpu_custom_call" | custom-call | tf_op jit(solution)/shard_map/sum_and_refine/pallas_call | solution.py:561
Async XLA Ops:
  1.7 15.2 %collective-permute-start = (f32[333,128]{1,0:T(8,128)S(1)}, f32[333,128]{1,0:T(8,128)S(1)}, u32[]{:S(2)}, u32[]{:S(2)}) collective-permute-start(f32[333,128]{1,0:T(8,128)S(1)} %get-tuple-element.21), channel_id=1, source_target_pairs={{1,2},{3,4},{5,6},{7,8},{9,10},{11,12},{13,14},{15,16},{17,18},{19... | collective-permute-start | bytes 511496 | tf_op jit(solution)/shard_map/ppermute | solution.py:511
  2.3 14.6 %collective-permute-start.1 = (f32[333,128]{1,0:T(8,128)S(1)}, f32[333,128]{1,0:T(8,128)S(1)}, u32[]{:S(2)}, u32[]{:S(2)}) collective-permute-start(f32[333,128]{1,0:T(8,128)S(1)} %get-tuple-element.22), channel_id=1, source_target_pairs={{0,1},{2,3},{4,5},{6,7},{8,9},{10,11},{12,13},{14,15},{16,17},{18,... | collective-permute-start | bytes 511496 | tf_op jit(solution)/shard_map/ppermute | solution.py:512
  6.8 14.5 %all-to-all-start = ((f32[32,1,128]{2,1,0:T(1,128)}), f32[32,1,128]{2,1,0:T(1,128)S(1)}, u32[]{:S(2)}, u32[]{:S(2)}) async-start(f32[32,1,128]{2,1,0:T(1,128)} %bitcast.7), calls=%async_computation | async-start | bytes 32768 | tf_op jit(solution)/shard_map/all_to_all | solution.py:513
  16.3 0.6 %copy-start.4 = (bf16[120,128]{1,0:T(8,128)(2,1)}, bf16[120,128]{1,0:T(8,128)(2,1)S(1)}, u32[]{:S(2)}) copy-start(bf16[120,128]{1,0:T(8,128)(2,1)S(1)} %get-tuple-element.26.weights) | copy-start | bytes 92164
  19.9 0.7 %copy-start = (f32[30,24,128]{2,1,0:T(8,128)}, f32[30,24,128]{2,1,0:T(8,128)S(1)}, u32[]{:S(2)}) copy-start(f32[30,24,128]{2,1,0:T(8,128)S(1)} %get-tuple-element.25.twice_ref) | copy-start | bytes 1105924
  20.6 0.6 %copy-start.2 = (f32[2,48,128]{2,1,0:T(8,128)}, f32[2,48,128]{2,1,0:T(8,128)S(1)}, u32[]{:S(2)}) copy-start(f32[2,48,128]{2,1,0:T(8,128)S(1)} %get-tuple-element.27.base_ref) | copy-start | bytes 147460
  21.2 1.0 %copy-start.1 = (f32[30,24,128]{2,1,0:T(8,128)S(1)}, f32[30,24,128]{2,1,0:T(8,128)}, u32[]{:S(2)}) copy-start(f32[30,24,128]{2,1,0:T(8,128)} %copy-done) | copy-start | bytes 1105924
  22.2 0.8 %copy-start.3 = (f32[2,48,128]{2,1,0:T(8,128)S(1)}, f32[2,48,128]{2,1,0:T(8,128)}, u32[]{:S(2)}) copy-start(f32[2,48,128]{2,1,0:T(8,128)} %copy-done.2) | copy-start | bytes 147460
  23.0 0.8 %copy-start.5 = (bf16[120,128]{1,0:T(8,128)(2,1)S(1)}, bf16[120,128]{1,0:T(8,128)(2,1)}, u32[]{:S(2)}) copy-start(bf16[120,128]{1,0:T(8,128)(2,1)} %copy-done.4) | copy-start | bytes 92164

commit v5 on v3

--- a/solution.py
+++ b/solution.py
@@ -14,6 +14,7 @@
 AXES = ("row", "col")
 FACES = ((0, 1, 2, 3), (3, 6, 8, 9), (9, 7, 4, 0))
 PACK = 40
+SENT = 37
 WIDE = 32
 PAD = 8
 
@@ -87,20 +88,20 @@
     for copy in copies[3:]:
         copy.wait()
     for ref, source, start in ((even_ref, state_even, even), (odd_ref, state_odd, odd)):
-        pack_state(source, ref, halo)
+        pack_state(source, ref, halo, SENT, 3)
         at = pl.ds(start, halo)
         dense = [depth_ref[at, :]]
         dense += [spread[pl.ds(8 * start + comp, halo, stride=8), :] for comp in range(4)]
         dense += [partner_ref[at, :].astype(jnp.float32), refine_ref[at, :].astype(jnp.float32)]
         for num, value in enumerate(dense):
-            ref[pl.ds(4 * num + 3, halo, stride=PACK), :] = value
+            ref[pl.ds(30 + num, halo, stride=SENT), :] = value
     sent.wait()
 
 
-def pack_state(source, target, blocks):
+def pack_state(source, target, blocks, height, width):
     for block in range(blocks):
         for node in range(10):
-            at = PACK * block + 4 * node
+            at = height * block + width * node
             target[at : at + 3, :] = source[node, :, LANES * block : LANES * (block + 1)]
 
 
@@ -140,13 +141,46 @@
     return first, last, partner == 0
 
 
-def tendency(load, geo, walls, index, inside, diff_ref, lift_ref):
+def volume_matrix(diff_ref):
+    d_r, d_s = diff_ref[:, 0, :], diff_ref[:, 1, :]
+    zero = jnp.zeros((10, 10), jnp.float32)
+    whole = jnp.concatenate(
+        [
+            jnp.concatenate([-d_r, -d_s, zero, jnp.zeros((10, 2), jnp.float32)], axis=1),
+            jnp.concatenate([zero, zero, d_r, jnp.zeros((10, 2), jnp.float32)], axis=1),
+            jnp.concatenate([zero, zero, d_s, jnp.zeros((10, 2), jnp.float32)], axis=1),
+            jnp.zeros((2, WIDE), jnp.float32),
+        ],
+        axis=0,
+    )
+    rounded = whole.astype(jnp.bfloat16)
+    rest = (whole - rounded.astype(jnp.float32)).astype(jnp.bfloat16)
+    return jnp.concatenate([rounded, rounded, rest], axis=1)
+
+
+def by_matrix(matrix, rows, laid, results):
+    for num, value in enumerate(rows):
+        laid[pl.ds(num, 8, stride=WIDE), :] = value
+    blocks = [laid[WIDE * sub : WIDE * (sub + 1), :] for sub in range(8)]
+    values = jnp.concatenate(blocks, axis=1)
+    high = values.astype(jnp.bfloat16)
+    low = (values - high.astype(jnp.float32)).astype(jnp.bfloat16)
+    stack = jnp.concatenate([high, low, high], axis=0)
+    products = jnp.dot(matrix, stack, preferred_element_type=jnp.float32)
+    for sub in range(8):
+        results[WIDE * sub : WIDE * (sub + 1), :] = products[:, LANES * sub : LANES * (sub + 1)]
+    return [results[pl.ds(num, 8, stride=WIDE), :] for num in range(len(rows))]
+
+
+def tendency(load, geo, walls, index, inside, volume, lift_ref):
     speed_sq, rx, ry, sx, sy = geo[:5]
     outer_sq, waves, ghosts = geo[5:8], geo[8:11], geo[11:14]
     own = [[load(10 * field + node, 0) for node in range(10)] for field in range(3)]
     eta, mom_x, mom_y = own
-    flow_r = [-(rx * mom_x[b] + ry * mom_y[b]) for b in range(10)]
-    flow_s = [-(sx * mom_x[b] + sy * mom_y[b]) for b in range(10)]
+    flow_r = [rx * mom_x[b] + ry * mom_y[b] for b in range(10)]
+    flow_s = [sx * mom_x[b] + sy * mom_y[b] for b in range(10)]
+    products = by_matrix(volume[0][...], flow_r + flow_s + eta, *volume[1:])
+    inflow, along_r, along_s = products[:10], products[10:20], products[20:]
     half_r = (0.5 * rx, 0.5 * ry)
     half_s = (0.5 * sx, 0.5 * sy)
     vectors = (
@@ -176,14 +210,11 @@
     push = (-speed_sq * sx, -speed_sq * sy)
     out = [[None] * 10 for _ in range(3)]
     for a in range(10):
-        total = along_r = along_s = None
-        for b in range(10):
-            d_r, d_s = diff_ref[a, 0, b], diff_ref[a, 1, b]
-            term = d_r * flow_r[b] + d_s * flow_s[b]
-            total = term if b == 0 else total + term
-            along_r = d_r * eta[b] if b == 0 else along_r + d_r * eta[b]
-            along_s = d_s * eta[b] if b == 0 else along_s + d_s * eta[b]
-        sums = [total, pull[0] * along_r + push[0] * along_s, pull[1] * along_r + push[1] * along_s]
+        sums = [
+            inflow[a],
+            pull[0] * along_r[a] + push[0] * along_s[a],
+            pull[1] * along_r[a] + push[1] * along_s[a],
+        ]
         for q in range(12):
             weight = lift_ref[a, q]
             for field in range(3):
@@ -235,7 +266,7 @@
     sizes, state_hbm, depth_hbm, metric_hbm, partner_hbm, refine_hbm, odd_ref, even_ref, diff_hbm, lift_hbm, prolong_hbm,
     cur, rate_ref, twice_ref, weights, ends_ref,
     geo_ref, state_ref, depth_ref, metric_ref, partner_ref, refine_ref, diff_ref, lift_ref, prolong_ref,
-    spread, wide, aux, sems,
+    spread, wide, aux, matrix, laid, results, sems,
 ):
     blocks, halo = sizes.blocks, sizes.halo
     top, bottom = PAD + halo, PAD + halo + blocks
@@ -258,25 +289,29 @@
         copy.wait()
     metric = split_metric(metric_ref, spread, blocks)
     dense = [depth_ref[...], *metric, partner_ref[...].astype(jnp.float32), refine_ref[...].astype(jnp.float32)]
-    pack_state(state_ref, wide, blocks)
+    pack_state(state_ref, wide, blocks, PACK, 4)
     even = place % 2 == 0
 
     def set_halo(target, num, row):
-        by_even = even_ref[pl.ds(row, halo, stride=PACK), :]
-        by_odd = odd_ref[pl.ds(row, halo, stride=PACK), :]
+        by_even = even_ref[pl.ds(row, halo, stride=SENT), :]
+        by_odd = odd_ref[pl.ds(row, halo, stride=SENT), :]
         target[num, top - halo : top, :] = jnp.where(even, by_odd, by_even)
         target[num, bottom : bottom + halo, :] = jnp.where(even, by_even, by_odd)
 
     for num in range(7):
-        set_halo(aux, num, 4 * num + 3)
+        set_halo(aux, num, 30 + num)
         aux[num, top:bottom, :] = dense[num]
     for field in range(3):
         for node in range(10):
             item = 10 * field + node
-            set_halo(cur, item, 4 * node + field)
+            set_halo(cur, item, 3 * node + field)
             cur[item, top:bottom, :] = wide[pl.ds(4 * node + field, blocks, stride=PACK), :]
 
     weights[...] = child_matrix(prolong_ref)
+    matrix[...] = volume_matrix(diff_ref)
+    for row in (30, 31):
+        laid[pl.ds(row, 8, stride=WIDE), :] = jnp.zeros((8, LANES), jnp.float32)
+    volume = (matrix, laid, results)
     begin = PAD + sizes.keep
     sum_children(sizes, aux[6, begin : begin + sizes.slots, :], ends_ref)
 
@@ -302,7 +337,7 @@
         ]
         ghosts = [8.0 / squares[k] for k in range(3)]
         geo = [speed_sq, rx, ry, sx, sy, *outer_sq, *waves, *ghosts]
-        rates = tendency(load, geo, walls, index, inside, diff_ref, lift_ref)
+        rates = tendency(load, geo, walls, index, inside, volume, lift_ref)
         at = pl.ds(pl.multiple_of(8 * group, 8), 8)
         for num, value in enumerate([*geo, partner]):
             geo_ref[num, at, :] = value
@@ -323,7 +358,7 @@
         partner = geo_ref[14, at, :]
         index, inside = pair_index(partner)
         walls = wall_masks(sizes, row, place, count, partner)
-        rates = tendency(load, geo, walls, index, inside, diff_ref, lift_ref)
+        rates = tendency(load, geo, walls, index, inside, volume, lift_ref)
         for item in range(30):
             twice_ref[item, pl.ds(pl.multiple_of(8 * group, 8), 8), :] = rates[item]
         return carry
@@ -445,7 +480,7 @@
         for x in (state, depth, metric, partner, refine, diff_ops, lift, prolong)
     ]
     f32, i32 = jnp.float32, jnp.int32
-    packed = jax.ShapeDtypeStruct((PACK * halo, LANES), f32)
+    packed = jax.ShapeDtypeStruct((SENT * halo, LANES), f32)
     dense = [
         pltpu.VMEM((blocks, LANES), f32),
         pltpu.VMEM(metric.shape, f32),
@@ -489,12 +524,15 @@
             pltpu.VMEM((15, rows, LANES), f32),
             pltpu.VMEM(state.shape, f32),
             *dense,
-            pltpu.SMEM(diff_ops.shape, f32),
+            pltpu.VMEM(diff_ops.shape, f32),
             pltpu.SMEM(lift.shape, f32),
             pltpu.VMEM(prolong.shape, f32),
             pltpu.VMEM((8 * blocks, LANES), f32),
             pltpu.VMEM((PACK * blocks, LANES), f32),
             pltpu.VMEM((7, sizes.tall, LANES), f32),
+            pltpu.VMEM((WIDE, 3 * WIDE), jnp.bfloat16),
+            pltpu.VMEM((8 * WIDE, LANES), f32),
+            pltpu.VMEM((8 * WIDE, LANES), f32),
             pltpu.SemaphoreType.DMA((8,)),
         ],
         compiler_params=PARAMS,

time: 23.9 us -> 24.7 us (1.033)
  Pallas kernels: 11.7 us -> 12.8 us
  waiting for transfers between devices: 3.11 us -> 2.86 us
    pallas_call x1, Pallas kernels: 6.45 us -> 7.57 us  [shards(): pl.pallas_call(functools.partial(first_kernel, sizes), name='rates_twice'...]
    ppermute x1, waiting for transfers between devices: 3.11 us -> 2.86 us  [shards(): odd = lax.ppermute(odd, AXES, swaps(1, count))]
  transfers between devices with their start and end apart: 3 -> 3, of which waited for: 1 -> 1; matrix products, arithmetic and copies ran while one was open for 0% -> 0% of each run, Pallas kernels for 27% -> 31%
where the time goes in v5:
time: 24.7 us; the launch traced here: 24.5 us
  Pallas kernels  12.8 us (52%)
  starting transfers between devices  8.74 us (35%)
  waiting for transfers between devices  2.86 us (12%)
    pallas_call x1, Pallas kernels, shards(): pl.pallas_call(functools.partial(first_kernel, sizes), name='rates_twice'...  7.57 us
    ppermute x1, starting transfers between devices, shards(): odd = lax.ppermute(odd, AXES, swaps(1, count))  5.82 us
    pallas_call x1, Pallas kernels, shards(): pl.pallas_call(functools.partial(refine_kernel, sizes), name='sum_and_ref...  3.58 us
    ppermute x1, waiting for transfers between devices, shards(): odd = lax.ppermute(odd, AXES, swaps(1, count))  2.86 us
    all_to_all x1, starting transfers between devices, shards(): stats = lax.all_to_all(stats, AXES, 0, 0, tiled=True)  2.85 us
    pallas_call x1, Pallas kernels, shards(): pl.pallas_call(functools.partial(pack_kernel, sizes), name='pack', out_sh...  1.65 us
  transfers between devices with their start and end apart: 3, of which 1 were waited for; matrix products, arithmetic and copies ran while one was open for 0% of the time, Pallas kernels for 31%

profile of v5, /device:TPU:4, one launch (start us, length us, event | category | flops | bytes accessed | tf_op | source)
XLA Modules:
  0.0 24.5 jit_solution(10075402623200176659)
XLA Ops:
  0.0 1.7 %pack.1 = (f32[32,128]{1,0:T(8,128)}, f32[333,128]{1,0:T(8,128)S(1)}, f32[333,128]{1,0:T(8,128)S(1)}) custom-call(f32[10,3,4096]{2,1,0:T(4,128)} %bitcast.12, f32[32,128]{1,0:T(8,128)} %bitcast.14, f32[4,4096]{1,0:T(4,128)} %metric_hbm.3, s32[32,128]{1,0:T(8,128)} %bitcast.16, s32[32,128]{1,0:T(8,128)} %bitcast.18), custom_call_target="tpu_custom_call" | custom-call | tf_op jit(solution)/shard_map/pack/pallas_call | solution.py:490
  1.7 5.8 %collective-permute-start = (f32[333,128]{1,0:T(8,128)S(1)}, f32[333,128]{1,0:T(8,128)S(1)}, u32[]{:S(2)}, u32[]{:S(2)}) collective-permute-start(f32[333,128]{1,0:T(8,128)S(1)} %get-tuple-element.13), channel_id=1, source_target_pairs={{1,2},{3,4},{5,6},{7,8},{9,10},{11,12},{13,14},{15,16},{17,18},{19... | collective-permute-start | bytes 511496 | tf_op jit(solution)/shard_map/ppermute | solution.py:507
  7.5 0.1 collective-permute-start.1
  7.6 2.9 %all-to-all-start = ((f32[32,1,128]{2,1,0:T(1,128)}), f32[32,1,128]{2,1,0:T(1,128)S(1)}, u32[]{:S(2)}, u32[]{:S(2)}) async-start(f32[32,1,128]{2,1,0:T(1,128)} %bitcast.7), calls=%async_computation | async-start | bytes 32768 | tf_op jit(solution)/shard_map/all_to_all | solution.py:509
  10.4 2.9 %collective-permute-done.odd_ref = f32[333,128]{1,0:T(8,128)S(1)} collective-permute-done((f32[333,128]{1,0:T(8,128)S(1)}, f32[333,128]{1,0:T(8,128)S(1)}, u32[]{:S(2)}, u32[]{:S(2)}) %collective-permute-start) | collective-permute-done | bytes 170528 | tf_op jit(solution)/shard_map/ppermute | solution.py:507
  13.3 0.0 collective-permute-done.1.even_ref
  13.3 7.6 %rates_twice.1 = (f32[30,72,128]{2,1,0:T(8,128)S(1)}, f32[30,72,128]{2,1,0:T(8,128)S(1)}, f32[30,48,128]{2,1,0:T(8,128)S(1)}, bf16[120,128]{1,0:T(8,128)(2,1)S(1)}, f32[2,48,128]{2,1,0:T(8,128)S(1)}) custom-call(f32[10,3,4096]{2,1,0:T(4,128)} %bitcast.13, f32[32,128]{1,0:T(8,128)} %bitcast.15, f32[4,4096]{1,0:T(4,128)} %metric_hbm.3, s32[32,128]{1,0:T(8,128)} %bitcast.17, ...), custom_call_target="tpu_custom_call" | custom-call | tf_op jit(solution)/shard_map/rates_twice/pallas_call | solution.py:511
  20.9 0.0 all-to-all-done
  20.9 3.6 %sum_and_refine.1 = f32[10,3,6144]{2,1,0:T(4,128)} custom-call(f32[30,72,128]{2,1,0:T(8,128)S(1)} %get-tuple-element.15.cur, f32[30,72,128]{2,1,0:T(8,128)S(1)} %get-tuple-element.16.rate_ref, f32[30,48,128]{2,1,0:T(8,128)S(1)} %get-tuple-element.17.twice_ref, bf16[120,128]{1,0:T(8,128)(2,1)S(1)} %get-tuple-element.18.weights, ...), custom_call_target="tpu_custom_call" | custom-call | tf_op jit(solution)/shard_map/sum_and_refine/pallas_call | solution.py:540
Async XLA Ops:
  1.7 11.6 %collective-permute-start = (f32[333,128]{1,0:T(8,128)S(1)}, f32[333,128]{1,0:T(8,128)S(1)}, u32[]{:S(2)}, u32[]{:S(2)}) collective-permute-start(f32[333,128]{1,0:T(8,128)S(1)} %get-tuple-element.13), channel_id=1, source_target_pairs={{1,2},{3,4},{5,6},{7,8},{9,10},{11,12},{13,14},{15,16},{17,18},{19... | collective-permute-start | bytes 511496 | tf_op jit(solution)/shard_map/ppermute | solution.py:507
  7.5 5.8 %collective-permute-start.1 = (f32[333,128]{1,0:T(8,128)S(1)}, f32[333,128]{1,0:T(8,128)S(1)}, u32[]{:S(2)}, u32[]{:S(2)}) collective-permute-start(f32[333,128]{1,0:T(8,128)S(1)} %get-tuple-element.14), channel_id=1, source_target_pairs={{0,1},{2,3},{4,5},{6,7},{8,9},{10,11},{12,13},{14,15},{16,17},{18,... | collective-permute-start | bytes 511496 | tf_op jit(solution)/shard_map/ppermute | solution.py:508
  7.6 13.3 %all-to-all-start = ((f32[32,1,128]{2,1,0:T(1,128)}), f32[32,1,128]{2,1,0:T(1,128)S(1)}, u32[]{:S(2)}, u32[]{:S(2)}) async-start(f32[32,1,128]{2,1,0:T(1,128)} %bitcast.7), calls=%async_computation | async-start | bytes 32768 | tf_op jit(solution)/shard_map/all_to_all | solution.py:509

commit v6 on v3

--- a/solution.py
+++ b/solution.py
@@ -14,7 +14,10 @@
 AXES = ("row", "col")
 FACES = ((0, 1, 2, 3), (3, 6, 8, 9), (9, 7, 4, 0))
 PACK = 40
+LAID = 41
+SENT = 37
 WIDE = 32
+STEP = 33
 PAD = 8
 
 VMEM = pl.BlockSpec(memory_space=pltpu.VMEM)
@@ -87,20 +90,20 @@
     for copy in copies[3:]:
         copy.wait()
     for ref, source, start in ((even_ref, state_even, even), (odd_ref, state_odd, odd)):
-        pack_state(source, ref, halo)
+        pack_state(source, ref, halo, SENT, 3)
         at = pl.ds(start, halo)
         dense = [depth_ref[at, :]]
         dense += [spread[pl.ds(8 * start + comp, halo, stride=8), :] for comp in range(4)]
         dense += [partner_ref[at, :].astype(jnp.float32), refine_ref[at, :].astype(jnp.float32)]
         for num, value in enumerate(dense):
-            ref[pl.ds(4 * num + 3, halo, stride=PACK), :] = value
+            ref[pl.ds(30 + num, halo, stride=SENT), :] = value
     sent.wait()
 
 
-def pack_state(source, target, blocks):
+def pack_state(source, target, blocks, height, width):
     for block in range(blocks):
         for node in range(10):
-            at = PACK * block + 4 * node
+            at = height * block + width * node
             target[at : at + 3, :] = source[node, :, LANES * block : LANES * (block + 1)]
 
 
@@ -231,16 +234,11 @@
     ends_ref[1] = before + whole
 
 
-def first_kernel(
-    sizes, state_hbm, depth_hbm, metric_hbm, partner_hbm, refine_hbm, odd_ref, even_ref, diff_hbm, lift_hbm, prolong_hbm,
-    cur, rate_ref, twice_ref, weights, ends_ref,
-    geo_ref, state_ref, depth_ref, metric_ref, partner_ref, refine_ref, diff_ref, lift_ref, prolong_ref,
-    spread, wide, aux, sems,
+def prep_kernel(
+    sizes, state_hbm, depth_hbm, metric_hbm, partner_hbm, refine_hbm, cur, aux,
+    state_ref, depth_ref, metric_ref, partner_ref, refine_ref, spread, wide, sems,
 ):
-    blocks, halo = sizes.blocks, sizes.halo
-    top, bottom = PAD + halo, PAD + halo + blocks
-    place = lax.axis_index(AXES)
-    count = lax.axis_size(AXES)
+    blocks = sizes.blocks
     copies = fetch_all(
         (
             (metric_hbm, metric_ref),
@@ -248,9 +246,6 @@
             (depth_hbm, depth_ref),
             (partner_hbm, partner_ref),
             (refine_hbm, refine_ref),
-            (diff_hbm, diff_ref),
-            (lift_hbm, lift_ref),
-            (prolong_hbm, prolong_ref),
         ),
         sems,
     )
@@ -258,24 +253,43 @@
         copy.wait()
     metric = split_metric(metric_ref, spread, blocks)
     dense = [depth_ref[...], *metric, partner_ref[...].astype(jnp.float32), refine_ref[...].astype(jnp.float32)]
-    pack_state(state_ref, wide, blocks)
+    for num in range(7):
+        aux[num] = dense[num]
+    pack_state(state_ref, wide, blocks, LAID, 4)
+    for field in range(3):
+        for node in range(10):
+            cur[10 * field + node] = wide[pl.ds(4 * node + field, blocks, stride=LAID), :]
+
+
+def first_kernel(
+    sizes, cur_own, aux_own, odd_ref, even_ref, diff_hbm, lift_hbm, prolong_hbm,
+    cur, rate_ref, twice_ref, weights, ends_ref,
+    geo_ref, aux, diff_ref, lift_ref, prolong_ref, sems,
+):
+    blocks, halo = sizes.blocks, sizes.halo
+    top, bottom = PAD + halo, PAD + halo + blocks
+    place = lax.axis_index(AXES)
+    count = lax.axis_size(AXES)
+    copies = fetch_all(((diff_hbm, diff_ref), (lift_hbm, lift_ref), (prolong_hbm, prolong_ref)), sems)
     even = place % 2 == 0
 
     def set_halo(target, num, row):
-        by_even = even_ref[pl.ds(row, halo, stride=PACK), :]
-        by_odd = odd_ref[pl.ds(row, halo, stride=PACK), :]
+        by_even = even_ref[pl.ds(row, halo, stride=SENT), :]
+        by_odd = odd_ref[pl.ds(row, halo, stride=SENT), :]
         target[num, top - halo : top, :] = jnp.where(even, by_odd, by_even)
         target[num, bottom : bottom + halo, :] = jnp.where(even, by_even, by_odd)
 
     for num in range(7):
-        set_halo(aux, num, 4 * num + 3)
-        aux[num, top:bottom, :] = dense[num]
+        set_halo(aux, num, 30 + num)
+        aux[num, top:bottom, :] = aux_own[num]
     for field in range(3):
         for node in range(10):
             item = 10 * field + node
-            set_halo(cur, item, 4 * node + field)
-            cur[item, top:bottom, :] = wide[pl.ds(4 * node + field, blocks, stride=PACK), :]
-
+            set_halo(cur, item, 3 * node + field)
+            cur[item, top:bottom, :] = cur_own[item]
+
+    for copy in copies:
+        copy.wait()
     weights[...] = child_matrix(prolong_ref)
     begin = PAD + sizes.keep
     sum_children(sizes, aux[6, begin : begin + sizes.slots, :], ends_ref)
@@ -333,7 +347,7 @@
 
 def refine_kernel(
     sizes, cur, rate_ref, twice_ref, weights, base_ref, stats_ref, out_hbm,
-    out_ref, ends_ref, place_v, place_s, wide, gathered, index_ref, out_sems, sem,
+    out_ref, ends_ref, place_v, place_s, wide, index_ref, out_sems, sem,
 ):
     slots, keep = sizes.slots, sizes.keep
     place = lax.axis_index(AXES)
@@ -359,9 +373,9 @@
     for item in range(30):
         now = slice(PAD + keep, PAD + keep + slots)
         value = cur[item, now, :] + step * rate_ref[item, now, :] + half_square * twice_ref[item]
-        wide[pl.ds(item, slots, stride=WIDE), :] = value
+        wide[pl.ds(item, slots, stride=STEP), :] = value
     for item in (30, 31):
-        wide[pl.ds(item, slots + 1, stride=WIDE), :] = jnp.zeros((slots + 1, LANES), jnp.float32)
+        wide[pl.ds(item, slots + 1, stride=STEP), :] = jnp.zeros((slots + 1, LANES), jnp.float32)
     copy.wait()
     for slot in range(slots):
         lead_at = place_s[0, slot]
@@ -389,22 +403,23 @@
     index_ref[0] = found.astype(jnp.float32)
     index_ref[1] = kind.astype(jnp.float32)
     index_ref[2] = (lane < jnp.broadcast_to(found[:, 0:1], (slots, LANES))).astype(jnp.float32)
-    for slot in range(slots):
-        lead_at = place_s[0, slot] * WIDE
-        lane_idx = jnp.broadcast_to(index_ref[0, slot : slot + 1, :], (8, LANES)).astype(jnp.int32)
-        ahead = jnp.broadcast_to(index_ref[2, slot : slot + 1, :], (8, LANES)) > 0.5
-        for part in range(0, WIDE, 8):
-            one = wide[pl.ds(pl.multiple_of(lead_at + part, 8), 8), :]
-            two = wide[pl.ds(pl.multiple_of(lead_at + WIDE + part, 8), 8), :]
-            gathered[part : part + 8, LANES * slot : LANES * (slot + 1)] = lane_gather(
-                jnp.where(ahead, two, one), lane_idx
-            )
     matrix = weights[...]
     chunk = 8 * LANES
     results = []
     for part in range(slots // 8):
         span = slice(chunk * part, chunk * (part + 1))
-        values = gathered[:, span]
+        columns = []
+        for slot in range(8 * part, 8 * part + 8):
+            lead_at = place_s[0, slot] * STEP
+            lane_idx = jnp.broadcast_to(index_ref[0, slot : slot + 1, :], (8, LANES)).astype(jnp.int32)
+            ahead = jnp.broadcast_to(index_ref[2, slot : slot + 1, :], (8, LANES)) > 0.5
+            tiles = []
+            for row in range(0, WIDE, 8):
+                one = wide[pl.ds(lead_at + row, 8), :]
+                two = wide[pl.ds(lead_at + STEP + row, 8), :]
+                tiles.append(lane_gather(jnp.where(ahead, two, one), lane_idx))
+            columns.append(jnp.concatenate(tiles, axis=0))
+        values = jnp.concatenate(columns, axis=1)
         high = values.astype(jnp.bfloat16)
         rest = values - high.astype(jnp.float32)
         low = rest.astype(jnp.bfloat16)
@@ -445,7 +460,7 @@
         for x in (state, depth, metric, partner, refine, diff_ops, lift, prolong)
     ]
     f32, i32 = jnp.float32, jnp.int32
-    packed = jax.ShapeDtypeStruct((PACK * halo, LANES), f32)
+    packed = jax.ShapeDtypeStruct((SENT * halo, LANES), f32)
     dense = [
         pltpu.VMEM((blocks, LANES), f32),
         pltpu.VMEM(metric.shape, f32),
@@ -473,9 +488,29 @@
     even = lax.ppermute(even, AXES, swaps(0, count))
     stats = lax.all_to_all(stats, AXES, 0, 0, tiled=True)
     even, odd, stats = [pltpu.with_memory_space_constraint(x, pltpu.VMEM) for x in (even, odd, stats)]
+    cur, aux = pl.pallas_call(
+        functools.partial(prep_kernel, sizes),
+        name="lay_out",
+        cost_estimate=pl.CostEstimate(flops=1 << 24, transcendentals=1 << 16, bytes_accessed=1 << 24),
+        out_shape=(
+            jax.ShapeDtypeStruct((30, blocks, LANES), f32),
+            jax.ShapeDtypeStruct((7, blocks, LANES), f32),
+        ),
+        in_specs=[HBM] * 5,
+        out_specs=(VMEM,) * 2,
+        scratch_shapes=[
+            pltpu.VMEM(state.shape, f32),
+            *dense,
+            pltpu.VMEM((8 * blocks, LANES), f32),
+            pltpu.VMEM((LAID * blocks, LANES), f32),
+            pltpu.SemaphoreType.DMA((5,)),
+        ],
+        compiler_params=PARAMS,
+    )(state, depth, metric, partner, refine)
     cur, rates, twice, weights, ends = pl.pallas_call(
         functools.partial(first_kernel, sizes),
         name="rates_twice",
+        cost_estimate=pl.CostEstimate(flops=1024, transcendentals=0, bytes_accessed=1024),
         out_shape=(
             jax.ShapeDtypeStruct((30, sizes.tall, LANES), f32),
             jax.ShapeDtypeStruct((30, sizes.tall, LANES), f32),
@@ -483,22 +518,18 @@
             jax.ShapeDtypeStruct((3 * PACK, 4 * WIDE), jnp.bfloat16),
             jax.ShapeDtypeStruct((2, slots, LANES), f32),
         ),
-        in_specs=[HBM] * 5 + [VMEM] * 2 + [HBM] * 3,
+        in_specs=[VMEM] * 4 + [HBM] * 3,
         out_specs=(VMEM,) * 5,
         scratch_shapes=[
             pltpu.VMEM((15, rows, LANES), f32),
-            pltpu.VMEM(state.shape, f32),
-            *dense,
+            pltpu.VMEM((7, sizes.tall, LANES), f32),
             pltpu.SMEM(diff_ops.shape, f32),
             pltpu.SMEM(lift.shape, f32),
             pltpu.VMEM(prolong.shape, f32),
-            pltpu.VMEM((8 * blocks, LANES), f32),
-            pltpu.VMEM((PACK * blocks, LANES), f32),
-            pltpu.VMEM((7, sizes.tall, LANES), f32),
-            pltpu.SemaphoreType.DMA((8,)),
+            pltpu.SemaphoreType.DMA((3,)),
         ],
         compiler_params=PARAMS,
-    )(state, depth, metric, partner, refine, odd, even, diff_ops, lift, prolong)
+    )(cur, aux, odd, even, diff_ops, lift, prolong)
     refined = pl.pallas_call(
         functools.partial(refine_kernel, sizes),
         name="sum_and_refine",
@@ -510,8 +541,7 @@
             pltpu.VMEM((slots + 8, LANES), f32),
             pltpu.VMEM((8, LANES), i32),
             pltpu.SMEM((8, LANES), i32),
-            pltpu.VMEM((WIDE * (slots + 1), LANES), f32),
-            pltpu.VMEM((WIDE, LANES * slots), f32),
+            pltpu.VMEM((STEP * (slots + 1), LANES), f32),
             pltpu.VMEM((3, slots, LANES), f32),
             pltpu.SemaphoreType.DMA((slots // 8,)),
             pltpu.SemaphoreType.DMA,

time: 23.9 us -> 23 us (0.962)
  waiting for transfers between devices: 3.11 us -> 1.51 us
  Pallas kernels: 11.7 us -> 12.3 us
    ppermute x1, waiting for transfers between devices: 3.11 us -> 1.5 us  [shards(): odd = lax.ppermute(odd, AXES, swaps(1, count))]
    pallas_call x0 -> x1, Pallas kernels: none -> 1.35 us  [shards(): pl.pallas_call(functools.partial(prep_kernel, sizes), name='lay_out', cos...]
    pallas_call x1, Pallas kernels: 6.45 us -> 5.95 us  [shards(): pl.pallas_call(functools.partial(first_kernel, sizes), name='rates_twice'...]
  transfers between devices with their start and end apart: 3 -> 3, of which waited for: 1 -> 1; matrix products, arithmetic and copies ran while one was open for 0% -> 0% of each run, Pallas kernels for 27% -> 32%
where the time goes in v6:
time: 23 us; the launch traced here: 22.6 us
  Pallas kernels  12.3 us (53%)
  starting transfers between devices  8.74 us (38%)
  waiting for transfers between devices  1.51 us (7%)
    pallas_call x1, Pallas kernels, shards(): pl.pallas_call(functools.partial(first_kernel, sizes), name='rates_twice'...  5.95 us
    ppermute x1, starting transfers between devices, shards(): odd = lax.ppermute(odd, AXES, swaps(1, count))  5.82 us
    pallas_call x1, Pallas kernels, shards(): pl.pallas_call(functools.partial(refine_kernel, sizes), name='sum_and_ref...  3.39 us
    all_to_all x1, starting transfers between devices, shards(): stats = lax.all_to_all(stats, AXES, 0, 0, tiled=True)  2.85 us
    pallas_call x1, Pallas kernels, shards(): pl.pallas_call(functools.partial(pack_kernel, sizes), name='pack', out_sh...  1.65 us
    ppermute x1, waiting for transfers between devices, shards(): odd = lax.ppermute(odd, AXES, swaps(1, count))  1.5 us
    pallas_call x1, Pallas kernels, shards(): pl.pallas_call(functools.partial(prep_kernel, sizes), name='lay_out', cos...  1.35 us
  transfers between devices with their start and end apart: 3, of which 1 were waited for; matrix products, arithmetic and copies ran while one was open for 0% of the time, Pallas kernels for 32%

profile of v6, /device:TPU:4, one launch (start us, length us, event | category | flops | bytes accessed | tf_op | source)
XLA Modules:
  0.0 22.6 jit_solution(6786737421488860285)
XLA Ops:
  0.0 1.7 %pack.1 = (f32[32,128]{1,0:T(8,128)}, f32[333,128]{1,0:T(8,128)S(1)}, f32[333,128]{1,0:T(8,128)S(1)}) custom-call(f32[10,3,4096]{2,1,0:T(4,128)} %bitcast.12, f32[32,128]{1,0:T(8,128)} %bitcast.14, f32[4,4096]{1,0:T(4,128)} %metric_hbm.3, s32[32,128]{1,0:T(8,128)} %bitcast.16, s32[32,128]{1,0:T(8,128)} %bitcast.18), custom_call_target="tpu_custom_call" | custom-call | tf_op jit(solution)/shard_map/pack/pallas_call | solution.py:470
  1.7 5.8 %collective-permute-start = (f32[333,128]{1,0:T(8,128)S(1)}, f32[333,128]{1,0:T(8,128)S(1)}, u32[]{:S(2)}, u32[]{:S(2)}) collective-permute-start(f32[333,128]{1,0:T(8,128)S(1)} %get-tuple-element.17), channel_id=1, source_target_pairs={{1,2},{3,4},{5,6},{7,8},{9,10},{11,12},{13,14},{15,16},{17,18},{19... | collective-permute-start | bytes 511496 | tf_op jit(solution)/shard_map/ppermute | solution.py:487
  7.5 0.1 collective-permute-start.1
  7.6 2.9 %all-to-all-start = ((f32[32,1,128]{2,1,0:T(1,128)}), f32[32,1,128]{2,1,0:T(1,128)S(1)}, u32[]{:S(2)}, u32[]{:S(2)}) async-start(f32[32,1,128]{2,1,0:T(1,128)} %bitcast.7), calls=%async_computation | async-start | bytes 32768 | tf_op jit(solution)/shard_map/all_to_all | solution.py:489
  10.4 1.3 %lay_out.1 = (f32[30,32,128]{2,1,0:T(8,128)S(1)}, f32[7,32,128]{2,1,0:T(8,128)S(1)}) custom-call(f32[10,3,4096]{2,1,0:T(4,128)} %bitcast.13, f32[32,128]{1,0:T(8,128)} %bitcast.15, f32[4,4096]{1,0:T(4,128)} %metric_hbm.3, s32[32,128]{1,0:T(8,128)} %bitcast.17, s32[32,128]{1,0:T(8,128)} %bitcast.19), custom_call_target="tpu_custom_call" | custom-call | flops 16777216 | bytes 16777216 | tf_op jit(solution)/shard_map/lay_out/pallas_call | solution.py:491
  11.8 1.5 %collective-permute-done.odd_ref = f32[333,128]{1,0:T(8,128)S(1)} collective-permute-done((f32[333,128]{1,0:T(8,128)S(1)}, f32[333,128]{1,0:T(8,128)S(1)}, u32[]{:S(2)}, u32[]{:S(2)}) %collective-permute-start) | collective-permute-done | bytes 170528 | tf_op jit(solution)/shard_map/ppermute | solution.py:487
  13.3 0.0 collective-permute-done.1.even_ref
  13.3 5.9 %rates_twice.1 = (f32[30,72,128]{2,1,0:T(8,128)S(1)}, f32[30,72,128]{2,1,0:T(8,128)S(1)}, f32[30,48,128]{2,1,0:T(8,128)S(1)}, bf16[120,128]{1,0:T(8,128)(2,1)S(1)}, f32[2,48,128]{2,1,0:T(8,128)S(1)}) custom-call(f32[30,32,128]{2,1,0:T(8,128)S(1)} %get-tuple-element.15.cur_own, f32[7,32,128]{2,1,0:T(8,128)S(1)} %get-tuple-element.16.aux_own, ...), custom_call_target="tpu_custom_call" | custom-call | flops 1024 | bytes 1024 | tf_op jit(solution)/shard_map/rates_twice/pallas_call | solution.py:510
  19.2 0.0 all-to-all-done
  19.3 3.4 %sum_and_refine.1 = f32[10,3,6144]{2,1,0:T(4,128)} custom-call(f32[30,72,128]{2,1,0:T(8,128)S(1)} %get-tuple-element.19.cur, f32[30,72,128]{2,1,0:T(8,128)S(1)} %get-tuple-element.20.rate_ref, f32[30,48,128]{2,1,0:T(8,128)S(1)} %get-tuple-element.21.twice_ref, bf16[120,128]{1,0:T(8,128)(2,1)S(1)} %get-tuple-element.22.weights, ...), custom_call_target="tpu_custom_call" | custom-call | tf_op jit(solution)/shard_map/sum_and_refine/pallas_call | solution.py:533
Async XLA Ops:
  1.7 11.6 %collective-permute-start = (f32[333,128]{1,0:T(8,128)S(1)}, f32[333,128]{1,0:T(8,128)S(1)}, u32[]{:S(2)}, u32[]{:S(2)}) collective-permute-start(f32[333,128]{1,0:T(8,128)S(1)} %get-tuple-element.17), channel_id=1, source_target_pairs={{1,2},{3,4},{5,6},{7,8},{9,10},{11,12},{13,14},{15,16},{17,18},{19... | collective-permute-start | bytes 511496 | tf_op jit(solution)/shard_map/ppermute | solution.py:487
  7.5 5.8 %collective-permute-start.1 = (f32[333,128]{1,0:T(8,128)S(1)}, f32[333,128]{1,0:T(8,128)S(1)}, u32[]{:S(2)}, u32[]{:S(2)}) collective-permute-start(f32[333,128]{1,0:T(8,128)S(1)} %get-tuple-element.18), channel_id=1, source_target_pairs={{0,1},{2,3},{4,5},{6,7},{8,9},{10,11},{12,13},{14,15},{16,17},{18,... | collective-permute-start | bytes 511496 | tf_op jit(solution)/shard_map/ppermute | solution.py:488
  7.6 11.7 %all-to-all-start = ((f32[32,1,128]{2,1,0:T(1,128)}), f32[32,1,128]{2,1,0:T(1,128)S(1)}, u32[]{:S(2)}, u32[]{:S(2)}) async-start(f32[32,1,128]{2,1,0:T(1,128)} %bitcast.7), calls=%async_computation | async-start | bytes 32768 | tf_op jit(solution)/shard_map/all_to_all | solution.py:489

commit v7 on v6

--- a/solution.py
+++ b/solution.py
@@ -146,10 +146,23 @@
 def tendency(load, geo, walls, index, inside, diff_ref, lift_ref):
     speed_sq, rx, ry, sx, sy = geo[:5]
     outer_sq, waves, ghosts = geo[5:8], geo[8:11], geo[11:14]
-    own = [[load(10 * field + node, 0) for node in range(10)] for field in range(3)]
-    eta, mom_x, mom_y = own
-    flow_r = [-(rx * mom_x[b] + ry * mom_y[b]) for b in range(10)]
-    flow_s = [-(sx * mom_x[b] + sy * mom_y[b]) for b in range(10)]
+    inflow, along_r, along_s = [None] * 10, [None] * 10, [None] * 10
+
+    def add(total, term):
+        return term if total is None else total + term
+
+    for b in range(10):
+        eta, mom_x, mom_y = [load(10 * field + b, 0) for field in range(3)]
+        flow_r = -(rx * mom_x + ry * mom_y)
+        flow_s = -(sx * mom_x + sy * mom_y)
+        for a in range(10):
+            d_r, d_s = diff_ref[a, 0, b], diff_ref[a, 1, b]
+            inflow[a] = add(inflow[a], d_r * flow_r + d_s * flow_s)
+            along_r[a] = add(along_r[a], d_r * eta)
+            along_s[a] = add(along_s[a], d_s * eta)
+    pull = (-speed_sq * rx, -speed_sq * ry)
+    push = (-speed_sq * sx, -speed_sq * sy)
+    sums = [inflow] + [[pull[k] * along_r[a] + push[k] * along_s[a] for a in range(10)] for k in range(2)]
     half_r = (0.5 * rx, 0.5 * ry)
     half_s = (0.5 * sx, 0.5 * sy)
     vectors = (
@@ -158,42 +171,29 @@
         (-half_r[0], -half_r[1]),
     )
     fetch = outer_values(load, index, inside)
-    jumps = ([], [], [])
     for face in range(3):
         vec_x, vec_y = vectors[face]
         theirs = FACES[(1, 0, 2)[face]]
         wall = walls[face]
         for j in range(4):
             node, match = FACES[face][j], theirs[3 - j]
-            in_eta, in_x, in_y = eta[node], mom_x[node], mom_y[node]
+            in_eta, in_x, in_y = [load(10 * field + node, 0) for field in range(3)]
             ext_eta, ext_x, ext_y = [fetch[face](10 * field + match) for field in range(3)]
             bounce = (in_x * vec_x + in_y * vec_y) * ghosts[face]
             d_eta = jnp.where(wall, 0.0, in_eta - ext_eta)
             d_x = jnp.where(wall, bounce * vec_x, in_x - ext_x)
             d_y = jnp.where(wall, bounce * vec_y, in_y - ext_y)
             head = jnp.where(wall, 0.0, speed_sq * in_eta - outer_sq[face] * ext_eta)
-            jumps[0].append(d_x * vec_x + d_y * vec_y - waves[face] * d_eta)
-            jumps[1].append(head * vec_x - waves[face] * d_x)
-            jumps[2].append(head * vec_y - waves[face] * d_y)
-    pull = (-speed_sq * rx, -speed_sq * ry)
-    push = (-speed_sq * sx, -speed_sq * sy)
-    out = [[None] * 10 for _ in range(3)]
-    for a in range(10):
-        total = along_r = along_s = None
-        for b in range(10):
-            d_r, d_s = diff_ref[a, 0, b], diff_ref[a, 1, b]
-            term = d_r * flow_r[b] + d_s * flow_s[b]
-            total = term if b == 0 else total + term
-            along_r = d_r * eta[b] if b == 0 else along_r + d_r * eta[b]
-            along_s = d_s * eta[b] if b == 0 else along_s + d_s * eta[b]
-        sums = [total, pull[0] * along_r + push[0] * along_s, pull[1] * along_r + push[1] * along_s]
-        for q in range(12):
-            weight = lift_ref[a, q]
-            for field in range(3):
-                sums[field] = sums[field] + weight * jumps[field][q]
-        for field in range(3):
-            out[field][a] = sums[field]
-    return [out[field][a] for field in range(3) for a in range(10)]
+            jumps = (
+                d_x * vec_x + d_y * vec_y - waves[face] * d_eta,
+                head * vec_x - waves[face] * d_x,
+                head * vec_y - waves[face] * d_y,
+            )
+            for a in range(10):
+                weight = lift_ref[a, 4 * face + j]
+                for field in range(3):
+                    sums[field][a] = sums[field][a] + weight * jumps[field]
+    return [sums[field][a] for field in range(3) for a in range(10)]
 
 
 def child_matrix(prolong_ref):
@@ -214,10 +214,10 @@
     whole = jnp.concatenate(parts, axis=0)
     rounded = whole.astype(jnp.bfloat16)
     rest = (whole - rounded.astype(f32)).astype(jnp.bfloat16)
-    return jnp.concatenate([rounded, rounded, rounded, rest], axis=1)
-
-
-def sum_children(sizes, refine, ends_ref):
+    return jnp.concatenate([rounded, rounded, rest], axis=1)
+
+
+def sum_children(sizes, refine, ends_ref, lines_ref):
     slots, f32 = sizes.slots, jnp.float32
     counts = (1.0 + refine).astype(jnp.bfloat16)
     row_i = lax.broadcasted_iota(jnp.int32, (LANES, LANES), 0)
@@ -232,6 +232,16 @@
     before = before - before[sizes.margin : sizes.margin + 1, :]
     ends_ref[0] = 2.0 * (within + before) + refine
     ends_ref[1] = before + whole
+    ones = jnp.ones((8, LANES), jnp.bfloat16)
+    sums = lax.dot_general(ones, counts, (((1,), (1,)), ((), ())), preferred_element_type=f32)
+    gap = lax.broadcasted_iota(jnp.int32, (slots, LANES), 1) - lax.broadcasted_iota(jnp.int32, (slots, LANES), 0)
+    lines = [
+        jnp.dot(sums.astype(jnp.bfloat16), (gap >= least).astype(jnp.bfloat16), preferred_element_type=f32)
+        for least in (2, 1, 0)
+    ]
+    own = lines[1][:, sizes.margin : sizes.margin + 1]
+    for num in range(3):
+        lines_ref[num] = lines[num] - own
 
 
 def prep_kernel(
@@ -263,7 +273,7 @@
 
 def first_kernel(
     sizes, cur_own, aux_own, odd_ref, even_ref, diff_hbm, lift_hbm, prolong_hbm,
-    cur, rate_ref, twice_ref, weights, ends_ref,
+    cur, rate_ref, twice_ref, weights, ends_ref, lines_ref,
     geo_ref, aux, diff_ref, lift_ref, prolong_ref, sems,
 ):
     blocks, halo = sizes.blocks, sizes.halo
@@ -292,7 +302,7 @@
         copy.wait()
     weights[...] = child_matrix(prolong_ref)
     begin = PAD + sizes.keep
-    sum_children(sizes, aux[6, begin : begin + sizes.slots, :], ends_ref)
+    sum_children(sizes, aux[6, begin : begin + sizes.slots, :], ends_ref, lines_ref)
 
     def step(group, carry):
         base = PAD + 8 * group
@@ -346,8 +356,8 @@
 
 
 def refine_kernel(
-    sizes, cur, rate_ref, twice_ref, weights, base_ref, stats_ref, out_hbm,
-    out_ref, ends_ref, place_v, place_s, wide, index_ref, out_sems, sem,
+    sizes, cur, rate_ref, twice_ref, weights, base_ref, lines_ref, stats_ref, out_hbm,
+    out_ref, place_v, place_s, wide, index_ref, out_sems, sem,
 ):
     slots, keep = sizes.slots, sizes.keep
     place = lax.axis_index(AXES)
@@ -362,8 +372,6 @@
     step = COURANT / top
     half_square = 0.5 * step * step
     start = earlier - (place * (sizes.cells // 2)).astype(jnp.float32)
-    ends_ref[:slots, :] = base_ref[0] + 2.0 * start
-    ends_ref[slots:, :] = jnp.full((8, LANES), 1e9, jnp.float32)
     first_slot = LANES * lax.broadcasted_iota(jnp.int32, (slots, LANES), 1).astype(jnp.float32)
     lead = jnp.sum((base_ref[1] + start <= first_slot).astype(jnp.float32), axis=0, keepdims=True)
     lead = jnp.clip(lead.astype(jnp.int32), 0, slots - 1)
@@ -376,12 +384,18 @@
         wide[pl.ds(item, slots, stride=STEP), :] = value
     for item in (30, 31):
         wide[pl.ds(item, slots + 1, stride=STEP), :] = jnp.zeros((slots + 1, LANES), jnp.float32)
-    copy.wait()
-    for slot in range(slots):
-        lead_at = place_s[0, slot]
-        index_ref[0, slot : slot + 1, :] = ends_ref[pl.ds(lead_at, 1), :]
-        index_ref[1, slot : slot + 1, :] = ends_ref[pl.ds(lead_at + 1, 1), :]
-    near, far = index_ref[0], index_ref[1]
+    slot_start = LANES * lax.broadcasted_iota(jnp.int32, (slots, LANES), 0).astype(jnp.float32)
+    begun = [lines_ref[num, 0:1, :] + start <= slot_start for num in range(3)]
+    near, far = [
+        2.0 * start
+        + jnp.dot(
+            (begun[num] & ~begun[num + 1]).astype(jnp.float32)[:, :slots],
+            base_ref[0],
+            precision=HIGH,
+            preferred_element_type=jnp.float32,
+        )
+        for num in (1, 0)
+    ]
     lane = lax.broadcasted_iota(jnp.int32, (slots, LANES), 1)
     slot_no = LANES * lax.broadcasted_iota(jnp.int32, (slots, LANES), 0) + lane
     goal = (2 * slot_no + 1).astype(jnp.float32)
@@ -403,6 +417,7 @@
     index_ref[0] = found.astype(jnp.float32)
     index_ref[1] = kind.astype(jnp.float32)
     index_ref[2] = (lane < jnp.broadcast_to(found[:, 0:1], (slots, LANES))).astype(jnp.float32)
+    copy.wait()
     matrix = weights[...]
     chunk = 8 * LANES
     results = []
@@ -421,10 +436,8 @@
             columns.append(jnp.concatenate(tiles, axis=0))
         values = jnp.concatenate(columns, axis=1)
         high = values.astype(jnp.bfloat16)
-        rest = values - high.astype(jnp.float32)
-        low = rest.astype(jnp.bfloat16)
-        last = (rest - low.astype(jnp.float32)).astype(jnp.bfloat16)
-        stack = jnp.concatenate([high, low, last, high], axis=0)
+        low = (values - high.astype(jnp.float32)).astype(jnp.bfloat16)
+        stack = jnp.concatenate([high, low, high], axis=0)
         children = jnp.dot(matrix, stack, preferred_element_type=jnp.float32)
         for sub in range(8):
             slot = 8 * part + sub
@@ -507,7 +520,7 @@
         ],
         compiler_params=PARAMS,
     )(state, depth, metric, partner, refine)
-    cur, rates, twice, weights, ends = pl.pallas_call(
+    cur, rates, twice, weights, ends, lines = pl.pallas_call(
         functools.partial(first_kernel, sizes),
         name="rates_twice",
         cost_estimate=pl.CostEstimate(flops=1024, transcendentals=0, bytes_accessed=1024),
@@ -515,11 +528,12 @@
             jax.ShapeDtypeStruct((30, sizes.tall, LANES), f32),
             jax.ShapeDtypeStruct((30, sizes.tall, LANES), f32),
             jax.ShapeDtypeStruct((30, slots, LANES), f32),
-            jax.ShapeDtypeStruct((3 * PACK, 4 * WIDE), jnp.bfloat16),
+            jax.ShapeDtypeStruct((3 * PACK, 3 * WIDE), jnp.bfloat16),
             jax.ShapeDtypeStruct((2, slots, LANES), f32),
+            jax.ShapeDtypeStruct((3, 8, LANES), f32),
         ),
         in_specs=[VMEM] * 4 + [HBM] * 3,
-        out_specs=(VMEM,) * 5,
+        out_specs=(VMEM,) * 6,
         scratch_shapes=[
             pltpu.VMEM((15, rows, LANES), f32),
             pltpu.VMEM((7, sizes.tall, LANES), f32),
@@ -534,11 +548,10 @@
         functools.partial(refine_kernel, sizes),
         name="sum_and_refine",
         out_shape=jax.ShapeDtypeStruct((10, 3, LANES * slots), f32),
-        in_specs=[VMEM] * 6,
+        in_specs=[VMEM] * 7,
         out_specs=HBM,
         scratch_shapes=[
             pltpu.VMEM((10, 3, LANES * slots), f32),
-            pltpu.VMEM((slots + 8, LANES), f32),
             pltpu.VMEM((8, LANES), i32),
             pltpu.SMEM((8, LANES), i32),
             pltpu.VMEM((STEP * (slots + 1), LANES), f32),
@@ -547,7 +560,7 @@
             pltpu.SemaphoreType.DMA,
         ],
         compiler_params=PARAMS,
-    )(cur, rates, twice, weights, ends, stats)
+    )(cur, rates, twice, weights, ends, lines, stats)
     return jnp.transpose(refined, (1, 0, 2))
 
 

time: 23 us -> 22.1 us (0.961)
  Pallas kernels: 12.3 us -> 11.4 us
    pallas_call x1, Pallas kernels: 3.39 us -> 2.5 us  [shards(): pl.pallas_call(functools.partial(refine_kernel, sizes), name='sum_and_ref...]
  transfers between devices with their start and end apart: 3 -> 3, of which waited for: 1 -> 1; matrix products, arithmetic and copies ran while one was open for 0% -> 0% of each run, Pallas kernels for 32% -> 33%
where the time goes in v7:
time: 22.1 us; the launch traced here: 21.7 us
  Pallas kernels  11.4 us (52%)
  starting transfers between devices  8.74 us (40%)
  waiting for transfers between devices  1.51 us (7%)
    pallas_call x1, Pallas kernels, shards(): pl.pallas_call(functools.partial(first_kernel, sizes), name='rates_twice'...  5.89 us
    ppermute x1, starting transfers between devices, shards(): odd = lax.ppermute(odd, AXES, swaps(1, count))  5.82 us
    all_to_all x1, starting transfers between devices, shards(): stats = lax.all_to_all(stats, AXES, 0, 0, tiled=True)  2.85 us
    pallas_call x1, Pallas kernels, shards(): pl.pallas_call(functools.partial(refine_kernel, sizes), name='sum_and_ref...  2.5 us
    pallas_call x1, Pallas kernels, shards(): pl.pallas_call(functools.partial(pack_kernel, sizes), name='pack', out_sh...  1.65 us
    ppermute x1, waiting for transfers between devices, shards(): odd = lax.ppermute(odd, AXES, swaps(1, count))  1.5 us
    pallas_call x1, Pallas kernels, shards(): pl.pallas_call(functools.partial(prep_kernel, sizes), name='lay_out', cos...  1.35 us
  transfers between devices with their start and end apart: 3, of which 1 were waited for; matrix products, arithmetic and copies ran while one was open for 0% of the time, Pallas kernels for 33%

profile of v7, /device:TPU:4, one launch (start us, length us, event | category | flops | bytes accessed | tf_op | source)
XLA Modules:
  0.0 21.7 jit_solution(42892424689011177)
XLA Ops:
  0.0 1.7 %pack.1 = (f32[32,128]{1,0:T(8,128)}, f32[333,128]{1,0:T(8,128)S(1)}, f32[333,128]{1,0:T(8,128)S(1)}) custom-call(f32[10,3,4096]{2,1,0:T(4,128)} %bitcast.12, f32[32,128]{1,0:T(8,128)} %bitcast.14, f32[4,4096]{1,0:T(4,128)} %metric_hbm.3, s32[32,128]{1,0:T(8,128)} %bitcast.16, s32[32,128]{1,0:T(8,128)} %bitcast.18), custom_call_target="tpu_custom_call" | custom-call | tf_op jit(solution)/shard_map/pack/pallas_call | solution.py:483
  1.7 5.8 %collective-permute-start = (f32[333,128]{1,0:T(8,128)S(1)}, f32[333,128]{1,0:T(8,128)S(1)}, u32[]{:S(2)}, u32[]{:S(2)}) collective-permute-start(f32[333,128]{1,0:T(8,128)S(1)} %get-tuple-element.18), channel_id=1, source_target_pairs={{1,2},{3,4},{5,6},{7,8},{9,10},{11,12},{13,14},{15,16},{17,18},{19... | collective-permute-start | bytes 511496 | tf_op jit(solution)/shard_map/ppermute | solution.py:500
  7.5 0.1 collective-permute-start.1
  7.6 2.9 %all-to-all-start = ((f32[32,1,128]{2,1,0:T(1,128)}), f32[32,1,128]{2,1,0:T(1,128)S(1)}, u32[]{:S(2)}, u32[]{:S(2)}) async-start(f32[32,1,128]{2,1,0:T(1,128)} %bitcast.7), calls=%async_computation | async-start | bytes 32768 | tf_op jit(solution)/shard_map/all_to_all | solution.py:502
  10.4 1.3 %lay_out.1 = (f32[30,32,128]{2,1,0:T(8,128)S(1)}, f32[7,32,128]{2,1,0:T(8,128)S(1)}) custom-call(f32[10,3,4096]{2,1,0:T(4,128)} %bitcast.13, f32[32,128]{1,0:T(8,128)} %bitcast.15, f32[4,4096]{1,0:T(4,128)} %metric_hbm.3, s32[32,128]{1,0:T(8,128)} %bitcast.17, s32[32,128]{1,0:T(8,128)} %bitcast.19), custom_call_target="tpu_custom_call" | custom-call | flops 16777216 | bytes 16777216 | tf_op jit(solution)/shard_map/lay_out/pallas_call | solution.py:504
  11.8 1.5 %collective-permute-done.odd_ref = f32[333,128]{1,0:T(8,128)S(1)} collective-permute-done((f32[333,128]{1,0:T(8,128)S(1)}, f32[333,128]{1,0:T(8,128)S(1)}, u32[]{:S(2)}, u32[]{:S(2)}) %collective-permute-start) | collective-permute-done | bytes 170528 | tf_op jit(solution)/shard_map/ppermute | solution.py:500
  13.3 0.0 collective-permute-done.1.even_ref
  13.3 5.9 %rates_twice.1 = (f32[30,72,128]{2,1,0:T(8,128)S(1)}, f32[30,72,128]{2,1,0:T(8,128)S(1)}, f32[30,48,128]{2,1,0:T(8,128)S(1)}, bf16[120,96]{1,0:T(8,128)(2,1)S(1)...) custom-call(f32[30,32,128]{2,1,0:T(8,128)S(1)} %get-tuple-element.16.cur_own, ...), custom_call_target="tpu_custom_call" | custom-call | flops 1024 | bytes 1024 | tf_op jit(solution)/shard_map/rates_twice/pallas_call | solution.py:523
  19.2 0.0 all-to-all-done
  19.2 2.5 %sum_and_refine.1 = f32[10,3,6144]{2,1,0:T(4,128)} custom-call(f32[30,72,128]{2,1,0:T(8,128)S(1)} %get-tuple-element.20.cur, f32[30,72,128]{2,1,0:T(8,128)S(1)} %get-tuple-element.21.rate_ref, f32[30,48,128]{2,1,0:T(8,128)S(1)} %get-tuple-element.22.twice_ref, bf16[120,96]{1,0:T(8,128)(2,1)S(1)} %get-tuple-element.23.weights, ...), custom_call_target="tpu_custom_call" | custom-call | tf_op jit(solution)/shard_map/sum_and_refine/pallas_call | solution.py:547
Async XLA Ops:
  1.7 11.6 %collective-permute-start = (f32[333,128]{1,0:T(8,128)S(1)}, f32[333,128]{1,0:T(8,128)S(1)}, u32[]{:S(2)}, u32[]{:S(2)}) collective-permute-start(f32[333,128]{1,0:T(8,128)S(1)} %get-tuple-element.18), channel_id=1, source_target_pairs={{1,2},{3,4},{5,6},{7,8},{9,10},{11,12},{13,14},{15,16},{17,18},{19... | collective-permute-start | bytes 511496 | tf_op jit(solution)/shard_map/ppermute | solution.py:500
  7.5 5.8 %collective-permute-start.1 = (f32[333,128]{1,0:T(8,128)S(1)}, f32[333,128]{1,0:T(8,128)S(1)}, u32[]{:S(2)}, u32[]{:S(2)}) collective-permute-start(f32[333,128]{1,0:T(8,128)S(1)} %get-tuple-element.19), channel_id=1, source_target_pairs={{0,1},{2,3},{4,5},{6,7},{8,9},{10,11},{12,13},{14,15},{16,17},{18,... | collective-permute-start | bytes 511496 | tf_op jit(solution)/shard_map/ppermute | solution.py:501
  7.6 11.6 %all-to-all-start = ((f32[32,1,128]{2,1,0:T(1,128)}), f32[32,1,128]{2,1,0:T(1,128)S(1)}, u32[]{:S(2)}, u32[]{:S(2)}) async-start(f32[32,1,128]{2,1,0:T(1,128)} %bitcast.7), calls=%async_computation | async-start | bytes 32768 | tf_op jit(solution)/shard_map/all_to_all | solution.py:502

commit v8 on v7

--- a/solution.py
+++ b/solution.py
@@ -18,6 +18,7 @@
 SENT = 37
 WIDE = 32
 STEP = 33
+TALL = 16
 PAD = 8
 
 VMEM = pl.BlockSpec(memory_space=pltpu.VMEM)
@@ -51,8 +52,8 @@
 
 
 def pack_kernel(
-    sizes, state_hbm, depth_hbm, metric_hbm, partner_hbm, refine_hbm, stats_hbm, even_ref, odd_ref,
-    stats_ref, state_even, state_odd, depth_ref, metric_ref, partner_ref, refine_ref, spread, sems, sem,
+    sizes, state_hbm, depth_hbm, metric_hbm, partner_hbm, refine_hbm, stats_ref, even_ref, odd_ref,
+    state_even, state_odd, depth_ref, metric_ref, partner_ref, refine_ref, spread, sems,
 ):
     blocks, halo = sizes.blocks, sizes.halo
     wide = LANES * halo
@@ -85,8 +86,6 @@
     stats_ref[...] = jnp.where(
         lane < LANES // 2, jnp.broadcast_to(top, shape), jnp.broadcast_to(extra, shape)
     )
-    sent = pltpu.make_async_copy(stats_ref, stats_hbm, sem)
-    sent.start()
     for copy in copies[3:]:
         copy.wait()
     for ref, source, start in ((even_ref, state_even, even), (odd_ref, state_odd, odd)):
@@ -97,7 +96,6 @@
         dense += [partner_ref[at, :].astype(jnp.float32), refine_ref[at, :].astype(jnp.float32)]
         for num, value in enumerate(dense):
             ref[pl.ds(30 + num, halo, stride=SENT), :] = value
-    sent.wait()
 
 
 def pack_state(source, target, blocks, height, width):
@@ -146,23 +144,10 @@
 def tendency(load, geo, walls, index, inside, diff_ref, lift_ref):
     speed_sq, rx, ry, sx, sy = geo[:5]
     outer_sq, waves, ghosts = geo[5:8], geo[8:11], geo[11:14]
-    inflow, along_r, along_s = [None] * 10, [None] * 10, [None] * 10
-
-    def add(total, term):
-        return term if total is None else total + term
-
-    for b in range(10):
-        eta, mom_x, mom_y = [load(10 * field + b, 0) for field in range(3)]
-        flow_r = -(rx * mom_x + ry * mom_y)
-        flow_s = -(sx * mom_x + sy * mom_y)
-        for a in range(10):
-            d_r, d_s = diff_ref[a, 0, b], diff_ref[a, 1, b]
-            inflow[a] = add(inflow[a], d_r * flow_r + d_s * flow_s)
-            along_r[a] = add(along_r[a], d_r * eta)
-            along_s[a] = add(along_s[a], d_s * eta)
-    pull = (-speed_sq * rx, -speed_sq * ry)
-    push = (-speed_sq * sx, -speed_sq * sy)
-    sums = [inflow] + [[pull[k] * along_r[a] + push[k] * along_s[a] for a in range(10)] for k in range(2)]
+    own = [[load(10 * field + node, 0) for node in range(10)] for field in range(3)]
+    eta, mom_x, mom_y = own
+    flow_r = [-(rx * mom_x[b] + ry * mom_y[b]) for b in range(10)]
+    flow_s = [-(sx * mom_x[b] + sy * mom_y[b]) for b in range(10)]
     half_r = (0.5 * rx, 0.5 * ry)
     half_s = (0.5 * sx, 0.5 * sy)
     vectors = (
@@ -171,29 +156,42 @@
         (-half_r[0], -half_r[1]),
     )
     fetch = outer_values(load, index, inside)
+    jumps = ([], [], [])
     for face in range(3):
         vec_x, vec_y = vectors[face]
         theirs = FACES[(1, 0, 2)[face]]
         wall = walls[face]
         for j in range(4):
             node, match = FACES[face][j], theirs[3 - j]
-            in_eta, in_x, in_y = [load(10 * field + node, 0) for field in range(3)]
+            in_eta, in_x, in_y = eta[node], mom_x[node], mom_y[node]
             ext_eta, ext_x, ext_y = [fetch[face](10 * field + match) for field in range(3)]
             bounce = (in_x * vec_x + in_y * vec_y) * ghosts[face]
             d_eta = jnp.where(wall, 0.0, in_eta - ext_eta)
             d_x = jnp.where(wall, bounce * vec_x, in_x - ext_x)
             d_y = jnp.where(wall, bounce * vec_y, in_y - ext_y)
             head = jnp.where(wall, 0.0, speed_sq * in_eta - outer_sq[face] * ext_eta)
-            jumps = (
-                d_x * vec_x + d_y * vec_y - waves[face] * d_eta,
-                head * vec_x - waves[face] * d_x,
-                head * vec_y - waves[face] * d_y,
-            )
-            for a in range(10):
-                weight = lift_ref[a, 4 * face + j]
-                for field in range(3):
-                    sums[field][a] = sums[field][a] + weight * jumps[field]
-    return [sums[field][a] for field in range(3) for a in range(10)]
+            jumps[0].append(d_x * vec_x + d_y * vec_y - waves[face] * d_eta)
+            jumps[1].append(head * vec_x - waves[face] * d_x)
+            jumps[2].append(head * vec_y - waves[face] * d_y)
+    pull = (-speed_sq * rx, -speed_sq * ry)
+    push = (-speed_sq * sx, -speed_sq * sy)
+    out = [[None] * 10 for _ in range(3)]
+    for a in range(10):
+        total = along_r = along_s = None
+        for b in range(10):
+            d_r, d_s = diff_ref[a, 0, b], diff_ref[a, 1, b]
+            term = d_r * flow_r[b] + d_s * flow_s[b]
+            total = term if b == 0 else total + term
+            along_r = d_r * eta[b] if b == 0 else along_r + d_r * eta[b]
+            along_s = d_s * eta[b] if b == 0 else along_s + d_s * eta[b]
+        sums = [total, pull[0] * along_r + push[0] * along_s, pull[1] * along_r + push[1] * along_s]
+        for q in range(12):
+            weight = lift_ref[a, q]
+            for field in range(3):
+                sums[field] = sums[field] + weight * jumps[field][q]
+        for field in range(3):
+            out[field][a] = sums[field]
+    return [out[field][a] for field in range(3) for a in range(10)]
 
 
 def child_matrix(prolong_ref):
@@ -245,8 +243,9 @@
 
 
 def prep_kernel(
-    sizes, state_hbm, depth_hbm, metric_hbm, partner_hbm, refine_hbm, cur, aux,
-    state_ref, depth_ref, metric_ref, partner_ref, refine_ref, spread, wide, sems,
+    sizes, state_hbm, depth_hbm, metric_hbm, partner_hbm, refine_hbm, diff_hbm, lift_hbm, prolong_hbm,
+    cur, aux, weights, diff_ref, lift_ref,
+    state_ref, depth_ref, metric_ref, partner_ref, refine_ref, prolong_ref, spread, wide, sems,
 ):
     blocks = sizes.blocks
     copies = fetch_all(
@@ -256,11 +255,15 @@
             (depth_hbm, depth_ref),
             (partner_hbm, partner_ref),
             (refine_hbm, refine_ref),
+            (prolong_hbm, prolong_ref),
+            (diff_hbm, diff_ref),
+            (lift_hbm, lift_ref),
         ),
         sems,
     )
     for copy in copies:
         copy.wait()
+    weights[...] = child_matrix(prolong_ref)
     metric = split_metric(metric_ref, spread, blocks)
     dense = [depth_ref[...], *metric, partner_ref[...].astype(jnp.float32), refine_ref[...].astype(jnp.float32)]
     for num in range(7):
@@ -272,15 +275,15 @@
 
 
 def first_kernel(
-    sizes, cur_own, aux_own, odd_ref, even_ref, diff_hbm, lift_hbm, prolong_hbm,
+    sizes, cur_own, aux_own, weights_in, diff_in, lift_in, odd_ref, even_ref,
     cur, rate_ref, twice_ref, weights, ends_ref, lines_ref,
-    geo_ref, aux, diff_ref, lift_ref, prolong_ref, sems,
+    geo_ref, aux, diff_ref, lift_ref, sems,
 ):
     blocks, halo = sizes.blocks, sizes.halo
     top, bottom = PAD + halo, PAD + halo + blocks
     place = lax.axis_index(AXES)
     count = lax.axis_size(AXES)
-    copies = fetch_all(((diff_hbm, diff_ref), (lift_hbm, lift_ref), (prolong_hbm, prolong_ref)), sems)
+    copies = fetch_all(((diff_in, diff_ref), (lift_in, lift_ref)), sems)
     even = place % 2 == 0
 
     def set_halo(target, num, row):
@@ -298,25 +301,25 @@
             set_halo(cur, item, 3 * node + field)
             cur[item, top:bottom, :] = cur_own[item]
 
+    weights[...] = weights_in[...]
+    begin = PAD + sizes.keep
+    sum_children(sizes, aux[6, begin : begin + sizes.slots, :], ends_ref, lines_ref)
     for copy in copies:
         copy.wait()
-    weights[...] = child_matrix(prolong_ref)
-    begin = PAD + sizes.keep
-    sum_children(sizes, aux[6, begin : begin + sizes.slots, :], ends_ref, lines_ref)
-
-    def step(group, carry):
-        base = PAD + 8 * group
+
+    def step(start, height):
+        base = PAD + start
 
         def load_aux(item, shift):
-            return aux[item, pl.ds(base + shift, 8), :]
+            return aux[item, pl.ds(base + shift, height), :]
 
         def load(item, shift):
-            return cur[item, pl.ds(base + shift, 8), :]
+            return cur[item, pl.ds(base + shift, height), :]
 
         depth, rx, ry, sx, sy, partner = [load_aux(num, 0) for num in range(6)]
         index, inside = pair_index(partner)
         fetch = outer_values(load_aux, index, inside)
-        walls = wall_masks(sizes, 8 * group, place, count, partner)
+        walls = wall_masks(sizes, start, place, count, partner)
         speed_sq = GRAVITY * depth
         outer_sq = [jnp.where(walls[k], speed_sq, GRAVITY * fetch[k](0)) for k in range(3)]
         faces = ((sx, sy), (rx + sx, ry + sy), (rx, ry))
@@ -327,21 +330,17 @@
         ghosts = [8.0 / squares[k] for k in range(3)]
         geo = [speed_sq, rx, ry, sx, sy, *outer_sq, *waves, *ghosts]
         rates = tendency(load, geo, walls, index, inside, diff_ref, lift_ref)
-        at = pl.ds(pl.multiple_of(8 * group, 8), 8)
         for num, value in enumerate([*geo, partner]):
-            geo_ref[num, at, :] = value
+            geo_ref[num, pl.ds(start, height), :] = value
         for item in range(30):
-            rate_ref[item, pl.ds(base, 8), :] = rates[item]
-        return carry
-
-    lax.fori_loop(0, sizes.rows // 8, step, 0)
-
-    def again(group, carry):
-        row = 8 * group + sizes.keep
-        at = pl.ds(row, 8)
+            rate_ref[item, pl.ds(base, height), :] = rates[item]
+
+    def again(start, height):
+        row = start + sizes.keep
+        at = pl.ds(row, height)
 
         def load(item, shift):
-            return rate_ref[item, pl.ds(PAD + row + shift, 8), :]
+            return rate_ref[item, pl.ds(PAD + row + shift, height), :]
 
         geo = [geo_ref[num, at, :] for num in range(14)]
         partner = geo_ref[14, at, :]
@@ -349,10 +348,21 @@
         walls = wall_masks(sizes, row, place, count, partner)
         rates = tendency(load, geo, walls, index, inside, diff_ref, lift_ref)
         for item in range(30):
-            twice_ref[item, pl.ds(pl.multiple_of(8 * group, 8), 8), :] = rates[item]
-        return carry
-
-    lax.fori_loop(0, sizes.slots // 8, again, 0)
+            twice_ref[item, pl.ds(start, height), :] = rates[item]
+
+    def sweep(work, rows):
+        def body(num, carry):
+            work(pl.multiple_of(TALL * num, TALL), TALL)
+            return carry
+
+        lax.fori_loop(0, rows // TALL, body, 0)
+
+    for start in range(sizes.rows // TALL * TALL, sizes.rows, 8):
+        step(start, 8)
+    sweep(step, sizes.rows)
+    for start in range(sizes.slots // TALL * TALL, sizes.slots, 8):
+        again(start, 8)
+    sweep(again, sizes.slots)
 
 
 def refine_kernel(
@@ -483,17 +493,15 @@
     stats, even, odd = pl.pallas_call(
         functools.partial(pack_kernel, sizes),
         name="pack",
-        out_shape=(jax.ShapeDtypeStruct((count, LANES), f32), packed, packed),
+        out_shape=(pltpu.VMEM((count, LANES), f32), packed, packed),
         in_specs=[HBM] * 5,
-        out_specs=(HBM, VMEM, VMEM),
+        out_specs=(VMEM,) * 3,
         scratch_shapes=[
-            pltpu.VMEM((count, LANES), f32),
             pltpu.VMEM((10, 3, LANES * halo), f32),
             pltpu.VMEM((10, 3, LANES * halo), f32),
             *dense,
             pltpu.VMEM((8 * blocks, LANES), f32),
             pltpu.SemaphoreType.DMA((6,)),
-            pltpu.SemaphoreType.DMA,
         ],
         compiler_params=PARAMS,
     )(state, depth, metric, partner, refine)
@@ -501,25 +509,29 @@
     even = lax.ppermute(even, AXES, swaps(0, count))
     stats = lax.all_to_all(stats, AXES, 0, 0, tiled=True)
     even, odd, stats = [pltpu.with_memory_space_constraint(x, pltpu.VMEM) for x in (even, odd, stats)]
-    cur, aux = pl.pallas_call(
+    cur, aux, weights, diff_near, lift_near = pl.pallas_call(
         functools.partial(prep_kernel, sizes),
         name="lay_out",
         cost_estimate=pl.CostEstimate(flops=1 << 24, transcendentals=1 << 16, bytes_accessed=1 << 24),
         out_shape=(
             jax.ShapeDtypeStruct((30, blocks, LANES), f32),
             jax.ShapeDtypeStruct((7, blocks, LANES), f32),
+            jax.ShapeDtypeStruct((3 * PACK, 3 * WIDE), jnp.bfloat16),
+            jax.ShapeDtypeStruct(diff_ops.shape, f32),
+            jax.ShapeDtypeStruct(lift.shape, f32),
         ),
-        in_specs=[HBM] * 5,
-        out_specs=(VMEM,) * 2,
+        in_specs=[HBM] * 8,
+        out_specs=(VMEM,) * 5,
         scratch_shapes=[
             pltpu.VMEM(state.shape, f32),
             *dense,
+            pltpu.VMEM(prolong.shape, f32),
             pltpu.VMEM((8 * blocks, LANES), f32),
             pltpu.VMEM((LAID * blocks, LANES), f32),
-            pltpu.SemaphoreType.DMA((5,)),
+            pltpu.SemaphoreType.DMA((8,)),
         ],
         compiler_params=PARAMS,
-    )(state, depth, metric, partner, refine)
+    )(state, depth, metric, partner, refine, diff_ops, lift, prolong)
     cur, rates, twice, weights, ends, lines = pl.pallas_call(
         functools.partial(first_kernel, sizes),
         name="rates_twice",
@@ -532,18 +544,17 @@
             jax.ShapeDtypeStruct((2, slots, LANES), f32),
             jax.ShapeDtypeStruct((3, 8, LANES), f32),
         ),
-        in_specs=[VMEM] * 4 + [HBM] * 3,
+        in_specs=[VMEM] * 7,
         out_specs=(VMEM,) * 6,
         scratch_shapes=[
             pltpu.VMEM((15, rows, LANES), f32),
             pltpu.VMEM((7, sizes.tall, LANES), f32),
             pltpu.SMEM(diff_ops.shape, f32),
             pltpu.SMEM(lift.shape, f32),
-            pltpu.VMEM(prolong.shape, f32),
-            pltpu.SemaphoreType.DMA((3,)),
+            pltpu.SemaphoreType.DMA((2,)),
         ],
         compiler_params=PARAMS,
-    )(cur, aux, odd, even, diff_ops, lift, prolong)
+    )(cur, aux, weights, diff_near, lift_near, odd, even)
     refined = pl.pallas_call(
         functools.partial(refine_kernel, sizes),
         name="sum_and_refine",

time: 22.1 us -> 21.8 us (0.986)
  the two profiles are of different devices: /device:TPU:4 before, /device:TPU:0 now
where the time goes in v8:
time: 21.8 us; the launch traced here: 21.5 us
  Pallas kernels  11.5 us (53%)
  starting transfers between devices  9.95 us (46%)
    pallas_call x1, Pallas kernels, shards(): pl.pallas_call(functools.partial(first_kernel, sizes), name='rates_twice'...  5.27 us
    all_to_all x1, starting transfers between devices, shards(): stats = lax.all_to_all(stats, AXES, 0, 0, tiled=True)  4.84 us
    ppermute x1, starting transfers between devices, shards(): even = lax.ppermute(even, AXES, swaps(0, count))  4.44 us
    pallas_call x1, Pallas kernels, shards(): pl.pallas_call(functools.partial(refine_kernel, sizes), name='sum_and_ref...  2.5 us
    pallas_call x1, Pallas kernels, shards(): pl.pallas_call(functools.partial(prep_kernel, sizes), name='lay_out', cos...  1.88 us
    pallas_call x1, Pallas kernels, shards(): pl.pallas_call(functools.partial(pack_kernel, sizes), name='pack', out_sh...  1.83 us
    ppermute x1, starting transfers between devices, shards(): odd = lax.ppermute(odd, AXES, swaps(1, count))  0.67 us
  transfers between devices with their start and end apart: 3, of which 0 were waited for; matrix products, arithmetic and copies ran while one was open for 0% of the time, Pallas kernels for 33%

profile of v8, /device:TPU:0, one launch (start us, length us, event | category | flops | bytes accessed | tf_op | source)
XLA Modules:
  0.0 21.5 jit_solution(10203249443080889960)
XLA Ops:
  0.0 1.8 %pack.1 = (f32[32,128]{1,0:T(8,128)}, f32[333,128]{1,0:T(8,128)S(1)}, f32[333,128]{1,0:T(8,128)S(1)}) custom-call(f32[10,3,4096]{2,1,0:T(4,128)} %bitcast.12, f32[32,128]{1,0:T(8,128)} %bitcast.14, f32[4,4096]{1,0:T(4,128)} %metric_hbm.3, s32[32,128]{1,0:T(8,128)} %bitcast.16, s32[32,128]{1,0:T(8,128)} %bitcast.18), custom_call_target="tpu_custom_call" | custom-call | tf_op jit(solution)/shard_map/pack/pallas_call | solution.py:493
  1.8 0.7 %collective-permute-start = (f32[333,128]{1,0:T(8,128)S(1)}, f32[333,128]{1,0:T(8,128)S(1)}, u32[]{:S(2)}, u32[]{:S(2)}) collective-permute-start(f32[333,128]{1,0:T(8,128)S(1)} %get-tuple-element.24), channel_id=1, source_target_pairs={{1,2},{3,4},{5,6},{7,8},{9,10},{11,12},{13,14},{15,16},{17,18},{19... | collective-permute-start | bytes 511496 | tf_op jit(solution)/shard_map/ppermute | solution.py:508
  2.5 4.4 %collective-permute-start.1 = (f32[333,128]{1,0:T(8,128)S(1)}, f32[333,128]{1,0:T(8,128)S(1)}, u32[]{:S(2)}, u32[]{:S(2)}) collective-permute-start(f32[333,128]{1,0:T(8,128)S(1)} %get-tuple-element.25), channel_id=1, source_target_pairs={{0,1},{2,3},{4,5},{6,7},{8,9},{10,11},{12,13},{14,15},{16,17},{18,... | collective-permute-start | bytes 511496 | tf_op jit(solution)/shard_map/ppermute | solution.py:509
  7.0 4.8 %all-to-all-start = ((f32[32,1,128]{2,1,0:T(1,128)}), f32[32,1,128]{2,1,0:T(1,128)S(1)}, u32[]{:S(2)}, u32[]{:S(2)}) async-start(f32[32,1,128]{2,1,0:T(1,128)} %bitcast.7), calls=%async_computation | async-start | bytes 32768 | tf_op jit(solution)/shard_map/all_to_all | solution.py:510
  11.8 1.9 %lay_out.1 = (f32[30,32,128]{2,1,0:T(8,128)S(1)}, f32[7,32,128]{2,1,0:T(8,128)S(1)}, bf16[120,96]{1,0:T(8,128)(2,1)S(1)}, f32[10,2,10]{2,1,0:T(2,128)S(1)}, f32[10,12]{1,0:T(8,128)S(1)}) custom-call(f32[10,3,4096]{2,1,0:T(4,128)} %bitcast.13, f32[32,128]{1,0:T(8,128)} %bitcast.15, f32[4,4096]{1,0:T(4,128)} %metric_hbm.3, s32[32,128]{1,0:T(8,128)} %bitcast.17, ...), custom_call_target="tpu_custom_call" | custom-call | flops 16777216 | bytes 16777216 | tf_op jit(solution)/shard_map/lay_out/pallas_call | solution.py:512
  13.7 0.0 collective-permute-done.odd_ref
  13.7 0.0 collective-permute-done.1.even_ref
  13.7 5.3 %rates_twice.1 = (f32[30,72,128]{2,1,0:T(8,128)S(1)}, f32[30,72,128]{2,1,0:T(8,128)S(1)}, f32[30,48,128]{2,1,0:T(8,128)S(1)}, bf16[120,96]{1,0:T(8,128)(2,1)S(1)...) custom-call(f32[30,32,128]{2,1,0:T(8,128)S(1)} %get-tuple-element.19.cur_own, ...), custom_call_target="tpu_custom_call" | custom-call | flops 1024 | bytes 1024 | tf_op jit(solution)/shard_map/rates_twice/pallas_call | solution.py:535
  19.0 0.0 all-to-all-done
  19.0 2.5 %sum_and_refine.1 = f32[10,3,6144]{2,1,0:T(4,128)} custom-call(f32[30,72,128]{2,1,0:T(8,128)S(1)} %get-tuple-element.26.cur, f32[30,72,128]{2,1,0:T(8,128)S(1)} %get-tuple-element.27.rate_ref, f32[30,48,128]{2,1,0:T(8,128)S(1)} %get-tuple-element.28.twice_ref, bf16[120,96]{1,0:T(8,128)(2,1)S(1)} %get-tuple-element.29.weights, ...), custom_call_target="tpu_custom_call" | custom-call | tf_op jit(solution)/shard_map/sum_and_refine/pallas_call | solution.py:558
Async XLA Ops:
  1.8 11.9 %collective-permute-start = (f32[333,128]{1,0:T(8,128)S(1)}, f32[333,128]{1,0:T(8,128)S(1)}, u32[]{:S(2)}, u32[]{:S(2)}) collective-permute-start(f32[333,128]{1,0:T(8,128)S(1)} %get-tuple-element.24), channel_id=1, source_target_pairs={{1,2},{3,4},{5,6},{7,8},{9,10},{11,12},{13,14},{15,16},{17,18},{19... | collective-permute-start | bytes 511496 | tf_op jit(solution)/shard_map/ppermute | solution.py:508
  2.5 11.2 %collective-permute-start.1 = (f32[333,128]{1,0:T(8,128)S(1)}, f32[333,128]{1,0:T(8,128)S(1)}, u32[]{:S(2)}, u32[]{:S(2)}) collective-permute-start(f32[333,128]{1,0:T(8,128)S(1)} %get-tuple-element.25), channel_id=1, source_target_pairs={{0,1},{2,3},{4,5},{6,7},{8,9},{10,11},{12,13},{14,15},{16,17},{18,... | collective-permute-start | bytes 511496 | tf_op jit(solution)/shard_map/ppermute | solution.py:509
  7.0 12.0 %all-to-all-start = ((f32[32,1,128]{2,1,0:T(1,128)}), f32[32,1,128]{2,1,0:T(1,128)S(1)}, u32[]{:S(2)}, u32[]{:S(2)}) async-start(f32[32,1,128]{2,1,0:T(1,128)} %bitcast.7), calls=%async_computation | async-start | bytes 32768 | tf_op jit(solution)/shard_map/all_to_all | solution.py:510

commit v9 on v8

--- a/solution.py
+++ b/solution.py
@@ -52,8 +52,8 @@
 
 
 def pack_kernel(
-    sizes, state_hbm, depth_hbm, metric_hbm, partner_hbm, refine_hbm, stats_ref, even_ref, odd_ref,
-    state_even, state_odd, depth_ref, metric_ref, partner_ref, refine_ref, spread, sems,
+    sizes, state_hbm, depth_hbm, metric_hbm, partner_hbm, refine_hbm, stats_hbm, even_ref, odd_ref,
+    stats_ref, state_even, state_odd, depth_ref, metric_ref, partner_ref, refine_ref, spread, sems, sem,
 ):
     blocks, halo = sizes.blocks, sizes.halo
     wide = LANES * halo
@@ -86,6 +86,8 @@
     stats_ref[...] = jnp.where(
         lane < LANES // 2, jnp.broadcast_to(top, shape), jnp.broadcast_to(extra, shape)
     )
+    sent = pltpu.make_async_copy(stats_ref, stats_hbm, sem)
+    sent.start()
     for copy in copies[3:]:
         copy.wait()
     for ref, source, start in ((even_ref, state_even, even), (odd_ref, state_odd, odd)):
@@ -96,6 +98,7 @@
         dense += [partner_ref[at, :].astype(jnp.float32), refine_ref[at, :].astype(jnp.float32)]
         for num, value in enumerate(dense):
             ref[pl.ds(30 + num, halo, stride=SENT), :] = value
+    sent.wait()
 
 
 def pack_state(source, target, blocks, height, width):
@@ -195,24 +198,30 @@
 
 
 def child_matrix(prolong_ref):
-    f32 = jnp.float32
-    node_r = lax.broadcasted_iota(jnp.int32, (PACK, 10), 0) // 4
-    spread_r = (node_r == lax.broadcasted_iota(jnp.int32, (PACK, 10), 1)).astype(f32)
-    item_c = lax.broadcasted_iota(jnp.int32, (10, WIDE), 1)
-    spread_c = (item_c % 10 == lax.broadcasted_iota(jnp.int32, (10, WIDE), 0)).astype(f32)
-    row = lax.broadcasted_iota(jnp.int32, (PACK, WIDE), 0)
-    col = lax.broadcasted_iota(jnp.int32, (PACK, WIDE), 1)
-    same = row % 4 == col // 10
+    f32, bf16 = jnp.float32, jnp.bfloat16
+
+    def number(shape, axis):
+        return lax.broadcasted_iota(jnp.int32, shape, axis)
+
+    both = jnp.concatenate([prolong_ref[:, 0, :], prolong_ref[:, 1, :]], axis=0)
+    rounded = both.astype(bf16)
+    rest = (both - rounded.astype(f32)).astype(bf16)
+    shape = (10, WIDE)
+    columns = (number(shape, 1) % 10 == number(shape, 0)).astype(bf16)
+    shape = (2 * PACK, 20)
+    rows = (number(shape, 0) // 4 == number(shape, 1)).astype(bf16)
+    shape = (2 * PACK, WIDE)
+    same = number(shape, 0) % 4 == number(shape, 1) // 10
     parts = []
-    for child in range(2):
-        left = jnp.dot(spread_r, prolong_ref[:, child, :], precision=HIGH, preferred_element_type=f32)
-        full = jnp.dot(left, spread_c, precision=HIGH, preferred_element_type=f32)
+    for matrix in (rounded, rest):
+        spread = jnp.dot(matrix, columns, preferred_element_type=f32).astype(bf16)
+        full = jnp.dot(rows, spread, preferred_element_type=f32)
         parts.append(jnp.where(same, full, 0.0))
-    parts.append((same & (row // 4 == col % 10)).astype(f32))
-    whole = jnp.concatenate(parts, axis=0)
-    rounded = whole.astype(jnp.bfloat16)
-    rest = (whole - rounded.astype(f32)).astype(jnp.bfloat16)
-    return jnp.concatenate([rounded, rounded, rest], axis=1)
+    shape = (PACK, WIDE)
+    same = (number(shape, 0) % 4 == number(shape, 1) // 10) & (number(shape, 0) // 4 == number(shape, 1) % 10)
+    first = jnp.concatenate([parts[0], same.astype(f32)], axis=0)
+    last = jnp.concatenate([parts[1], jnp.zeros(shape, f32)], axis=0)
+    return jnp.concatenate([first, first, last], axis=1).astype(bf16)
 
 
 def sum_children(sizes, refine, ends_ref, lines_ref):
@@ -493,15 +502,17 @@
     stats, even, odd = pl.pallas_call(
         functools.partial(pack_kernel, sizes),
         name="pack",
-        out_shape=(pltpu.VMEM((count, LANES), f32), packed, packed),
+        out_shape=(jax.ShapeDtypeStruct((count, LANES), f32), packed, packed),
         in_specs=[HBM] * 5,
-        out_specs=(VMEM,) * 3,
+        out_specs=(HBM, VMEM, VMEM),
         scratch_shapes=[
+            pltpu.VMEM((count, LANES), f32),
             pltpu.VMEM((10, 3, LANES * halo), f32),
             pltpu.VMEM((10, 3, LANES * halo), f32),
             *dense,
             pltpu.VMEM((8 * blocks, LANES), f32),
             pltpu.SemaphoreType.DMA((6,)),
+            pltpu.SemaphoreType.DMA,
         ],
         compiler_params=PARAMS,
     )(state, depth, metric, partner, refine)

time: 21.8 us -> 21.5 us (0.986)
  Pallas kernels: 11.5 us -> 11.1 us
where the time goes in v9:
time: 21.5 us; the launch traced here: 21.2 us
  Pallas kernels  11.1 us (52%)
  starting transfers between devices  9.95 us (46%)
    pallas_call x1, Pallas kernels, shards(): pl.pallas_call(functools.partial(first_kernel, sizes), name='rates_twice'...  5.27 us
    all_to_all x1, starting transfers between devices, shards(): stats = lax.all_to_all(stats, AXES, 0, 0, tiled=True)  4.84 us
    ppermute x1, starting transfers between devices, shards(): even = lax.ppermute(even, AXES, swaps(0, count))  4.44 us
    pallas_call x1, Pallas kernels, shards(): pl.pallas_call(functools.partial(refine_kernel, sizes), name='sum_and_ref...  2.5 us
    pallas_call x1, Pallas kernels, shards(): pl.pallas_call(functools.partial(prep_kernel, sizes), name='lay_out', cos...  1.73 us
    pallas_call x1, Pallas kernels, shards(): pl.pallas_call(functools.partial(pack_kernel, sizes), name='pack', out_sh...  1.65 us
    ppermute x1, starting transfers between devices, shards(): odd = lax.ppermute(odd, AXES, swaps(1, count))  0.67 us
  transfers between devices with their start and end apart: 3, of which 0 were waited for; matrix products, arithmetic and copies ran while one was open for 0% of the time, Pallas kernels for 33%

profile of v9, /device:TPU:0, one launch (start us, length us, event | category | flops | bytes accessed | tf_op | source)
XLA Modules:
  0.0 21.2 jit_solution(16380213525551552473)
XLA Ops:
  0.0 1.7 %pack.1 = (f32[32,128]{1,0:T(8,128)}, f32[333,128]{1,0:T(8,128)S(1)}, f32[333,128]{1,0:T(8,128)S(1)}) custom-call(f32[10,3,4096]{2,1,0:T(4,128)} %bitcast.12, f32[32,128]{1,0:T(8,128)} %bitcast.14, f32[4,4096]{1,0:T(4,128)} %metric_hbm.3, s32[32,128]{1,0:T(8,128)} %bitcast.16, s32[32,128]{1,0:T(8,128)} %bitcast.18), custom_call_target="tpu_custom_call" | custom-call | tf_op jit(solution)/shard_map/pack/pallas_call | solution.py:502
  1.7 0.7 %collective-permute-start = (f32[333,128]{1,0:T(8,128)S(1)}, f32[333,128]{1,0:T(8,128)S(1)}, u32[]{:S(2)}, u32[]{:S(2)}) collective-permute-start(f32[333,128]{1,0:T(8,128)S(1)} %get-tuple-element.24), channel_id=1, source_target_pairs={{1,2},{3,4},{5,6},{7,8},{9,10},{11,12},{13,14},{15,16},{17,18},{19... | collective-permute-start | bytes 511496 | tf_op jit(solution)/shard_map/ppermute | solution.py:519
  2.3 4.4 %collective-permute-start.1 = (f32[333,128]{1,0:T(8,128)S(1)}, f32[333,128]{1,0:T(8,128)S(1)}, u32[]{:S(2)}, u32[]{:S(2)}) collective-permute-start(f32[333,128]{1,0:T(8,128)S(1)} %get-tuple-element.25), channel_id=1, source_target_pairs={{0,1},{2,3},{4,5},{6,7},{8,9},{10,11},{12,13},{14,15},{16,17},{18,... | collective-permute-start | bytes 511496 | tf_op jit(solution)/shard_map/ppermute | solution.py:520
  6.8 4.8 %all-to-all-start = ((f32[32,1,128]{2,1,0:T(1,128)}), f32[32,1,128]{2,1,0:T(1,128)S(1)}, u32[]{:S(2)}, u32[]{:S(2)}) async-start(f32[32,1,128]{2,1,0:T(1,128)} %bitcast.7), calls=%async_computation | async-start | bytes 32768 | tf_op jit(solution)/shard_map/all_to_all | solution.py:521
  11.6 1.7 %lay_out.1 = (f32[30,32,128]{2,1,0:T(8,128)S(1)}, f32[7,32,128]{2,1,0:T(8,128)S(1)}, bf16[120,96]{1,0:T(8,128)(2,1)S(1)}, f32[10,2,10]{2,1,0:T(2,128)S(1)}, f32[10,12]{1,0:T(8,128)S(1)}) custom-call(f32[10,3,4096]{2,1,0:T(4,128)} %bitcast.13, f32[32,128]{1,0:T(8,128)} %bitcast.15, f32[4,4096]{1,0:T(4,128)} %metric_hbm.3, s32[32,128]{1,0:T(8,128)} %bitcast.17, ...), custom_call_target="tpu_custom_call" | custom-call | flops 16777216 | bytes 16777216 | tf_op jit(solution)/shard_map/lay_out/pallas_call | solution.py:523
  13.4 0.0 collective-permute-done.odd_ref
  13.4 0.0 collective-permute-done.1.even_ref
  13.4 5.3 %rates_twice.1 = (f32[30,72,128]{2,1,0:T(8,128)S(1)}, f32[30,72,128]{2,1,0:T(8,128)S(1)}, f32[30,48,128]{2,1,0:T(8,128)S(1)}, bf16[120,96]{1,0:T(8,128)(2,1)S(1)...) custom-call(f32[30,32,128]{2,1,0:T(8,128)S(1)} %get-tuple-element.19.cur_own, ...), custom_call_target="tpu_custom_call" | custom-call | flops 1024 | bytes 1024 | tf_op jit(solution)/shard_map/rates_twice/pallas_call | solution.py:546
  18.7 0.0 all-to-all-done
  18.7 2.5 %sum_and_refine.1 = f32[10,3,6144]{2,1,0:T(4,128)} custom-call(f32[30,72,128]{2,1,0:T(8,128)S(1)} %get-tuple-element.26.cur, f32[30,72,128]{2,1,0:T(8,128)S(1)} %get-tuple-element.27.rate_ref, f32[30,48,128]{2,1,0:T(8,128)S(1)} %get-tuple-element.28.twice_ref, bf16[120,96]{1,0:T(8,128)(2,1)S(1)} %get-tuple-element.29.weights, ...), custom_call_target="tpu_custom_call" | custom-call | tf_op jit(solution)/shard_map/sum_and_refine/pallas_call | solution.py:569
Async XLA Ops:
  1.7 11.7 %collective-permute-start = (f32[333,128]{1,0:T(8,128)S(1)}, f32[333,128]{1,0:T(8,128)S(1)}, u32[]{:S(2)}, u32[]{:S(2)}) collective-permute-start(f32[333,128]{1,0:T(8,128)S(1)} %get-tuple-element.24), channel_id=1, source_target_pairs={{1,2},{3,4},{5,6},{7,8},{9,10},{11,12},{13,14},{15,16},{17,18},{19... | collective-permute-start | bytes 511496 | tf_op jit(solution)/shard_map/ppermute | solution.py:519
  2.3 11.0 %collective-permute-start.1 = (f32[333,128]{1,0:T(8,128)S(1)}, f32[333,128]{1,0:T(8,128)S(1)}, u32[]{:S(2)}, u32[]{:S(2)}) collective-permute-start(f32[333,128]{1,0:T(8,128)S(1)} %get-tuple-element.25), channel_id=1, source_target_pairs={{0,1},{2,3},{4,5},{6,7},{8,9},{10,11},{12,13},{14,15},{16,17},{18,... | collective-permute-start | bytes 511496 | tf_op jit(solution)/shard_map/ppermute | solution.py:520
  6.8 11.9 %all-to-all-start = ((f32[32,1,128]{2,1,0:T(1,128)}), f32[32,1,128]{2,1,0:T(1,128)S(1)}, u32[]{:S(2)}, u32[]{:S(2)}) async-start(f32[32,1,128]{2,1,0:T(1,128)} %bitcast.7), calls=%async_computation | async-start | bytes 32768 | tf_op jit(solution)/shard_map/all_to_all | solution.py:521

commit v10 on v9

--- a/solution.py
+++ b/solution.py
@@ -35,6 +35,7 @@
         self.rows = -(-(self.blocks + 2 * self.halo) // 8) * 8
         self.tall = self.rows + 2 * PAD
         self.slots = 3 * self.blocks // 2
+        self.children = self.slots + 2 * self.margin
         self.keep = self.halo - self.margin
 
 
@@ -224,31 +225,54 @@
     return jnp.concatenate([first, first, last], axis=1).astype(bf16)
 
 
-def sum_children(sizes, refine, ends_ref, lines_ref):
-    slots, f32 = sizes.slots, jnp.float32
-    counts = (1.0 + refine).astype(jnp.bfloat16)
+def find_parents(sizes, refine, code_ref, parent_ref):
+    slots, margin, f32, bf16 = sizes.slots, sizes.margin, jnp.float32, jnp.bfloat16
+    counts = (1.0 + refine).astype(bf16)
     row_i = lax.broadcasted_iota(jnp.int32, (LANES, LANES), 0)
     col_i = lax.broadcasted_iota(jnp.int32, (LANES, LANES), 1)
-    upper = (row_i <= col_i).astype(jnp.bfloat16)
-    within = jnp.dot(counts, upper, preferred_element_type=f32)
-    whole = jnp.dot(counts, jnp.ones((LANES, LANES), jnp.bfloat16), preferred_element_type=f32)
+    within = jnp.dot(counts, (row_i <= col_i).astype(bf16), preferred_element_type=f32)
+    whole = jnp.dot(counts, jnp.ones((LANES, LANES), bf16), preferred_element_type=f32)
     row_s = lax.broadcasted_iota(jnp.int32, (slots, slots), 0)
     col_s = lax.broadcasted_iota(jnp.int32, (slots, slots), 1)
-    lower = (col_s < row_s).astype(jnp.bfloat16)
-    before = jnp.dot(lower, whole.astype(jnp.bfloat16), preferred_element_type=f32)
-    before = before - before[sizes.margin : sizes.margin + 1, :]
-    ends_ref[0] = 2.0 * (within + before) + refine
-    ends_ref[1] = before + whole
-    ones = jnp.ones((8, LANES), jnp.bfloat16)
-    sums = lax.dot_general(ones, counts, (((1,), (1,)), ((), ())), preferred_element_type=f32)
+    before = jnp.dot((col_s < row_s).astype(bf16), whole.astype(bf16), preferred_element_type=f32)
+    ends = 2.0 * (within + before - before[margin : margin + 1, :]) + refine
+    sums = lax.dot_general(
+        jnp.ones((8, LANES), bf16), counts, (((1,), (1,)), ((), ())), preferred_element_type=f32
+    ).astype(bf16)
     gap = lax.broadcasted_iota(jnp.int32, (slots, LANES), 1) - lax.broadcasted_iota(jnp.int32, (slots, LANES), 0)
-    lines = [
-        jnp.dot(sums.astype(jnp.bfloat16), (gap >= least).astype(jnp.bfloat16), preferred_element_type=f32)
-        for least in (2, 1, 0)
+    lines = [jnp.dot(sums, (gap >= least).astype(bf16), preferred_element_type=f32)[0:1] for least in (2, 1, 0)]
+    own = lines[1][:, margin : margin + 1]
+    shape = (sizes.children, LANES)
+    lane = lax.broadcasted_iota(jnp.int32, shape, 1)
+    row_start = LANES * (lax.broadcasted_iota(jnp.int32, shape, 0) - margin)
+    begun = [line - own <= row_start.astype(f32) for line in lines]
+    high = jnp.floor(ends * (1.0 / 256.0))
+    rows = lax.broadcasted_iota(jnp.int32, (slots, LANES), 0).astype(f32)
+    stack = jnp.concatenate([high, ends - 256.0 * high, rows], axis=1).astype(bf16)
+    found_rows = [
+        jnp.dot((begun[k] & ~begun[k + 1]).astype(bf16)[:, :slots], stack, preferred_element_type=f32)
+        for k in (1, 0)
     ]
-    own = lines[1][:, sizes.margin : sizes.margin + 1]
-    for num in range(3):
-        lines_ref[num] = lines[num] - own
+    near, far = [256.0 * x[:, :LANES] + x[:, LANES : 2 * LANES] for x in found_rows]
+    child = row_start + lane
+    goal = (2 * child + 1).astype(f32)
+    beyond = jnp.broadcast_to(near[:, LANES - 1 :], shape) <= goal
+
+    def pick(index):
+        return jnp.where(beyond, lane_gather(far, index), lane_gather(near, index))
+
+    found = jnp.zeros(shape, jnp.int32)
+    size = LANES // 2
+    while size:
+        passed = pick(found + (size - 1)) <= goal
+        found = jnp.where(passed, found + size, found)
+        size //= 2
+    mine = pick(found).astype(jnp.int32)
+    split = mine & 1
+    begin = (mine >> 1) - 1 - split
+    code_ref[: sizes.children, :] = (found + LANES * split * (1 + child - begin)).astype(f32)
+    code_ref[sizes.children :, :] = jnp.zeros((8, LANES), f32)
+    parent_ref[...] = found_rows[0][:, 2 * LANES :].astype(jnp.int32) + beyond.astype(jnp.int32)
 
 
 def prep_kernel(
@@ -285,7 +309,7 @@
 
 def first_kernel(
     sizes, cur_own, aux_own, weights_in, diff_in, lift_in, odd_ref, even_ref,
-    cur, rate_ref, twice_ref, weights, ends_ref, lines_ref,
+    cur, rate_ref, twice_ref, weights, code_ref, parent_ref,
     geo_ref, aux, diff_ref, lift_ref, sems,
 ):
     blocks, halo = sizes.blocks, sizes.halo
@@ -312,9 +336,9 @@
 
     weights[...] = weights_in[...]
     begin = PAD + sizes.keep
-    sum_children(sizes, aux[6, begin : begin + sizes.slots, :], ends_ref, lines_ref)
     for copy in copies:
         copy.wait()
+    find_parents(sizes, aux[6, begin : begin + sizes.slots, :], code_ref, parent_ref)
 
     def step(start, height):
         base = PAD + start
@@ -375,68 +399,42 @@
 
 
 def refine_kernel(
-    sizes, cur, rate_ref, twice_ref, weights, base_ref, lines_ref, stats_ref, out_hbm,
-    out_ref, place_v, place_s, wide, index_ref, out_sems, sem,
+    sizes, cur, rate_ref, twice_ref, weights, code_ref, parent_ref, stats_ref, out_hbm,
+    out_ref, parents, wide, index_ref, out_sems, sem,
 ):
-    slots, keep = sizes.slots, sizes.keep
+    slots, keep, margin = sizes.slots, sizes.keep, LANES * sizes.margin
     place = lax.axis_index(AXES)
+    copy = pltpu.make_async_copy(parent_ref, parents, sem)
+    copy.start()
     stats = stats_ref[...]
     half = LANES // 2
     row_n = lax.broadcasted_iota(jnp.int32, stats.shape, 0)
+    lane_n = lax.broadcasted_iota(jnp.int32, stats.shape, 1)
     top = jnp.max(stats, axis=0, keepdims=True)
-    earlier = jnp.sum(jnp.where(row_n < place, stats, 0.0), axis=0, keepdims=True)
     left = lax.broadcasted_iota(jnp.int32, (1, LANES), 1) < half
-    top = jnp.where(left, top, pltpu.roll(top, half, 1))
-    earlier = jnp.where(left, pltpu.roll(earlier, half, 1), earlier)
-    step = COURANT / top
+    step = COURANT / jnp.where(left, top, pltpu.roll(top, half, 1))
     half_square = 0.5 * step * step
-    start = earlier - (place * (sizes.cells // 2)).astype(jnp.float32)
-    first_slot = LANES * lax.broadcasted_iota(jnp.int32, (slots, LANES), 1).astype(jnp.float32)
-    lead = jnp.sum((base_ref[1] + start <= first_slot).astype(jnp.float32), axis=0, keepdims=True)
-    lead = jnp.clip(lead.astype(jnp.int32), 0, slots - 1)
-    place_v[...] = jnp.broadcast_to(lead, (8, LANES))
-    copy = pltpu.make_async_copy(place_v, place_s, sem)
-    copy.start()
+    earlier = jnp.sum(jnp.where((row_n < place) & (lane_n == LANES - 1), stats, 0.0))
+    shift = margin - (earlier.astype(jnp.int32) - place * (sizes.cells // 2))
+    shift = jnp.clip(shift, 0, 2 * margin)
+    row_shift, lane_shift = shift // LANES, shift % LANES
+    lane = lax.broadcasted_iota(jnp.int32, (slots, LANES), 1)
+    code = jnp.where(
+        lane < lane_shift, code_ref[pl.ds(row_shift + 1, slots), :], code_ref[pl.ds(row_shift, slots), :]
+    )
+    code = pltpu.roll(code, (LANES - lane_shift) % LANES, 1).astype(jnp.int32)
+    found = code & (LANES - 1)
+    index_ref[0] = found
+    index_ref[1] = code >> 7
+    index_ref[2] = jnp.broadcast_to(found[:, 0:1], (slots, LANES))
     for item in range(30):
         now = slice(PAD + keep, PAD + keep + slots)
         value = cur[item, now, :] + step * rate_ref[item, now, :] + half_square * twice_ref[item]
         wide[pl.ds(item, slots, stride=STEP), :] = value
     for item in (30, 31):
         wide[pl.ds(item, slots + 1, stride=STEP), :] = jnp.zeros((slots + 1, LANES), jnp.float32)
-    slot_start = LANES * lax.broadcasted_iota(jnp.int32, (slots, LANES), 0).astype(jnp.float32)
-    begun = [lines_ref[num, 0:1, :] + start <= slot_start for num in range(3)]
-    near, far = [
-        2.0 * start
-        + jnp.dot(
-            (begun[num] & ~begun[num + 1]).astype(jnp.float32)[:, :slots],
-            base_ref[0],
-            precision=HIGH,
-            preferred_element_type=jnp.float32,
-        )
-        for num in (1, 0)
-    ]
-    lane = lax.broadcasted_iota(jnp.int32, (slots, LANES), 1)
-    slot_no = LANES * lax.broadcasted_iota(jnp.int32, (slots, LANES), 0) + lane
-    goal = (2 * slot_no + 1).astype(jnp.float32)
-    beyond = jnp.broadcast_to(near[:, LANES - 1 :], (slots, LANES)) <= goal
-
-    def pick(index):
-        return jnp.where(beyond, lane_gather(far, index), lane_gather(near, index))
-
-    found = jnp.zeros((slots, LANES), jnp.int32)
-    size = LANES // 2
-    while size:
-        passed = pick(found + (size - 1)) <= goal
-        found = jnp.where(passed, found + size, found)
-        size //= 2
-    mine = pick(found).astype(jnp.int32)
-    split = mine & 1
-    begin = (mine >> 1) - 1 - split
-    kind = split * (1 + slot_no - begin)
-    index_ref[0] = found.astype(jnp.float32)
-    index_ref[1] = kind.astype(jnp.float32)
-    index_ref[2] = (lane < jnp.broadcast_to(found[:, 0:1], (slots, LANES))).astype(jnp.float32)
     copy.wait()
+    lane8 = lax.broadcasted_iota(jnp.int32, (8, LANES), 1)
     matrix = weights[...]
     chunk = 8 * LANES
     results = []
@@ -444,9 +442,9 @@
         span = slice(chunk * part, chunk * (part + 1))
         columns = []
         for slot in range(8 * part, 8 * part + 8):
-            lead_at = place_s[0, slot] * STEP
-            lane_idx = jnp.broadcast_to(index_ref[0, slot : slot + 1, :], (8, LANES)).astype(jnp.int32)
-            ahead = jnp.broadcast_to(index_ref[2, slot : slot + 1, :], (8, LANES)) > 0.5
+            lead_at = jnp.clip(parents[slot + row_shift, lane_shift], 0, slots - 1) * STEP
+            lane_idx = jnp.broadcast_to(index_ref[0, slot : slot + 1, :], (8, LANES))
+            ahead = lane8 < jnp.broadcast_to(index_ref[2, slot : slot + 1, :], (8, LANES))
             tiles = []
             for row in range(0, WIDE, 8):
                 one = wide[pl.ds(lead_at + row, 8), :]
@@ -463,9 +461,9 @@
             cut = slice(LANES * sub, LANES * (sub + 1))
             tag = jnp.broadcast_to(index_ref[1, slot : slot + 1, :], (PACK, LANES))
             value = jnp.where(
-                tag < 0.5,
+                tag == 0,
                 children[2 * PACK :, cut],
-                jnp.where(tag < 1.5, children[:PACK, cut], children[PACK : 2 * PACK, cut]),
+                jnp.where(tag == 1, children[:PACK, cut], children[PACK : 2 * PACK, cut]),
             )
             for node in range(10):
                 out_ref[node, :, LANES * slot : LANES * (slot + 1)] = value[4 * node : 4 * node + 3]
@@ -543,7 +541,7 @@
         ],
         compiler_params=PARAMS,
     )(state, depth, metric, partner, refine, diff_ops, lift, prolong)
-    cur, rates, twice, weights, ends, lines = pl.pallas_call(
+    cur, rates, twice, weights, codes, parents = pl.pallas_call(
         functools.partial(first_kernel, sizes),
         name="rates_twice",
         cost_estimate=pl.CostEstimate(flops=1024, transcendentals=0, bytes_accessed=1024),
@@ -552,8 +550,8 @@
             jax.ShapeDtypeStruct((30, sizes.tall, LANES), f32),
             jax.ShapeDtypeStruct((30, slots, LANES), f32),
             jax.ShapeDtypeStruct((3 * PACK, 3 * WIDE), jnp.bfloat16),
-            jax.ShapeDtypeStruct((2, slots, LANES), f32),
-            jax.ShapeDtypeStruct((3, 8, LANES), f32),
+            jax.ShapeDtypeStruct((sizes.children + 8, LANES), f32),
+            jax.ShapeDtypeStruct((sizes.children, LANES), i32),
         ),
         in_specs=[VMEM] * 7,
         out_specs=(VMEM,) * 6,
@@ -574,15 +572,14 @@
         out_specs=HBM,
         scratch_shapes=[
             pltpu.VMEM((10, 3, LANES * slots), f32),
-            pltpu.VMEM((8, LANES), i32),
-            pltpu.SMEM((8, LANES), i32),
+            pltpu.SMEM((sizes.children, LANES), i32),
             pltpu.VMEM((STEP * (slots + 1), LANES), f32),
-            pltpu.VMEM((3, slots, LANES), f32),
+            pltpu.VMEM((3, slots, LANES), i32),
             pltpu.SemaphoreType.DMA((slots // 8,)),
             pltpu.SemaphoreType.DMA,
         ],
         compiler_params=PARAMS,
-    )(cur, rates, twice, weights, ends, lines, stats)
+    )(cur, rates, twice, weights, codes, parents, stats)
     return jnp.transpose(refined, (1, 0, 2))
 
 

time: 21.5 us -> 22.6 us (1.051)
  Pallas kernels: 11.1 us -> 12.3 us
    pallas_call x1, Pallas kernels: 5.27 us -> 6.22 us  [shards(): pl.pallas_call(functools.partial(first_kernel, sizes), name='rates_twice'...]
    pallas_call x1, Pallas kernels: 2.5 us -> 2.73 us  [shards(): pl.pallas_call(functools.partial(refine_kernel, sizes), name='sum_and_ref...]
  transfers between devices with their start and end apart: 3 -> 3, of which waited for: 0 -> 0; matrix products, arithmetic and copies ran while one was open for 0% -> 0% of each run, Pallas kernels for 33% -> 35%
where the time goes in v10:
time: 22.6 us; the launch traced here: 22.4 us
  Pallas kernels  12.3 us (54%)
  starting transfers between devices  9.95 us (44%)
    pallas_call x1, Pallas kernels, shards(): pl.pallas_call(functools.partial(first_kernel, sizes), name='rates_twice'...  6.22 us
    all_to_all x1, starting transfers between devices, shards(): stats = lax.all_to_all(stats, AXES, 0, 0, tiled=True)  4.84 us
    ppermute x1, starting transfers between devices, shards(): even = lax.ppermute(even, AXES, swaps(0, count))  4.44 us
    pallas_call x1, Pallas kernels, shards(): pl.pallas_call(functools.partial(refine_kernel, sizes), name='sum_and_ref...  2.73 us
    pallas_call x1, Pallas kernels, shards(): pl.pallas_call(functools.partial(prep_kernel, sizes), name='lay_out', cos...  1.73 us
    pallas_call x1, Pallas kernels, shards(): pl.pallas_call(functools.partial(pack_kernel, sizes), name='pack', out_sh...  1.65 us
    ppermute x1, starting transfers between devices, shards(): odd = lax.ppermute(odd, AXES, swaps(1, count))  0.67 us
  transfers between devices with their start and end apart: 3, of which 0 were waited for; matrix products, arithmetic and copies ran while one was open for 0% of the time, Pallas kernels for 35%

profile of v10, /device:TPU:0, one launch (start us, length us, event | category | flops | bytes accessed | tf_op | source)
XLA Modules:
  0.0 22.4 jit_solution(9421534189283414145)
XLA Ops:
  0.0 1.7 %pack.1 = (f32[32,128]{1,0:T(8,128)}, f32[333,128]{1,0:T(8,128)S(1)}, f32[333,128]{1,0:T(8,128)S(1)}) custom-call(f32[10,3,4096]{2,1,0:T(4,128)} %bitcast.12, f32[32,128]{1,0:T(8,128)} %bitcast.14, f32[4,4096]{1,0:T(4,128)} %metric_hbm.3, s32[32,128]{1,0:T(8,128)} %bitcast.16, s32[32,128]{1,0:T(8,128)} %bitcast.18), custom_call_target="tpu_custom_call" | custom-call | tf_op jit(solution)/shard_map/pack/pallas_call | solution.py:500
  1.7 0.7 %collective-permute-start = (f32[333,128]{1,0:T(8,128)S(1)}, f32[333,128]{1,0:T(8,128)S(1)}, u32[]{:S(2)}, u32[]{:S(2)}) collective-permute-start(f32[333,128]{1,0:T(8,128)S(1)} %get-tuple-element.24), channel_id=1, source_target_pairs={{1,2},{3,4},{5,6},{7,8},{9,10},{11,12},{13,14},{15,16},{17,18},{19... | collective-permute-start | bytes 511496 | tf_op jit(solution)/shard_map/ppermute | solution.py:517
  2.3 4.4 %collective-permute-start.1 = (f32[333,128]{1,0:T(8,128)S(1)}, f32[333,128]{1,0:T(8,128)S(1)}, u32[]{:S(2)}, u32[]{:S(2)}) collective-permute-start(f32[333,128]{1,0:T(8,128)S(1)} %get-tuple-element.25), channel_id=1, source_target_pairs={{0,1},{2,3},{4,5},{6,7},{8,9},{10,11},{12,13},{14,15},{16,17},{18,... | collective-permute-start | bytes 511496 | tf_op jit(solution)/shard_map/ppermute | solution.py:518
  6.8 4.8 %all-to-all-start = ((f32[32,1,128]{2,1,0:T(1,128)}), f32[32,1,128]{2,1,0:T(1,128)S(1)}, u32[]{:S(2)}, u32[]{:S(2)}) async-start(f32[32,1,128]{2,1,0:T(1,128)} %bitcast.7), calls=%async_computation | async-start | bytes 32768 | tf_op jit(solution)/shard_map/all_to_all | solution.py:519
  11.6 1.7 %lay_out.1 = (f32[30,32,128]{2,1,0:T(8,128)S(1)}, f32[7,32,128]{2,1,0:T(8,128)S(1)}, bf16[120,96]{1,0:T(8,128)(2,1)S(1)}, f32[10,2,10]{2,1,0:T(2,128)S(1)}, f32[10,12]{1,0:T(8,128)S(1)}) custom-call(f32[10,3,4096]{2,1,0:T(4,128)} %bitcast.13, f32[32,128]{1,0:T(8,128)} %bitcast.15, f32[4,4096]{1,0:T(4,128)} %metric_hbm.3, s32[32,128]{1,0:T(8,128)} %bitcast.17, ...), custom_call_target="tpu_custom_call" | custom-call | flops 16777216 | bytes 16777216 | tf_op jit(solution)/shard_map/lay_out/pallas_call | solution.py:521
  13.4 0.0 collective-permute-done.odd_ref
  13.4 0.0 collective-permute-done.1.even_ref
  13.4 6.2 %rates_twice.1 = (f32[30,72,128]{2,1,0:T(8,128)S(1)}, f32[30,72,128]{2,1,0:T(8,128)S(1)}, f32[30,48,128]{2,1,0:T(8,128)S(1)}, bf16[120,96]{1,0:T(8,128)(2,1)S(1)...) custom-call(f32[30,32,128]{2,1,0:T(8,128)S(1)} %get-tuple-element.19.cur_own, ...), custom_call_target="tpu_custom_call" | custom-call | flops 1024 | bytes 1024 | tf_op jit(solution)/shard_map/rates_twice/pallas_call | solution.py:544
  19.6 0.0 all-to-all-done
  19.6 2.7 %sum_and_refine.1 = f32[10,3,6144]{2,1,0:T(4,128)} custom-call(f32[30,72,128]{2,1,0:T(8,128)S(1)} %get-tuple-element.26.cur, f32[30,72,128]{2,1,0:T(8,128)S(1)} %get-tuple-element.27.rate_ref, f32[30,48,128]{2,1,0:T(8,128)S(1)} %get-tuple-element.28.twice_ref, bf16[120,96]{1,0:T(8,128)(2,1)S(1)} %get-tuple-element.29.weights, ...), custom_call_target="tpu_custom_call" | custom-call | tf_op jit(solution)/shard_map/sum_and_refine/pallas_call | solution.py:567
Async XLA Ops:
  1.7 11.7 %collective-permute-start = (f32[333,128]{1,0:T(8,128)S(1)}, f32[333,128]{1,0:T(8,128)S(1)}, u32[]{:S(2)}, u32[]{:S(2)}) collective-permute-start(f32[333,128]{1,0:T(8,128)S(1)} %get-tuple-element.24), channel_id=1, source_target_pairs={{1,2},{3,4},{5,6},{7,8},{9,10},{11,12},{13,14},{15,16},{17,18},{19... | collective-permute-start | bytes 511496 | tf_op jit(solution)/shard_map/ppermute | solution.py:517
  2.3 11.0 %collective-permute-start.1 = (f32[333,128]{1,0:T(8,128)S(1)}, f32[333,128]{1,0:T(8,128)S(1)}, u32[]{:S(2)}, u32[]{:S(2)}) collective-permute-start(f32[333,128]{1,0:T(8,128)S(1)} %get-tuple-element.25), channel_id=1, source_target_pairs={{0,1},{2,3},{4,5},{6,7},{8,9},{10,11},{12,13},{14,15},{16,17},{18,... | collective-permute-start | bytes 511496 | tf_op jit(solution)/shard_map/ppermute | solution.py:518
  6.8 12.8 %all-to-all-start = ((f32[32,1,128]{2,1,0:T(1,128)}), f32[32,1,128]{2,1,0:T(1,128)S(1)}, u32[]{:S(2)}, u32[]{:S(2)}) async-start(f32[32,1,128]{2,1,0:T(1,128)} %bitcast.7), calls=%async_computation | async-start | bytes 32768 | tf_op jit(solution)/shard_map/all_to_all | solution.py:519

commit v11 on v9

--- a/solution.py
+++ b/solution.py
@@ -17,7 +17,7 @@
 LAID = 41
 SENT = 37
 WIDE = 32
-STEP = 33
+STEP = 40
 TALL = 16
 PAD = 8
 
@@ -144,7 +144,7 @@
     return first, last, partner == 0
 
 
-def tendency(load, geo, walls, index, inside, diff_ref, lift_ref):
+def tendency(load, geo, walls, index, inside, operators):
     speed_sq, rx, ry, sx, sy = geo[:5]
     outer_sq, waves, ghosts = geo[5:8], geo[8:11], geo[11:14]
     own = [[load(10 * field + node, 0) for node in range(10)] for field in range(3)]
@@ -182,14 +182,14 @@
     for a in range(10):
         total = along_r = along_s = None
         for b in range(10):
-            d_r, d_s = diff_ref[a, 0, b], diff_ref[a, 1, b]
+            d_r, d_s = operators[a // 4, a % 4 * 32 + b], operators[a // 4, a % 4 * 32 + 10 + b]
             term = d_r * flow_r[b] + d_s * flow_s[b]
             total = term if b == 0 else total + term
             along_r = d_r * eta[b] if b == 0 else along_r + d_r * eta[b]
             along_s = d_s * eta[b] if b == 0 else along_s + d_s * eta[b]
         sums = [total, pull[0] * along_r + push[0] * along_s, pull[1] * along_r + push[1] * along_s]
         for q in range(12):
-            weight = lift_ref[a, q]
+            weight = operators[a // 4, a % 4 * 32 + 20 + q]
             for field in range(3):
                 sums[field] = sums[field] + weight * jumps[field][q]
         for field in range(3):
@@ -253,8 +253,8 @@
 
 def prep_kernel(
     sizes, state_hbm, depth_hbm, metric_hbm, partner_hbm, refine_hbm, diff_hbm, lift_hbm, prolong_hbm,
-    cur, aux, weights, diff_ref, lift_ref,
-    state_ref, depth_ref, metric_ref, partner_ref, refine_ref, prolong_ref, spread, wide, sems,
+    cur, aux, weights, operators,
+    state_ref, depth_ref, metric_ref, partner_ref, refine_ref, prolong_ref, diff_ref, lift_ref, spread, wide, sems,
 ):
     blocks = sizes.blocks
     copies = fetch_all(
@@ -273,6 +273,12 @@
     for copy in copies:
         copy.wait()
     weights[...] = child_matrix(prolong_ref)
+    rows = jnp.concatenate([diff_ref[:, 0, :], diff_ref[:, 1, :], lift_ref[...]], axis=1)
+    rows = jnp.concatenate([rows, jnp.zeros((2, 32), jnp.float32)], axis=0)
+    for row in range(3):
+        for part in range(4):
+            at = 4 * row + part
+            operators[row : row + 1, 32 * part : 32 * part + 32] = rows[at : at + 1]
     metric = split_metric(metric_ref, spread, blocks)
     dense = [depth_ref[...], *metric, partner_ref[...].astype(jnp.float32), refine_ref[...].astype(jnp.float32)]
     for num in range(7):
@@ -284,15 +290,15 @@
 
 
 def first_kernel(
-    sizes, cur_own, aux_own, weights_in, diff_in, lift_in, odd_ref, even_ref,
+    sizes, cur_own, aux_own, weights_in, operators_in, odd_ref, even_ref,
     cur, rate_ref, twice_ref, weights, ends_ref, lines_ref,
-    geo_ref, aux, diff_ref, lift_ref, sems,
+    geo_ref, aux, operators, sems,
 ):
     blocks, halo = sizes.blocks, sizes.halo
     top, bottom = PAD + halo, PAD + halo + blocks
     place = lax.axis_index(AXES)
     count = lax.axis_size(AXES)
-    copies = fetch_all(((diff_in, diff_ref), (lift_in, lift_ref)), sems)
+    copies = fetch_all(((operators_in, operators),), sems)
     even = place % 2 == 0
 
     def set_halo(target, num, row):
@@ -338,7 +344,7 @@
         ]
         ghosts = [8.0 / squares[k] for k in range(3)]
         geo = [speed_sq, rx, ry, sx, sy, *outer_sq, *waves, *ghosts]
-        rates = tendency(load, geo, walls, index, inside, diff_ref, lift_ref)
+        rates = tendency(load, geo, walls, index, inside, operators)
         for num, value in enumerate([*geo, partner]):
             geo_ref[num, pl.ds(start, height), :] = value
         for item in range(30):
@@ -355,7 +361,7 @@
         partner = geo_ref[14, at, :]
         index, inside = pair_index(partner)
         walls = wall_masks(sizes, row, place, count, partner)
-        rates = tendency(load, geo, walls, index, inside, diff_ref, lift_ref)
+        rates = tendency(load, geo, walls, index, inside, operators)
         for item in range(30):
             twice_ref[item, pl.ds(start, height), :] = rates[item]
 
@@ -394,7 +400,7 @@
     first_slot = LANES * lax.broadcasted_iota(jnp.int32, (slots, LANES), 1).astype(jnp.float32)
     lead = jnp.sum((base_ref[1] + start <= first_slot).astype(jnp.float32), axis=0, keepdims=True)
     lead = jnp.clip(lead.astype(jnp.int32), 0, slots - 1)
-    place_v[...] = jnp.broadcast_to(lead, (8, LANES))
+    place_v[...] = lead
     copy = pltpu.make_async_copy(place_v, place_s, sem)
     copy.start()
     for item in range(30):
@@ -449,8 +455,8 @@
             ahead = jnp.broadcast_to(index_ref[2, slot : slot + 1, :], (8, LANES)) > 0.5
             tiles = []
             for row in range(0, WIDE, 8):
-                one = wide[pl.ds(lead_at + row, 8), :]
-                two = wide[pl.ds(lead_at + STEP + row, 8), :]
+                one = wide[pl.ds(pl.multiple_of(lead_at + row, 8), 8), :]
+                two = wide[pl.ds(pl.multiple_of(lead_at + STEP + row, 8), 8), :]
                 tiles.append(lane_gather(jnp.where(ahead, two, one), lane_idx))
             columns.append(jnp.concatenate(tiles, axis=0))
         values = jnp.concatenate(columns, axis=1)
@@ -520,7 +526,7 @@
     even = lax.ppermute(even, AXES, swaps(0, count))
     stats = lax.all_to_all(stats, AXES, 0, 0, tiled=True)
     even, odd, stats = [pltpu.with_memory_space_constraint(x, pltpu.VMEM) for x in (even, odd, stats)]
-    cur, aux, weights, diff_near, lift_near = pl.pallas_call(
+    cur, aux, weights, operators = pl.pallas_call(
         functools.partial(prep_kernel, sizes),
         name="lay_out",
         cost_estimate=pl.CostEstimate(flops=1 << 24, transcendentals=1 << 16, bytes_accessed=1 << 24),
@@ -528,15 +534,16 @@
             jax.ShapeDtypeStruct((30, blocks, LANES), f32),
             jax.ShapeDtypeStruct((7, blocks, LANES), f32),
             jax.ShapeDtypeStruct((3 * PACK, 3 * WIDE), jnp.bfloat16),
-            jax.ShapeDtypeStruct(diff_ops.shape, f32),
-            jax.ShapeDtypeStruct(lift.shape, f32),
+            jax.ShapeDtypeStruct((3, LANES), f32),
         ),
         in_specs=[HBM] * 8,
-        out_specs=(VMEM,) * 5,
+        out_specs=(VMEM,) * 4,
         scratch_shapes=[
             pltpu.VMEM(state.shape, f32),
             *dense,
             pltpu.VMEM(prolong.shape, f32),
+            pltpu.VMEM(diff_ops.shape, f32),
+            pltpu.VMEM(lift.shape, f32),
             pltpu.VMEM((8 * blocks, LANES), f32),
             pltpu.VMEM((LAID * blocks, LANES), f32),
             pltpu.SemaphoreType.DMA((8,)),
@@ -555,17 +562,16 @@
             jax.ShapeDtypeStruct((2, slots, LANES), f32),
             jax.ShapeDtypeStruct((3, 8, LANES), f32),
         ),
-        in_specs=[VMEM] * 7,
+        in_specs=[VMEM] * 6,
         out_specs=(VMEM,) * 6,
         scratch_shapes=[
             pltpu.VMEM((15, rows, LANES), f32),
             pltpu.VMEM((7, sizes.tall, LANES), f32),
-            pltpu.SMEM(diff_ops.shape, f32),
-            pltpu.SMEM(lift.shape, f32),
-            pltpu.SemaphoreType.DMA((2,)),
+            pltpu.SMEM((3, LANES), f32),
+            pltpu.SemaphoreType.DMA((1,)),
         ],
         compiler_params=PARAMS,
-    )(cur, aux, weights, diff_near, lift_near, odd, even)
+    )(cur, aux, weights, operators, odd, even)
     refined = pl.pallas_call(
         functools.partial(refine_kernel, sizes),
         name="sum_and_refine",
@@ -574,8 +580,8 @@
         out_specs=HBM,
         scratch_shapes=[
             pltpu.VMEM((10, 3, LANES * slots), f32),
-            pltpu.VMEM((8, LANES), i32),
-            pltpu.SMEM((8, LANES), i32),
+            pltpu.VMEM((1, LANES), i32),
+            pltpu.SMEM((1, LANES), i32),
             pltpu.VMEM((STEP * (slots + 1), LANES), f32),
             pltpu.VMEM((3, slots, LANES), f32),
             pltpu.SemaphoreType.DMA((slots // 8,)),

time: 21.5 us -> 21.5 us (level)
  no operation moved by 1% of the time
where the time goes in v11:
time: 21.5 us; the launch traced here: 21.3 us
  Pallas kernels  11.2 us (52%)
  starting transfers between devices  9.95 us (46%)
    pallas_call x1, Pallas kernels, shards(): pl.pallas_call(functools.partial(first_kernel, sizes), name='rates_twice'...  5.31 us
    all_to_all x1, starting transfers between devices, shards(): stats = lax.all_to_all(stats, AXES, 0, 0, tiled=True)  4.84 us
    ppermute x1, starting transfers between devices, shards(): even = lax.ppermute(even, AXES, swaps(0, count))  4.44 us
    pallas_call x1, Pallas kernels, shards(): pl.pallas_call(functools.partial(refine_kernel, sizes), name='sum_and_ref...  2.55 us
    pallas_call x1, Pallas kernels, shards(): pl.pallas_call(functools.partial(prep_kernel, sizes), name='lay_out', cos...  1.73 us
    pallas_call x1, Pallas kernels, shards(): pl.pallas_call(functools.partial(pack_kernel, sizes), name='pack', out_sh...  1.65 us
    ppermute x1, starting transfers between devices, shards(): odd = lax.ppermute(odd, AXES, swaps(1, count))  0.67 us
  transfers between devices with their start and end apart: 3, of which 0 were waited for; matrix products, arithmetic and copies ran while one was open for 0% of the time, Pallas kernels for 33%

profile of v11, /device:TPU:0, one launch (start us, length us, event | category | flops | bytes accessed | tf_op | source)
XLA Modules:
  0.0 21.3 jit_solution(9379701642094851675)
XLA Ops:
  0.0 1.7 %pack.1 = (f32[32,128]{1,0:T(8,128)}, f32[333,128]{1,0:T(8,128)S(1)}, f32[333,128]{1,0:T(8,128)S(1)}) custom-call(f32[10,3,4096]{2,1,0:T(4,128)} %bitcast.12, f32[32,128]{1,0:T(8,128)} %bitcast.14, f32[4,4096]{1,0:T(4,128)} %metric_hbm.3, s32[32,128]{1,0:T(8,128)} %bitcast.16, s32[32,128]{1,0:T(8,128)} %bitcast.18), custom_call_target="tpu_custom_call" | custom-call | tf_op jit(solution)/shard_map/pack/pallas_call | solution.py:508
  1.7 0.7 %collective-permute-start = (f32[333,128]{1,0:T(8,128)S(1)}, f32[333,128]{1,0:T(8,128)S(1)}, u32[]{:S(2)}, u32[]{:S(2)}) collective-permute-start(f32[333,128]{1,0:T(8,128)S(1)} %get-tuple-element.22), channel_id=1, source_target_pairs={{1,2},{3,4},{5,6},{7,8},{9,10},{11,12},{13,14},{15,16},{17,18},{19... | collective-permute-start | bytes 511496 | tf_op jit(solution)/shard_map/ppermute | solution.py:525
  2.3 4.4 %collective-permute-start.1 = (f32[333,128]{1,0:T(8,128)S(1)}, f32[333,128]{1,0:T(8,128)S(1)}, u32[]{:S(2)}, u32[]{:S(2)}) collective-permute-start(f32[333,128]{1,0:T(8,128)S(1)} %get-tuple-element.23), channel_id=1, source_target_pairs={{0,1},{2,3},{4,5},{6,7},{8,9},{10,11},{12,13},{14,15},{16,17},{18,... | collective-permute-start | bytes 511496 | tf_op jit(solution)/shard_map/ppermute | solution.py:526
  6.8 4.8 %all-to-all-start = ((f32[32,1,128]{2,1,0:T(1,128)}), f32[32,1,128]{2,1,0:T(1,128)S(1)}, u32[]{:S(2)}, u32[]{:S(2)}) async-start(f32[32,1,128]{2,1,0:T(1,128)} %bitcast.7), calls=%async_computation | async-start | bytes 32768 | tf_op jit(solution)/shard_map/all_to_all | solution.py:527
  11.6 1.7 %lay_out.1 = (f32[30,32,128]{2,1,0:T(8,128)S(1)}, f32[7,32,128]{2,1,0:T(8,128)S(1)}, bf16[120,96]{1,0:T(8,128)(2,1)S(1)}, f32[3,128]{1,0:T(4,128)S(1)}) custom-call(f32[10,3,4096]{2,1,0:T(4,128)} %bitcast.13, f32[32,128]{1,0:T(8,128)} %bitcast.15, f32[4,4096]{1,0:T(4,128)} %metric_hbm.3, s32[32,128]{1,0:T(8,128)} %bitcast.17, s32[32,128]{1,0:T(8,128)} %bitcast.19, ...), custom_call_target="tpu_custom_call" | custom-call | flops 16777216 | bytes 16777216 | tf_op jit(solution)/shard_map/lay_out/pallas_call | solution.py:529
  13.4 0.0 collective-permute-done.odd_ref
  13.4 0.0 collective-permute-done.1.even_ref
  13.4 5.3 %rates_twice.1 = (f32[30,72,128]{2,1,0:T(8,128)S(1)}, f32[30,72,128]{2,1,0:T(8,128)S(1)}, f32[30,48,128]{2,1,0:T(8,128)S(1)}, bf16[120,96]{1,0:T(8,128)(2,1)S(1)...) custom-call(f32[30,32,128]{2,1,0:T(8,128)S(1)} %get-tuple-element.18.cur_own, ...), custom_call_target="tpu_custom_call" | custom-call | flops 1024 | bytes 1024 | tf_op jit(solution)/shard_map/rates_twice/pallas_call | solution.py:553
  18.7 0.0 all-to-all-done
  18.7 2.6 %sum_and_refine.1 = f32[10,3,6144]{2,1,0:T(4,128)} custom-call(f32[30,72,128]{2,1,0:T(8,128)S(1)} %get-tuple-element.24.cur, f32[30,72,128]{2,1,0:T(8,128)S(1)} %get-tuple-element.25.rate_ref, f32[30,48,128]{2,1,0:T(8,128)S(1)} %get-tuple-element.26.twice_ref, bf16[120,96]{1,0:T(8,128)(2,1)S(1)} %get-tuple-element.27.weights, ...), custom_call_target="tpu_custom_call" | custom-call | tf_op jit(solution)/shard_map/sum_and_refine/pallas_call | solution.py:575
Async XLA Ops:
  1.7 11.7 %collective-permute-start = (f32[333,128]{1,0:T(8,128)S(1)}, f32[333,128]{1,0:T(8,128)S(1)}, u32[]{:S(2)}, u32[]{:S(2)}) collective-permute-start(f32[333,128]{1,0:T(8,128)S(1)} %get-tuple-element.22), channel_id=1, source_target_pairs={{1,2},{3,4},{5,6},{7,8},{9,10},{11,12},{13,14},{15,16},{17,18},{19... | collective-permute-start | bytes 511496 | tf_op jit(solution)/shard_map/ppermute | solution.py:525
  2.3 11.0 %collective-permute-start.1 = (f32[333,128]{1,0:T(8,128)S(1)}, f32[333,128]{1,0:T(8,128)S(1)}, u32[]{:S(2)}, u32[]{:S(2)}) collective-permute-start(f32[333,128]{1,0:T(8,128)S(1)} %get-tuple-element.23), channel_id=1, source_target_pairs={{0,1},{2,3},{4,5},{6,7},{8,9},{10,11},{12,13},{14,15},{16,17},{18,... | collective-permute-start | bytes 511496 | tf_op jit(solution)/shard_map/ppermute | solution.py:526
  6.8 11.9 %all-to-all-start = ((f32[32,1,128]{2,1,0:T(1,128)}), f32[32,1,128]{2,1,0:T(1,128)S(1)}, u32[]{:S(2)}, u32[]{:S(2)}) async-start(f32[32,1,128]{2,1,0:T(1,128)} %bitcast.7), calls=%async_computation | async-start | bytes 32768 | tf_op jit(solution)/shard_map/all_to_all | solution.py:527

commit v12 on v11

--- a/solution.py
+++ b/solution.py
@@ -17,7 +17,7 @@
 LAID = 41
 SENT = 37
 WIDE = 32
-STEP = 40
+STEP = 33
 TALL = 16
 PAD = 8
 
@@ -224,7 +224,7 @@
     return jnp.concatenate([first, first, last], axis=1).astype(bf16)
 
 
-def sum_children(sizes, refine, ends_ref, lines_ref):
+def sum_children(sizes, refine, ends_ref, full_ref, lines_ref):
     slots, f32 = sizes.slots, jnp.float32
     counts = (1.0 + refine).astype(jnp.bfloat16)
     row_i = lax.broadcasted_iota(jnp.int32, (LANES, LANES), 0)
@@ -237,8 +237,10 @@
     lower = (col_s < row_s).astype(jnp.bfloat16)
     before = jnp.dot(lower, whole.astype(jnp.bfloat16), preferred_element_type=f32)
     before = before - before[sizes.margin : sizes.margin + 1, :]
-    ends_ref[0] = 2.0 * (within + before) + refine
-    ends_ref[1] = before + whole
+    ends = 2.0 * (within + before) + refine
+    high = jnp.floor(ends * (1.0 / 256.0))
+    ends_ref[...] = jnp.concatenate([high, ends - 256.0 * high], axis=1).astype(jnp.bfloat16)
+    full_ref[...] = before + whole
     ones = jnp.ones((8, LANES), jnp.bfloat16)
     sums = lax.dot_general(ones, counts, (((1,), (1,)), ((), ())), preferred_element_type=f32)
     gap = lax.broadcasted_iota(jnp.int32, (slots, LANES), 1) - lax.broadcasted_iota(jnp.int32, (slots, LANES), 0)
@@ -291,7 +293,7 @@
 
 def first_kernel(
     sizes, cur_own, aux_own, weights_in, operators_in, odd_ref, even_ref,
-    cur, rate_ref, twice_ref, weights, ends_ref, lines_ref,
+    cur, rate_ref, twice_ref, weights, ends_ref, full_ref, lines_ref,
     geo_ref, aux, operators, sems,
 ):
     blocks, halo = sizes.blocks, sizes.halo
@@ -318,7 +320,7 @@
 
     weights[...] = weights_in[...]
     begin = PAD + sizes.keep
-    sum_children(sizes, aux[6, begin : begin + sizes.slots, :], ends_ref, lines_ref)
+    sum_children(sizes, aux[6, begin : begin + sizes.slots, :], ends_ref, full_ref, lines_ref)
     for copy in copies:
         copy.wait()
 
@@ -366,11 +368,8 @@
             twice_ref[item, pl.ds(start, height), :] = rates[item]
 
     def sweep(work, rows):
-        def body(num, carry):
-            work(pl.multiple_of(TALL * num, TALL), TALL)
-            return carry
-
-        lax.fori_loop(0, rows // TALL, body, 0)
+        for start in range(0, rows // TALL * TALL, TALL):
+            work(start, TALL)
 
     for start in range(sizes.rows // TALL * TALL, sizes.rows, 8):
         step(start, 8)
@@ -381,7 +380,7 @@
 
 
 def refine_kernel(
-    sizes, cur, rate_ref, twice_ref, weights, base_ref, lines_ref, stats_ref, out_hbm,
+    sizes, cur, rate_ref, twice_ref, weights, base_ref, full_ref, lines_ref, stats_ref, out_hbm,
     out_ref, place_v, place_s, wide, index_ref, out_sems, sem,
 ):
     slots, keep = sizes.slots, sizes.keep
@@ -398,7 +397,7 @@
     half_square = 0.5 * step * step
     start = earlier - (place * (sizes.cells // 2)).astype(jnp.float32)
     first_slot = LANES * lax.broadcasted_iota(jnp.int32, (slots, LANES), 1).astype(jnp.float32)
-    lead = jnp.sum((base_ref[1] + start <= first_slot).astype(jnp.float32), axis=0, keepdims=True)
+    lead = jnp.sum((full_ref[...] + start <= first_slot).astype(jnp.float32), axis=0, keepdims=True)
     lead = jnp.clip(lead.astype(jnp.int32), 0, slots - 1)
     place_v[...] = lead
     copy = pltpu.make_async_copy(place_v, place_s, sem)
@@ -411,16 +410,15 @@
         wide[pl.ds(item, slots + 1, stride=STEP), :] = jnp.zeros((slots + 1, LANES), jnp.float32)
     slot_start = LANES * lax.broadcasted_iota(jnp.int32, (slots, LANES), 0).astype(jnp.float32)
     begun = [lines_ref[num, 0:1, :] + start <= slot_start for num in range(3)]
-    near, far = [
-        2.0 * start
-        + jnp.dot(
-            (begun[num] & ~begun[num + 1]).astype(jnp.float32)[:, :slots],
-            base_ref[0],
-            precision=HIGH,
+    halves = [
+        jnp.dot(
+            (begun[num] & ~begun[num + 1]).astype(jnp.bfloat16)[:, :slots],
+            base_ref[...],
             preferred_element_type=jnp.float32,
         )
         for num in (1, 0)
     ]
+    near, far = [256.0 * x[:, :LANES] + (x[:, LANES:] + 2.0 * start) for x in halves]
     lane = lax.broadcasted_iota(jnp.int32, (slots, LANES), 1)
     slot_no = LANES * lax.broadcasted_iota(jnp.int32, (slots, LANES), 0) + lane
     goal = (2 * slot_no + 1).astype(jnp.float32)
@@ -430,11 +428,10 @@
         return jnp.where(beyond, lane_gather(far, index), lane_gather(near, index))
 
     found = jnp.zeros((slots, LANES), jnp.int32)
-    size = LANES // 2
-    while size:
-        passed = pick(found + (size - 1)) <= goal
-        found = jnp.where(passed, found + size, found)
-        size //= 2
+    for size in (LANES // 4, LANES // 16, LANES // 64):
+        passed = [(pick(found + (probe * size - 1)) <= goal).astype(jnp.int32) for probe in (1, 2, 3)]
+        found = found + size * (passed[0] + passed[1] + passed[2])
+    found = found + (pick(found) <= goal).astype(jnp.int32)
     mine = pick(found).astype(jnp.int32)
     split = mine & 1
     begin = (mine >> 1) - 1 - split
@@ -444,19 +441,19 @@
     index_ref[2] = (lane < jnp.broadcast_to(found[:, 0:1], (slots, LANES))).astype(jnp.float32)
     copy.wait()
     matrix = weights[...]
-    chunk = 8 * LANES
     results = []
-    for part in range(slots // 8):
-        span = slice(chunk * part, chunk * (part + 1))
+    parts = [(at, 8) for at in range(0, slots - 8, 8)] + [(slots - 8, 4), (slots - 4, 4)]
+    for part, (begin_at, height) in enumerate(parts):
+        span = slice(LANES * begin_at, LANES * (begin_at + height))
         columns = []
-        for slot in range(8 * part, 8 * part + 8):
+        for slot in range(begin_at, begin_at + height):
             lead_at = place_s[0, slot] * STEP
             lane_idx = jnp.broadcast_to(index_ref[0, slot : slot + 1, :], (8, LANES)).astype(jnp.int32)
             ahead = jnp.broadcast_to(index_ref[2, slot : slot + 1, :], (8, LANES)) > 0.5
             tiles = []
             for row in range(0, WIDE, 8):
-                one = wide[pl.ds(pl.multiple_of(lead_at + row, 8), 8), :]
-                two = wide[pl.ds(pl.multiple_of(lead_at + STEP + row, 8), 8), :]
+                one = wide[pl.ds(lead_at + row, 8), :]
+                two = wide[pl.ds(lead_at + STEP + row, 8), :]
                 tiles.append(lane_gather(jnp.where(ahead, two, one), lane_idx))
             columns.append(jnp.concatenate(tiles, axis=0))
         values = jnp.concatenate(columns, axis=1)
@@ -464,8 +461,8 @@
         low = (values - high.astype(jnp.float32)).astype(jnp.bfloat16)
         stack = jnp.concatenate([high, low, high], axis=0)
         children = jnp.dot(matrix, stack, preferred_element_type=jnp.float32)
-        for sub in range(8):
-            slot = 8 * part + sub
+        for sub in range(height):
+            slot = begin_at + sub
             cut = slice(LANES * sub, LANES * (sub + 1))
             tag = jnp.broadcast_to(index_ref[1, slot : slot + 1, :], (PACK, LANES))
             value = jnp.where(
@@ -550,7 +547,7 @@
         ],
         compiler_params=PARAMS,
     )(state, depth, metric, partner, refine, diff_ops, lift, prolong)
-    cur, rates, twice, weights, ends, lines = pl.pallas_call(
+    cur, rates, twice, weights, ends, full, lines = pl.pallas_call(
         functools.partial(first_kernel, sizes),
         name="rates_twice",
         cost_estimate=pl.CostEstimate(flops=1024, transcendentals=0, bytes_accessed=1024),
@@ -559,11 +556,12 @@
             jax.ShapeDtypeStruct((30, sizes.tall, LANES), f32),
             jax.ShapeDtypeStruct((30, slots, LANES), f32),
             jax.ShapeDtypeStruct((3 * PACK, 3 * WIDE), jnp.bfloat16),
-            jax.ShapeDtypeStruct((2, slots, LANES), f32),
+            jax.ShapeDtypeStruct((slots, 2 * LANES), jnp.bfloat16),
+            jax.ShapeDtypeStruct((slots, LANES), f32),
             jax.ShapeDtypeStruct((3, 8, LANES), f32),
         ),
         in_specs=[VMEM] * 6,
-        out_specs=(VMEM,) * 6,
+        out_specs=(VMEM,) * 7,
         scratch_shapes=[
             pltpu.VMEM((15, rows, LANES), f32),
             pltpu.VMEM((7, sizes.tall, LANES), f32),
@@ -576,7 +574,7 @@
         functools.partial(refine_kernel, sizes),
         name="sum_and_refine",
         out_shape=jax.ShapeDtypeStruct((10, 3, LANES * slots), f32),
-        in_specs=[VMEM] * 7,
+        in_specs=[VMEM] * 8,
         out_specs=HBM,
         scratch_shapes=[
             pltpu.VMEM((10, 3, LANES * slots), f32),
@@ -584,11 +582,11 @@
             pltpu.SMEM((1, LANES), i32),
             pltpu.VMEM((STEP * (slots + 1), LANES), f32),
             pltpu.VMEM((3, slots, LANES), f32),
-            pltpu.SemaphoreType.DMA((slots // 8,)),
+            pltpu.SemaphoreType.DMA((slots // 8 + 1,)),
             pltpu.SemaphoreType.DMA,
         ],
         compiler_params=PARAMS,
-    )(cur, rates, twice, weights, ends, lines, stats)
+    )(cur, rates, twice, weights, ends, full, lines, stats)
     return jnp.transpose(refined, (1, 0, 2))
 
 

time: 21.5 us -> 21.3 us (level)
  Pallas kernels: 11.2 us -> 10.7 us
  waiting for transfers between devices: 0.01 us -> 0.32 us
    pallas_call x1, Pallas kernels: 5.31 us -> 4.98 us  [shards(): pl.pallas_call(functools.partial(first_kernel, sizes), name='rates_twice'...]
    all_to_all x1, waiting for transfers between devices: 0.01 us -> 0.32 us  [shards(): stats = lax.all_to_all(stats, AXES, 0, 0, tiled=True)]
  transfers between devices with their start and end apart: 3 -> 3, of which waited for: 0 -> 1; matrix products, arithmetic and copies ran while one was open for 0% -> 0% of each run, Pallas kernels for 33% -> 32%
where the time goes in v12:
time: 21.3 us; the launch traced here: 21.1 us
  Pallas kernels  10.7 us (50%)
  starting transfers between devices  9.95 us (47%)
  waiting for transfers between devices  0.32 us (2%)
    pallas_call x1, Pallas kernels, shards(): pl.pallas_call(functools.partial(first_kernel, sizes), name='rates_twice'...  4.98 us
    all_to_all x1, starting transfers between devices, shards(): stats = lax.all_to_all(stats, AXES, 0, 0, tiled=True)  4.84 us
    ppermute x1, starting transfers between devices, shards(): even = lax.ppermute(even, AXES, swaps(0, count))  4.44 us
    pallas_call x1, Pallas kernels, shards(): pl.pallas_call(functools.partial(refine_kernel, sizes), name='sum_and_ref...  2.38 us
    pallas_call x1, Pallas kernels, shards(): pl.pallas_call(functools.partial(prep_kernel, sizes), name='lay_out', cos...  1.73 us
    pallas_call x1, Pallas kernels, shards(): pl.pallas_call(functools.partial(pack_kernel, sizes), name='pack', out_sh...  1.65 us
    ppermute x1, starting transfers between devices, shards(): odd = lax.ppermute(odd, AXES, swaps(1, count))  0.67 us
  transfers between devices with their start and end apart: 3, of which 1 were waited for; matrix products, arithmetic and copies ran while one was open for 0% of the time, Pallas kernels for 32%

profile of v12, /device:TPU:0, one launch (start us, length us, event | category | flops | bytes accessed | tf_op | source)
XLA Modules:
  0.0 21.1 jit_solution(8356308055857248648)
XLA Ops:
  0.0 1.7 %pack.1 = (f32[32,128]{1,0:T(8,128)}, f32[333,128]{1,0:T(8,128)S(1)}, f32[333,128]{1,0:T(8,128)S(1)}) custom-call(f32[10,3,4096]{2,1,0:T(4,128)} %bitcast.12, f32[32,128]{1,0:T(8,128)} %bitcast.14, f32[4,4096]{1,0:T(4,128)} %metric_hbm.3, s32[32,128]{1,0:T(8,128)} %bitcast.16, s32[32,128]{1,0:T(8,128)} %bitcast.18), custom_call_target="tpu_custom_call" | custom-call | tf_op jit(solution)/shard_map/pack/pallas_call | solution.py:505
  1.7 0.7 %collective-permute-start = (f32[333,128]{1,0:T(8,128)S(1)}, f32[333,128]{1,0:T(8,128)S(1)}, u32[]{:S(2)}, u32[]{:S(2)}) collective-permute-start(f32[333,128]{1,0:T(8,128)S(1)} %get-tuple-element.23), channel_id=1, source_target_pairs={{1,2},{3,4},{5,6},{7,8},{9,10},{11,12},{13,14},{15,16},{17,18},{19... | collective-permute-start | bytes 511496 | tf_op jit(solution)/shard_map/ppermute | solution.py:522
  2.3 4.4 %collective-permute-start.1 = (f32[333,128]{1,0:T(8,128)S(1)}, f32[333,128]{1,0:T(8,128)S(1)}, u32[]{:S(2)}, u32[]{:S(2)}) collective-permute-start(f32[333,128]{1,0:T(8,128)S(1)} %get-tuple-element.24), channel_id=1, source_target_pairs={{0,1},{2,3},{4,5},{6,7},{8,9},{10,11},{12,13},{14,15},{16,17},{18,... | collective-permute-start | bytes 511496 | tf_op jit(solution)/shard_map/ppermute | solution.py:523
  6.8 4.8 %all-to-all-start = ((f32[32,1,128]{2,1,0:T(1,128)}), f32[32,1,128]{2,1,0:T(1,128)S(1)}, u32[]{:S(2)}, u32[]{:S(2)}) async-start(f32[32,1,128]{2,1,0:T(1,128)} %bitcast.7), calls=%async_computation | async-start | bytes 32768 | tf_op jit(solution)/shard_map/all_to_all | solution.py:524
  11.6 1.7 %lay_out.1 = (f32[30,32,128]{2,1,0:T(8,128)S(1)}, f32[7,32,128]{2,1,0:T(8,128)S(1)}, bf16[120,96]{1,0:T(8,128)(2,1)S(1)}, f32[3,128]{1,0:T(4,128)S(1)}) custom-call(f32[10,3,4096]{2,1,0:T(4,128)} %bitcast.13, f32[32,128]{1,0:T(8,128)} %bitcast.15, f32[4,4096]{1,0:T(4,128)} %metric_hbm.3, s32[32,128]{1,0:T(8,128)} %bitcast.17, s32[32,128]{1,0:T(8,128)} %bitcast.19, ...), custom_call_target="tpu_custom_call" | custom-call | flops 16777216 | bytes 16777216 | tf_op jit(solution)/shard_map/lay_out/pallas_call | solution.py:526
  13.4 0.0 collective-permute-done.odd_ref
  13.4 0.0 collective-permute-done.1.even_ref
  13.4 5.0 %rates_twice.1 = (f32[30,72,128]{2,1,0:T(8,128)S(1)}, f32[30,72,128]{2,1,0:T(8,128)S(1)}, f32[30,48,128]{2,1,0:T(8,128)S(1)}, bf16[120,96]{1,0:T(8,128)(2,1)S(1)...) custom-call(f32[30,32,128]{2,1,0:T(8,128)S(1)} %get-tuple-element.19.cur_own, ...), custom_call_target="tpu_custom_call" | custom-call | flops 1024 | bytes 1024 | tf_op jit(solution)/shard_map/rates_twice/pallas_call | solution.py:550
  18.4 0.3 %all-to-all-done = f32[32,1,128]{2,1,0:T(1,128)S(1)} async-done(((f32[32,1,128]{2,1,0:T(1,128)}), f32[32,1,128]{2,1,0:T(1,128)S(1)}, u32[]{:S(2)}, u32[]{:S(2)}) %all-to-all-start) | async-done | bytes 16416 | tf_op jit(solution)/shard_map/all_to_all | solution.py:524
  18.7 2.4 %sum_and_refine.1 = f32[10,3,6144]{2,1,0:T(4,128)} custom-call(f32[30,72,128]{2,1,0:T(8,128)S(1)} %get-tuple-element.25.cur, f32[30,72,128]{2,1,0:T(8,128)S(1)} %get-tuple-element.26.rate_ref, f32[30,48,128]{2,1,0:T(8,128)S(1)} %get-tuple-element.27.twice_ref, bf16[120,96]{1,0:T(8,128)(2,1)S(1)} %get-tuple-element.28.weights, ...), custom_call_target="tpu_custom_call" | custom-call | tf_op jit(solution)/shard_map/sum_and_refine/pallas_call | solution.py:573
Async XLA Ops:
  1.7 11.7 %collective-permute-start = (f32[333,128]{1,0:T(8,128)S(1)}, f32[333,128]{1,0:T(8,128)S(1)}, u32[]{:S(2)}, u32[]{:S(2)}) collective-permute-start(f32[333,128]{1,0:T(8,128)S(1)} %get-tuple-element.23), channel_id=1, source_target_pairs={{1,2},{3,4},{5,6},{7,8},{9,10},{11,12},{13,14},{15,16},{17,18},{19... | collective-permute-start | bytes 511496 | tf_op jit(solution)/shard_map/ppermute | solution.py:522
  2.3 11.0 %collective-permute-start.1 = (f32[333,128]{1,0:T(8,128)S(1)}, f32[333,128]{1,0:T(8,128)S(1)}, u32[]{:S(2)}, u32[]{:S(2)}) collective-permute-start(f32[333,128]{1,0:T(8,128)S(1)} %get-tuple-element.24), channel_id=1, source_target_pairs={{0,1},{2,3},{4,5},{6,7},{8,9},{10,11},{12,13},{14,15},{16,17},{18,... | collective-permute-start | bytes 511496 | tf_op jit(solution)/shard_map/ppermute | solution.py:523
  6.8 11.9 %all-to-all-start = ((f32[32,1,128]{2,1,0:T(1,128)}), f32[32,1,128]{2,1,0:T(1,128)S(1)}, u32[]{:S(2)}, u32[]{:S(2)}) async-start(f32[32,1,128]{2,1,0:T(1,128)} %bitcast.7), calls=%async_computation | async-start | bytes 32768 | tf_op jit(solution)/shard_map/all_to_all | solution.py:524

commit v13 on v12

--- a/solution.py
+++ b/solution.py
@@ -302,36 +302,40 @@
     count = lax.axis_size(AXES)
     copies = fetch_all(((operators_in, operators),), sems)
     even = place % 2 == 0
+    zero = jnp.minimum(place, 0)
 
     def set_halo(target, num, row):
         by_even = even_ref[pl.ds(row, halo, stride=SENT), :]
         by_odd = odd_ref[pl.ds(row, halo, stride=SENT), :]
         target[num, top - halo : top, :] = jnp.where(even, by_odd, by_even)
-        target[num, bottom : bottom + halo, :] = jnp.where(even, by_even, by_odd)
+        target[num, pl.ds(zero + bottom, halo), :] = jnp.where(even, by_even, by_odd)
 
     for num in range(7):
         set_halo(aux, num, 30 + num)
-        aux[num, top:bottom, :] = aux_own[num]
+        aux[num, pl.ds(zero + top, blocks), :] = aux_own[num]
     for field in range(3):
         for node in range(10):
             item = 10 * field + node
             set_halo(cur, item, 3 * node + field)
-            cur[item, top:bottom, :] = cur_own[item]
+            cur[item, pl.ds(zero + top, blocks), :] = cur_own[item]
 
     weights[...] = weights_in[...]
     begin = PAD + sizes.keep
-    sum_children(sizes, aux[6, begin : begin + sizes.slots, :], ends_ref, full_ref, lines_ref)
+    sum_children(sizes, aux[6, pl.ds(zero + begin, sizes.slots), :], ends_ref, full_ref, lines_ref)
     for copy in copies:
         copy.wait()
 
     def step(start, height):
         base = PAD + start
 
+        def rows(shift):
+            return pl.ds(zero + (base + shift) if shift else base, height)
+
         def load_aux(item, shift):
-            return aux[item, pl.ds(base + shift, height), :]
+            return aux[item, rows(shift), :]
 
         def load(item, shift):
-            return cur[item, pl.ds(base + shift, height), :]
+            return cur[item, rows(shift), :]
 
         depth, rx, ry, sx, sy, partner = [load_aux(num, 0) for num in range(6)]
         index, inside = pair_index(partner)
@@ -354,10 +358,10 @@
 
     def again(start, height):
         row = start + sizes.keep
-        at = pl.ds(row, height)
+        at = pl.ds(zero + row, height)
 
         def load(item, shift):
-            return rate_ref[item, pl.ds(PAD + row + shift, height), :]
+            return rate_ref[item, pl.ds(zero + (PAD + row + shift), height), :]
 
         geo = [geo_ref[num, at, :] for num in range(14)]
         partner = geo_ref[14, at, :]
@@ -385,6 +389,7 @@
 ):
     slots, keep = sizes.slots, sizes.keep
     place = lax.axis_index(AXES)
+    zero = jnp.minimum(place, 0)
     stats = stats_ref[...]
     half = LANES // 2
     row_n = lax.broadcasted_iota(jnp.int32, stats.shape, 0)
@@ -403,7 +408,7 @@
     copy = pltpu.make_async_copy(place_v, place_s, sem)
     copy.start()
     for item in range(30):
-        now = slice(PAD + keep, PAD + keep + slots)
+        now = pl.ds(zero + (PAD + keep), slots)
         value = cur[item, now, :] + step * rate_ref[item, now, :] + half_square * twice_ref[item]
         wide[pl.ds(item, slots, stride=STEP), :] = value
     for item in (30, 31):

time: 21.3 us -> 21.3 us (level)
  waiting for transfers between devices: 0.32 us -> 0.55 us
    pallas_call x1, Pallas kernels: 4.98 us -> 4.75 us  [shards(): pl.pallas_call(functools.partial(first_kernel, sizes), name='rates_twice'...]
    all_to_all x1, waiting for transfers between devices: 0.32 us -> 0.55 us  [shards(): stats = lax.all_to_all(stats, AXES, 0, 0, tiled=True)]
  transfers between devices with their start and end apart: 3 -> 3, of which waited for: 1 -> 1; matrix products, arithmetic and copies ran while one was open for 0% -> 0% of each run, Pallas kernels for 32% -> 31%
where the time goes in v13:
time: 21.3 us; the launch traced here: 21.1 us
  Pallas kernels  10.5 us (49%)
  starting transfers between devices  9.95 us (47%)
  waiting for transfers between devices  0.55 us (3%)
    all_to_all x1, starting transfers between devices, shards(): stats = lax.all_to_all(stats, AXES, 0, 0, tiled=True)  4.84 us
    pallas_call x1, Pallas kernels, shards(): pl.pallas_call(functools.partial(first_kernel, sizes), name='rates_twice'...  4.75 us
    ppermute x1, starting transfers between devices, shards(): even = lax.ppermute(even, AXES, swaps(0, count))  4.44 us
    pallas_call x1, Pallas kernels, shards(): pl.pallas_call(functools.partial(refine_kernel, sizes), name='sum_and_ref...  2.37 us
    pallas_call x1, Pallas kernels, shards(): pl.pallas_call(functools.partial(prep_kernel, sizes), name='lay_out', cos...  1.73 us
    pallas_call x1, Pallas kernels, shards(): pl.pallas_call(functools.partial(pack_kernel, sizes), name='pack', out_sh...  1.65 us
    ppermute x1, starting transfers between devices, shards(): odd = lax.ppermute(odd, AXES, swaps(1, count))  0.67 us
    all_to_all x1, waiting for transfers between devices, shards(): stats = lax.all_to_all(stats, AXES, 0, 0, tiled=True)  0.55 us
  transfers between devices with their start and end apart: 3, of which 1 were waited for; matrix products, arithmetic and copies ran while one was open for 0% of the time, Pallas kernels for 31%

profile of v13, /device:TPU:0, one launch (start us, length us, event | category | flops | bytes accessed | tf_op | source)
XLA Modules:
  0.0 21.1 jit_solution(3627450790069620808)
XLA Ops:
  0.0 1.7 %pack.1 = (f32[32,128]{1,0:T(8,128)}, f32[333,128]{1,0:T(8,128)S(1)}, f32[333,128]{1,0:T(8,128)S(1)}) custom-call(f32[10,3,4096]{2,1,0:T(4,128)} %bitcast.12, f32[32,128]{1,0:T(8,128)} %bitcast.14, f32[4,4096]{1,0:T(4,128)} %metric_hbm.3, s32[32,128]{1,0:T(8,128)} %bitcast.16, s32[32,128]{1,0:T(8,128)} %bitcast.18), custom_call_target="tpu_custom_call" | custom-call | tf_op jit(solution)/shard_map/pack/pallas_call | solution.py:510
  1.7 0.7 %collective-permute-start = (f32[333,128]{1,0:T(8,128)S(1)}, f32[333,128]{1,0:T(8,128)S(1)}, u32[]{:S(2)}, u32[]{:S(2)}) collective-permute-start(f32[333,128]{1,0:T(8,128)S(1)} %get-tuple-element.23), channel_id=1, source_target_pairs={{1,2},{3,4},{5,6},{7,8},{9,10},{11,12},{13,14},{15,16},{17,18},{19... | collective-permute-start | bytes 511496 | tf_op jit(solution)/shard_map/ppermute | solution.py:527
  2.3 4.4 %collective-permute-start.1 = (f32[333,128]{1,0:T(8,128)S(1)}, f32[333,128]{1,0:T(8,128)S(1)}, u32[]{:S(2)}, u32[]{:S(2)}) collective-permute-start(f32[333,128]{1,0:T(8,128)S(1)} %get-tuple-element.24), channel_id=1, source_target_pairs={{0,1},{2,3},{4,5},{6,7},{8,9},{10,11},{12,13},{14,15},{16,17},{18,... | collective-permute-start | bytes 511496 | tf_op jit(solution)/shard_map/ppermute | solution.py:528
  6.8 4.8 %all-to-all-start = ((f32[32,1,128]{2,1,0:T(1,128)}), f32[32,1,128]{2,1,0:T(1,128)S(1)}, u32[]{:S(2)}, u32[]{:S(2)}) async-start(f32[32,1,128]{2,1,0:T(1,128)} %bitcast.7), calls=%async_computation | async-start | bytes 32768 | tf_op jit(solution)/shard_map/all_to_all | solution.py:529
  11.6 1.7 %lay_out.1 = (f32[30,32,128]{2,1,0:T(8,128)S(1)}, f32[7,32,128]{2,1,0:T(8,128)S(1)}, bf16[120,96]{1,0:T(8,128)(2,1)S(1)}, f32[3,128]{1,0:T(4,128)S(1)}) custom-call(f32[10,3,4096]{2,1,0:T(4,128)} %bitcast.13, f32[32,128]{1,0:T(8,128)} %bitcast.15, f32[4,4096]{1,0:T(4,128)} %metric_hbm.3, s32[32,128]{1,0:T(8,128)} %bitcast.17, s32[32,128]{1,0:T(8,128)} %bitcast.19, ...), custom_call_target="tpu_custom_call" | custom-call | flops 16777216 | bytes 16777216 | tf_op jit(solution)/shard_map/lay_out/pallas_call | solution.py:531
  13.4 0.0 collective-permute-done.odd_ref
  13.4 0.0 collective-permute-done.1.even_ref
  13.4 4.8 %rates_twice.1 = (f32[30,72,128]{2,1,0:T(8,128)S(1)}, f32[30,72,128]{2,1,0:T(8,128)S(1)}, f32[30,48,128]{2,1,0:T(8,128)S(1)}, bf16[120,96]{1,0:T(8,128)(2,1)S(1)...) custom-call(f32[30,32,128]{2,1,0:T(8,128)S(1)} %get-tuple-element.19.cur_own, ...), custom_call_target="tpu_custom_call" | custom-call | flops 1024 | bytes 1024 | tf_op jit(solution)/shard_map/rates_twice/pallas_call | solution.py:555
  18.1 0.5 %all-to-all-done = f32[32,1,128]{2,1,0:T(1,128)S(1)} async-done(((f32[32,1,128]{2,1,0:T(1,128)}), f32[32,1,128]{2,1,0:T(1,128)S(1)}, u32[]{:S(2)}, u32[]{:S(2)}) %all-to-all-start) | async-done | bytes 16416 | tf_op jit(solution)/shard_map/all_to_all | solution.py:529
  18.7 2.4 %sum_and_refine.1 = f32[10,3,6144]{2,1,0:T(4,128)} custom-call(f32[30,72,128]{2,1,0:T(8,128)S(1)} %get-tuple-element.25.cur, f32[30,72,128]{2,1,0:T(8,128)S(1)} %get-tuple-element.26.rate_ref, f32[30,48,128]{2,1,0:T(8,128)S(1)} %get-tuple-element.27.twice_ref, bf16[120,96]{1,0:T(8,128)(2,1)S(1)} %get-tuple-element.28.weights, ...), custom_call_target="tpu_custom_call" | custom-call | tf_op jit(solution)/shard_map/sum_and_refine/pallas_call | solution.py:578
Async XLA Ops:
  1.7 11.7 %collective-permute-start = (f32[333,128]{1,0:T(8,128)S(1)}, f32[333,128]{1,0:T(8,128)S(1)}, u32[]{:S(2)}, u32[]{:S(2)}) collective-permute-start(f32[333,128]{1,0:T(8,128)S(1)} %get-tuple-element.23), channel_id=1, source_target_pairs={{1,2},{3,4},{5,6},{7,8},{9,10},{11,12},{13,14},{15,16},{17,18},{19... | collective-permute-start | bytes 511496 | tf_op jit(solution)/shard_map/ppermute | solution.py:527
  2.3 11.0 %collective-permute-start.1 = (f32[333,128]{1,0:T(8,128)S(1)}, f32[333,128]{1,0:T(8,128)S(1)}, u32[]{:S(2)}, u32[]{:S(2)}) collective-permute-start(f32[333,128]{1,0:T(8,128)S(1)} %get-tuple-element.24), channel_id=1, source_target_pairs={{0,1},{2,3},{4,5},{6,7},{8,9},{10,11},{12,13},{14,15},{16,17},{18,... | collective-permute-start | bytes 511496 | tf_op jit(solution)/shard_map/ppermute | solution.py:528
  6.8 11.9 %all-to-all-start = ((f32[32,1,128]{2,1,0:T(1,128)}), f32[32,1,128]{2,1,0:T(1,128)S(1)}, u32[]{:S(2)}, u32[]{:S(2)}) async-start(f32[32,1,128]{2,1,0:T(1,128)} %bitcast.7), calls=%async_computation | async-start | bytes 32768 | tf_op jit(solution)/shard_map/all_to_all | solution.py:529

commit v14 on v13

--- a/solution.py
+++ b/solution.py
@@ -77,9 +77,9 @@
     depth = depth_ref[...]
     refine = refine_ref[...].astype(jnp.float32)
     faces = ((sx, sy), (rx + sx, ry + sy), (rx, ry))
-    lengths = [jnp.sqrt(vx * vx + vy * vy) for vx, vy in faces]
-    rate = jnp.sqrt(GRAVITY * depth) * jnp.maximum(jnp.maximum(lengths[0], lengths[1]), lengths[2])
-    top = jnp.max(jnp.max(rate, axis=0, keepdims=True), axis=1, keepdims=True)
+    squares = [vx * vx + vy * vy for vx, vy in faces]
+    rate = (GRAVITY * depth) * jnp.maximum(jnp.maximum(squares[0], squares[1]), squares[2])
+    top = jnp.sqrt(jnp.max(jnp.max(rate, axis=0, keepdims=True), axis=1, keepdims=True))
     extra = jnp.sum(jnp.sum(refine, axis=0, keepdims=True), axis=1, keepdims=True)
     shape = stats_ref.shape
     lane = lax.broadcasted_iota(jnp.int32, shape, 1)
@@ -102,10 +102,11 @@
 
 
 def pack_state(source, target, blocks, height, width):
+    zero = jnp.minimum(lax.axis_index(AXES), 0)
     for block in range(blocks):
         for node in range(10):
-            at = height * block + width * node
-            target[at : at + 3, :] = source[node, :, LANES * block : LANES * (block + 1)]
+            at = zero + (height * block + width * node)
+            target[pl.ds(at, 3), :] = source[node, :, LANES * block : LANES * (block + 1)]
 
 
 def pair_index(partner):
@@ -447,7 +448,7 @@
     copy.wait()
     matrix = weights[...]
     results = []
-    parts = [(at, 8) for at in range(0, slots - 8, 8)] + [(slots - 8, 4), (slots - 4, 4)]
+    parts = [(at, 4) for at in range(0, slots, 4)]
     for part, (begin_at, height) in enumerate(parts):
         span = slice(LANES * begin_at, LANES * (begin_at + height))
         columns = []
@@ -587,7 +588,7 @@
             pltpu.SMEM((1, LANES), i32),
             pltpu.VMEM((STEP * (slots + 1), LANES), f32),
             pltpu.VMEM((3, slots, LANES), f32),
-            pltpu.SemaphoreType.DMA((slots // 8 + 1,)),
+            pltpu.SemaphoreType.DMA((slots // 4,)),
             pltpu.SemaphoreType.DMA,
         ],
         compiler_params=PARAMS,

time: 21.3 us -> 21.4 us (level)
  no operation moved by 1% of the time
where the time goes in v14:
time: 21.4 us; the launch traced here: 21.1 us
  Pallas kernels  10.5 us (49%)
  starting transfers between devices  9.95 us (46%)
  waiting for transfers between devices  0.55 us (3%)
    all_to_all x1, starting transfers between devices, shards(): stats = lax.all_to_all(stats, AXES, 0, 0, tiled=True)  4.84 us
    pallas_call x1, Pallas kernels, shards(): pl.pallas_call(functools.partial(first_kernel, sizes), name='rates_twice'...  4.75 us
    ppermute x1, starting transfers between devices, shards(): even = lax.ppermute(even, AXES, swaps(0, count))  4.44 us
    pallas_call x1, Pallas kernels, shards(): pl.pallas_call(functools.partial(refine_kernel, sizes), name='sum_and_ref...  2.42 us
    pallas_call x1, Pallas kernels, shards(): pl.pallas_call(functools.partial(prep_kernel, sizes), name='lay_out', cos...  1.73 us
    pallas_call x1, Pallas kernels, shards(): pl.pallas_call(functools.partial(pack_kernel, sizes), name='pack', out_sh...  1.64 us
    ppermute x1, starting transfers between devices, shards(): odd = lax.ppermute(odd, AXES, swaps(1, count))  0.67 us
    all_to_all x1, waiting for transfers between devices, shards(): stats = lax.all_to_all(stats, AXES, 0, 0, tiled=True)  0.55 us
  transfers between devices with their start and end apart: 3, of which 1 were waited for; matrix products, arithmetic and copies ran while one was open for 0% of the time, Pallas kernels for 31%

profile of v14, /device:TPU:0, one launch (start us, length us, event | category | flops | bytes accessed | tf_op | source)
XLA Modules:
  0.0 21.1 jit_solution(16493902974922689185)
XLA Ops:
  0.0 1.6 %pack.1 = (f32[32,128]{1,0:T(8,128)}, f32[333,128]{1,0:T(8,128)S(1)}, f32[333,128]{1,0:T(8,128)S(1)}) custom-call(f32[10,3,4096]{2,1,0:T(4,128)} %bitcast.12, f32[32,128]{1,0:T(8,128)} %bitcast.14, f32[4,4096]{1,0:T(4,128)} %metric_hbm.3, s32[32,128]{1,0:T(8,128)} %bitcast.16, s32[32,128]{1,0:T(8,128)} %bitcast.18), custom_call_target="tpu_custom_call" | custom-call | tf_op jit(solution)/shard_map/pack/pallas_call | solution.py:511
  1.7 0.7 %collective-permute-start = (f32[333,128]{1,0:T(8,128)S(1)}, f32[333,128]{1,0:T(8,128)S(1)}, u32[]{:S(2)}, u32[]{:S(2)}) collective-permute-start(f32[333,128]{1,0:T(8,128)S(1)} %get-tuple-element.23), channel_id=1, source_target_pairs={{1,2},{3,4},{5,6},{7,8},{9,10},{11,12},{13,14},{15,16},{17,18},{19... | collective-permute-start | bytes 511496 | tf_op jit(solution)/shard_map/ppermute | solution.py:528
  2.3 4.4 %collective-permute-start.1 = (f32[333,128]{1,0:T(8,128)S(1)}, f32[333,128]{1,0:T(8,128)S(1)}, u32[]{:S(2)}, u32[]{:S(2)}) collective-permute-start(f32[333,128]{1,0:T(8,128)S(1)} %get-tuple-element.24), channel_id=1, source_target_pairs={{0,1},{2,3},{4,5},{6,7},{8,9},{10,11},{12,13},{14,15},{16,17},{18,... | collective-permute-start | bytes 511496 | tf_op jit(solution)/shard_map/ppermute | solution.py:529
  6.8 4.8 %all-to-all-start = ((f32[32,1,128]{2,1,0:T(1,128)}), f32[32,1,128]{2,1,0:T(1,128)S(1)}, u32[]{:S(2)}, u32[]{:S(2)}) async-start(f32[32,1,128]{2,1,0:T(1,128)} %bitcast.7), calls=%async_computation | async-start | bytes 32768 | tf_op jit(solution)/shard_map/all_to_all | solution.py:530
  11.6 1.7 %lay_out.1 = (f32[30,32,128]{2,1,0:T(8,128)S(1)}, f32[7,32,128]{2,1,0:T(8,128)S(1)}, bf16[120,96]{1,0:T(8,128)(2,1)S(1)}, f32[3,128]{1,0:T(4,128)S(1)}) custom-call(f32[10,3,4096]{2,1,0:T(4,128)} %bitcast.13, f32[32,128]{1,0:T(8,128)} %bitcast.15, f32[4,4096]{1,0:T(4,128)} %metric_hbm.3, s32[32,128]{1,0:T(8,128)} %bitcast.17, s32[32,128]{1,0:T(8,128)} %bitcast.19, ...), custom_call_target="tpu_custom_call" | custom-call | flops 16777216 | bytes 16777216 | tf_op jit(solution)/shard_map/lay_out/pallas_call | solution.py:532
  13.4 0.0 collective-permute-done.odd_ref
  13.4 0.0 collective-permute-done.1.even_ref
  13.4 4.8 %rates_twice.1 = (f32[30,72,128]{2,1,0:T(8,128)S(1)}, f32[30,72,128]{2,1,0:T(8,128)S(1)}, f32[30,48,128]{2,1,0:T(8,128)S(1)}, bf16[120,96]{1,0:T(8,128)(2,1)S(1)...) custom-call(f32[30,32,128]{2,1,0:T(8,128)S(1)} %get-tuple-element.19.cur_own, ...), custom_call_target="tpu_custom_call" | custom-call | flops 1024 | bytes 1024 | tf_op jit(solution)/shard_map/rates_twice/pallas_call | solution.py:556
  18.1 0.5 %all-to-all-done = f32[32,1,128]{2,1,0:T(1,128)S(1)} async-done(((f32[32,1,128]{2,1,0:T(1,128)}), f32[32,1,128]{2,1,0:T(1,128)S(1)}, u32[]{:S(2)}, u32[]{:S(2)}) %all-to-all-start) | async-done | bytes 16416 | tf_op jit(solution)/shard_map/all_to_all | solution.py:530
  18.7 2.4 %sum_and_refine.1 = f32[10,3,6144]{2,1,0:T(4,128)} custom-call(f32[30,72,128]{2,1,0:T(8,128)S(1)} %get-tuple-element.25.cur, f32[30,72,128]{2,1,0:T(8,128)S(1)} %get-tuple-element.26.rate_ref, f32[30,48,128]{2,1,0:T(8,128)S(1)} %get-tuple-element.27.twice_ref, bf16[120,96]{1,0:T(8,128)(2,1)S(1)} %get-tuple-element.28.weights, ...), custom_call_target="tpu_custom_call" | custom-call | tf_op jit(solution)/shard_map/sum_and_refine/pallas_call | solution.py:579
Async XLA Ops:
  1.7 11.7 %collective-permute-start = (f32[333,128]{1,0:T(8,128)S(1)}, f32[333,128]{1,0:T(8,128)S(1)}, u32[]{:S(2)}, u32[]{:S(2)}) collective-permute-start(f32[333,128]{1,0:T(8,128)S(1)} %get-tuple-element.23), channel_id=1, source_target_pairs={{1,2},{3,4},{5,6},{7,8},{9,10},{11,12},{13,14},{15,16},{17,18},{19... | collective-permute-start | bytes 511496 | tf_op jit(solution)/shard_map/ppermute | solution.py:528
  2.3 11.0 %collective-permute-start.1 = (f32[333,128]{1,0:T(8,128)S(1)}, f32[333,128]{1,0:T(8,128)S(1)}, u32[]{:S(2)}, u32[]{:S(2)}) collective-permute-start(f32[333,128]{1,0:T(8,128)S(1)} %get-tuple-element.24), channel_id=1, source_target_pairs={{0,1},{2,3},{4,5},{6,7},{8,9},{10,11},{12,13},{14,15},{16,17},{18,... | collective-permute-start | bytes 511496 | tf_op jit(solution)/shard_map/ppermute | solution.py:529
  6.8 11.9 %all-to-all-start = ((f32[32,1,128]{2,1,0:T(1,128)}), f32[32,1,128]{2,1,0:T(1,128)S(1)}, u32[]{:S(2)}, u32[]{:S(2)}) async-start(f32[32,1,128]{2,1,0:T(1,128)} %bitcast.7), calls=%async_computation | async-start | bytes 32768 | tf_op jit(solution)/shard_map/all_to_all | solution.py:530

commit v15 on v13

--- a/solution.py
+++ b/solution.py
@@ -17,7 +17,6 @@
 LAID = 41
 SENT = 37
 WIDE = 32
-STEP = 33
 TALL = 16
 PAD = 8
 
@@ -407,12 +406,16 @@
     place_v[...] = lead
     copy = pltpu.make_async_copy(place_v, place_s, sem)
     copy.start()
-    for item in range(30):
-        now = pl.ds(zero + (PAD + keep), slots)
-        value = cur[item, now, :] + step * rate_ref[item, now, :] + half_square * twice_ref[item]
-        wide[pl.ds(item, slots, stride=STEP), :] = value
-    for item in (30, 31):
-        wide[pl.ds(item, slots + 1, stride=STEP), :] = jnp.zeros((slots + 1, LANES), jnp.float32)
+    now = pl.ds(zero + (PAD + keep), slots)
+    for first in range(0, WIDE, 8):
+        values = []
+        for item in range(first, first + 8):
+            if item < 30:
+                once = cur[item, now, :] + step * rate_ref[item, now, :]
+                values.append(once + half_square * twice_ref[item])
+            else:
+                values.append(jnp.zeros((slots, LANES), jnp.float32))
+        wide[:slots, first : first + 8, :] = jnp.swapaxes(jnp.stack(values, axis=0), 0, 1)
     slot_start = LANES * lax.broadcasted_iota(jnp.int32, (slots, LANES), 0).astype(jnp.float32)
     begun = [lines_ref[num, 0:1, :] + start <= slot_start for num in range(3)]
     halves = [
@@ -452,13 +455,13 @@
         span = slice(LANES * begin_at, LANES * (begin_at + height))
         columns = []
         for slot in range(begin_at, begin_at + height):
-            lead_at = place_s[0, slot] * STEP
+            lead_at = place_s[0, slot]
             lane_idx = jnp.broadcast_to(index_ref[0, slot : slot + 1, :], (8, LANES)).astype(jnp.int32)
             ahead = jnp.broadcast_to(index_ref[2, slot : slot + 1, :], (8, LANES)) > 0.5
             tiles = []
             for row in range(0, WIDE, 8):
-                one = wide[pl.ds(lead_at + row, 8), :]
-                two = wide[pl.ds(lead_at + STEP + row, 8), :]
+                one = wide[lead_at, row : row + 8, :]
+                two = wide[lead_at + 1, row : row + 8, :]
                 tiles.append(lane_gather(jnp.where(ahead, two, one), lane_idx))
             columns.append(jnp.concatenate(tiles, axis=0))
         values = jnp.concatenate(columns, axis=1)
@@ -585,7 +588,7 @@
             pltpu.VMEM((10, 3, LANES * slots), f32),
             pltpu.VMEM((1, LANES), i32),
             pltpu.SMEM((1, LANES), i32),
-            pltpu.VMEM((STEP * (slots + 1), LANES), f32),
+            pltpu.VMEM((slots + 1, WIDE, LANES), f32),
             pltpu.VMEM((3, slots, LANES), f32),
             pltpu.SemaphoreType.DMA((slots // 8 + 1,)),
             pltpu.SemaphoreType.DMA,

time: 21.3 us -> 21.4 us (level)
  no operation moved by 1% of the time
where the time goes in v15:
time: 21.4 us; the launch traced here: 21.1 us
  Pallas kernels  10.6 us (50%)
  starting transfers between devices  9.95 us (46%)
  waiting for transfers between devices  0.55 us (3%)
    all_to_all x1, starting transfers between devices, shards(): stats = lax.all_to_all(stats, AXES, 0, 0, tiled=True)  4.84 us
    pallas_call x1, Pallas kernels, shards(): pl.pallas_call(functools.partial(first_kernel, sizes), name='rates_twice'...  4.75 us
    ppermute x1, starting transfers between devices, shards(): even = lax.ppermute(even, AXES, swaps(0, count))  4.44 us
    pallas_call x1, Pallas kernels, shards(): pl.pallas_call(functools.partial(refine_kernel, sizes), name='sum_and_ref...  2.45 us
    pallas_call x1, Pallas kernels, shards(): pl.pallas_call(functools.partial(prep_kernel, sizes), name='lay_out', cos...  1.73 us
    pallas_call x1, Pallas kernels, shards(): pl.pallas_call(functools.partial(pack_kernel, sizes), name='pack', out_sh...  1.65 us
    ppermute x1, starting transfers between devices, shards(): odd = lax.ppermute(odd, AXES, swaps(1, count))  0.67 us
    all_to_all x1, waiting for transfers between devices, shards(): stats = lax.all_to_all(stats, AXES, 0, 0, tiled=True)  0.55 us
  transfers between devices with their start and end apart: 3, of which 1 were waited for; matrix products, arithmetic and copies ran while one was open for 0% of the time, Pallas kernels for 31%

profile of v15, /device:TPU:0, one launch (start us, length us, event | category | flops | bytes accessed | tf_op | source)
XLA Modules:
  0.0 21.1 jit_solution(12812260470717734957)
XLA Ops:
  0.0 1.7 %pack.1 = (f32[32,128]{1,0:T(8,128)}, f32[333,128]{1,0:T(8,128)S(1)}, f32[333,128]{1,0:T(8,128)S(1)}) custom-call(f32[10,3,4096]{2,1,0:T(4,128)} %bitcast.12, f32[32,128]{1,0:T(8,128)} %bitcast.14, f32[4,4096]{1,0:T(4,128)} %metric_hbm.3, s32[32,128]{1,0:T(8,128)} %bitcast.16, s32[32,128]{1,0:T(8,128)} %bitcast.18), custom_call_target="tpu_custom_call" | custom-call | tf_op jit(solution)/shard_map/pack/pallas_call | solution.py:513
  1.7 0.7 %collective-permute-start = (f32[333,128]{1,0:T(8,128)S(1)}, f32[333,128]{1,0:T(8,128)S(1)}, u32[]{:S(2)}, u32[]{:S(2)}) collective-permute-start(f32[333,128]{1,0:T(8,128)S(1)} %get-tuple-element.23), channel_id=1, source_target_pairs={{1,2},{3,4},{5,6},{7,8},{9,10},{11,12},{13,14},{15,16},{17,18},{19... | collective-permute-start | bytes 511496 | tf_op jit(solution)/shard_map/ppermute | solution.py:530
  2.3 4.4 %collective-permute-start.1 = (f32[333,128]{1,0:T(8,128)S(1)}, f32[333,128]{1,0:T(8,128)S(1)}, u32[]{:S(2)}, u32[]{:S(2)}) collective-permute-start(f32[333,128]{1,0:T(8,128)S(1)} %get-tuple-element.24), channel_id=1, source_target_pairs={{0,1},{2,3},{4,5},{6,7},{8,9},{10,11},{12,13},{14,15},{16,17},{18,... | collective-permute-start | bytes 511496 | tf_op jit(solution)/shard_map/ppermute | solution.py:531
  6.8 4.8 %all-to-all-start = ((f32[32,1,128]{2,1,0:T(1,128)}), f32[32,1,128]{2,1,0:T(1,128)S(1)}, u32[]{:S(2)}, u32[]{:S(2)}) async-start(f32[32,1,128]{2,1,0:T(1,128)} %bitcast.7), calls=%async_computation | async-start | bytes 32768 | tf_op jit(solution)/shard_map/all_to_all | solution.py:532
  11.6 1.7 %lay_out.1 = (f32[30,32,128]{2,1,0:T(8,128)S(1)}, f32[7,32,128]{2,1,0:T(8,128)S(1)}, bf16[120,96]{1,0:T(8,128)(2,1)S(1)}, f32[3,128]{1,0:T(4,128)S(1)}) custom-call(f32[10,3,4096]{2,1,0:T(4,128)} %bitcast.13, f32[32,128]{1,0:T(8,128)} %bitcast.15, f32[4,4096]{1,0:T(4,128)} %metric_hbm.3, s32[32,128]{1,0:T(8,128)} %bitcast.17, s32[32,128]{1,0:T(8,128)} %bitcast.19, ...), custom_call_target="tpu_custom_call" | custom-call | flops 16777216 | bytes 16777216 | tf_op jit(solution)/shard_map/lay_out/pallas_call | solution.py:534
  13.4 0.0 collective-permute-done.odd_ref
  13.4 0.0 collective-permute-done.1.even_ref
  13.4 4.8 %rates_twice.1 = (f32[30,72,128]{2,1,0:T(8,128)S(1)}, f32[30,72,128]{2,1,0:T(8,128)S(1)}, f32[30,48,128]{2,1,0:T(8,128)S(1)}, bf16[120,96]{1,0:T(8,128)(2,1)S(1)...) custom-call(f32[30,32,128]{2,1,0:T(8,128)S(1)} %get-tuple-element.19.cur_own, ...), custom_call_target="tpu_custom_call" | custom-call | flops 1024 | bytes 1024 | tf_op jit(solution)/shard_map/rates_twice/pallas_call | solution.py:558
  18.1 0.5 %all-to-all-done = f32[32,1,128]{2,1,0:T(1,128)S(1)} async-done(((f32[32,1,128]{2,1,0:T(1,128)}), f32[32,1,128]{2,1,0:T(1,128)S(1)}, u32[]{:S(2)}, u32[]{:S(2)}) %all-to-all-start) | async-done | bytes 16416 | tf_op jit(solution)/shard_map/all_to_all | solution.py:532
  18.7 2.5 %sum_and_refine.1 = f32[10,3,6144]{2,1,0:T(4,128)} custom-call(f32[30,72,128]{2,1,0:T(8,128)S(1)} %get-tuple-element.25.cur, f32[30,72,128]{2,1,0:T(8,128)S(1)} %get-tuple-element.26.rate_ref, f32[30,48,128]{2,1,0:T(8,128)S(1)} %get-tuple-element.27.twice_ref, bf16[120,96]{1,0:T(8,128)(2,1)S(1)} %get-tuple-element.28.weights, ...), custom_call_target="tpu_custom_call" | custom-call | tf_op jit(solution)/shard_map/sum_and_refine/pallas_call | solution.py:581
Async XLA Ops:
  1.7 11.7 %collective-permute-start = (f32[333,128]{1,0:T(8,128)S(1)}, f32[333,128]{1,0:T(8,128)S(1)}, u32[]{:S(2)}, u32[]{:S(2)}) collective-permute-start(f32[333,128]{1,0:T(8,128)S(1)} %get-tuple-element.23), channel_id=1, source_target_pairs={{1,2},{3,4},{5,6},{7,8},{9,10},{11,12},{13,14},{15,16},{17,18},{19... | collective-permute-start | bytes 511496 | tf_op jit(solution)/shard_map/ppermute | solution.py:530
  2.3 11.0 %collective-permute-start.1 = (f32[333,128]{1,0:T(8,128)S(1)}, f32[333,128]{1,0:T(8,128)S(1)}, u32[]{:S(2)}, u32[]{:S(2)}) collective-permute-start(f32[333,128]{1,0:T(8,128)S(1)} %get-tuple-element.24), channel_id=1, source_target_pairs={{0,1},{2,3},{4,5},{6,7},{8,9},{10,11},{12,13},{14,15},{16,17},{18,... | collective-permute-start | bytes 511496 | tf_op jit(solution)/shard_map/ppermute | solution.py:531
  6.8 11.9 %all-to-all-start = ((f32[32,1,128]{2,1,0:T(1,128)}), f32[32,1,128]{2,1,0:T(1,128)S(1)}, u32[]{:S(2)}, u32[]{:S(2)}) async-start(f32[32,1,128]{2,1,0:T(1,128)} %bitcast.7), calls=%async_computation | async-start | bytes 32768 | tf_op jit(solution)/shard_map/all_to_all | solution.py:532

commit v16 on v13

--- a/solution.py
+++ b/solution.py
@@ -433,10 +433,9 @@
         return jnp.where(beyond, lane_gather(far, index), lane_gather(near, index))
 
     found = jnp.zeros((slots, LANES), jnp.int32)
-    for size in (LANES // 4, LANES // 16, LANES // 64):
-        passed = [(pick(found + (probe * size - 1)) <= goal).astype(jnp.int32) for probe in (1, 2, 3)]
-        found = found + size * (passed[0] + passed[1] + passed[2])
-    found = found + (pick(found) <= goal).astype(jnp.int32)
+    for ways, size in ((8, LANES // 8), (4, LANES // 32), (4, LANES // 128)):
+        passed = [(pick(found + (probe * size - 1)) <= goal).astype(jnp.int32) for probe in range(1, ways)]
+        found = found + size * sum(passed)
     mine = pick(found).astype(jnp.int32)
     split = mine & 1
     begin = (mine >> 1) - 1 - split
@@ -447,7 +446,8 @@
     copy.wait()
     matrix = weights[...]
     results = []
-    parts = [(at, 8) for at in range(0, slots - 8, 8)] + [(slots - 8, 4), (slots - 4, 4)]
+    parts = [(at, 16) for at in range(0, slots - 16, 16)]
+    parts += [(slots - 16, 8), (slots - 8, 4), (slots - 4, 4)]
     for part, (begin_at, height) in enumerate(parts):
         span = slice(LANES * begin_at, LANES * (begin_at + height))
         columns = []

time: 21.3 us -> 21.3 us (level)
  no operation moved by 1% of the time
where the time goes in v16:
time: 21.3 us; the launch traced here: 21 us
  Pallas kernels  10.5 us (49%)
  starting transfers between devices  9.95 us (47%)
  waiting for transfers between devices  0.55 us (3%)
    all_to_all x1, starting transfers between devices, shards(): stats = lax.all_to_all(stats, AXES, 0, 0, tiled=True)  4.84 us
    pallas_call x1, Pallas kernels, shards(): pl.pallas_call(functools.partial(first_kernel, sizes), name='rates_twice'...  4.75 us
    ppermute x1, starting transfers between devices, shards(): even = lax.ppermute(even, AXES, swaps(0, count))  4.44 us
    pallas_call x1, Pallas kernels, shards(): pl.pallas_call(functools.partial(refine_kernel, sizes), name='sum_and_ref...  2.33 us
    pallas_call x1, Pallas kernels, shards(): pl.pallas_call(functools.partial(prep_kernel, sizes), name='lay_out', cos...  1.73 us
    pallas_call x1, Pallas kernels, shards(): pl.pallas_call(functools.partial(pack_kernel, sizes), name='pack', out_sh...  1.65 us
    ppermute x1, starting transfers between devices, shards(): odd = lax.ppermute(odd, AXES, swaps(1, count))  0.67 us
    all_to_all x1, waiting for transfers between devices, shards(): stats = lax.all_to_all(stats, AXES, 0, 0, tiled=True)  0.55 us
  transfers between devices with their start and end apart: 3, of which 1 were waited for; matrix products, arithmetic and copies ran while one was open for 0% of the time, Pallas kernels for 31%

profile of v16, /device:TPU:0, one launch (start us, length us, event | category | flops | bytes accessed | tf_op | source)
XLA Modules:
  0.0 21.0 jit_solution(6439687805393463237)
XLA Ops:
  0.0 1.7 %pack.1 = (f32[32,128]{1,0:T(8,128)}, f32[333,128]{1,0:T(8,128)S(1)}, f32[333,128]{1,0:T(8,128)S(1)}) custom-call(f32[10,3,4096]{2,1,0:T(4,128)} %bitcast.12, f32[32,128]{1,0:T(8,128)} %bitcast.14, f32[4,4096]{1,0:T(4,128)} %metric_hbm.3, s32[32,128]{1,0:T(8,128)} %bitcast.16, s32[32,128]{1,0:T(8,128)} %bitcast.18), custom_call_target="tpu_custom_call" | custom-call | tf_op jit(solution)/shard_map/pack/pallas_call | solution.py:510
  1.7 0.7 %collective-permute-start = (f32[333,128]{1,0:T(8,128)S(1)}, f32[333,128]{1,0:T(8,128)S(1)}, u32[]{:S(2)}, u32[]{:S(2)}) collective-permute-start(f32[333,128]{1,0:T(8,128)S(1)} %get-tuple-element.23), channel_id=1, source_target_pairs={{1,2},{3,4},{5,6},{7,8},{9,10},{11,12},{13,14},{15,16},{17,18},{19... | collective-permute-start | bytes 511496 | tf_op jit(solution)/shard_map/ppermute | solution.py:527
  2.3 4.4 %collective-permute-start.1 = (f32[333,128]{1,0:T(8,128)S(1)}, f32[333,128]{1,0:T(8,128)S(1)}, u32[]{:S(2)}, u32[]{:S(2)}) collective-permute-start(f32[333,128]{1,0:T(8,128)S(1)} %get-tuple-element.24), channel_id=1, source_target_pairs={{0,1},{2,3},{4,5},{6,7},{8,9},{10,11},{12,13},{14,15},{16,17},{18,... | collective-permute-start | bytes 511496 | tf_op jit(solution)/shard_map/ppermute | solution.py:528
  6.8 4.8 %all-to-all-start = ((f32[32,1,128]{2,1,0:T(1,128)}), f32[32,1,128]{2,1,0:T(1,128)S(1)}, u32[]{:S(2)}, u32[]{:S(2)}) async-start(f32[32,1,128]{2,1,0:T(1,128)} %bitcast.7), calls=%async_computation | async-start | bytes 32768 | tf_op jit(solution)/shard_map/all_to_all | solution.py:529
  11.6 1.7 %lay_out.1 = (f32[30,32,128]{2,1,0:T(8,128)S(1)}, f32[7,32,128]{2,1,0:T(8,128)S(1)}, bf16[120,96]{1,0:T(8,128)(2,1)S(1)}, f32[3,128]{1,0:T(4,128)S(1)}) custom-call(f32[10,3,4096]{2,1,0:T(4,128)} %bitcast.13, f32[32,128]{1,0:T(8,128)} %bitcast.15, f32[4,4096]{1,0:T(4,128)} %metric_hbm.3, s32[32,128]{1,0:T(8,128)} %bitcast.17, s32[32,128]{1,0:T(8,128)} %bitcast.19, ...), custom_call_target="tpu_custom_call" | custom-call | flops 16777216 | bytes 16777216 | tf_op jit(solution)/shard_map/lay_out/pallas_call | solution.py:531
  13.4 0.0 collective-permute-done.odd_ref
  13.4 0.0 collective-permute-done.1.even_ref
  13.4 4.8 %rates_twice.1 = (f32[30,72,128]{2,1,0:T(8,128)S(1)}, f32[30,72,128]{2,1,0:T(8,128)S(1)}, f32[30,48,128]{2,1,0:T(8,128)S(1)}, bf16[120,96]{1,0:T(8,128)(2,1)S(1)...) custom-call(f32[30,32,128]{2,1,0:T(8,128)S(1)} %get-tuple-element.19.cur_own, ...), custom_call_target="tpu_custom_call" | custom-call | flops 1024 | bytes 1024 | tf_op jit(solution)/shard_map/rates_twice/pallas_call | solution.py:555
  18.1 0.5 %all-to-all-done = f32[32,1,128]{2,1,0:T(1,128)S(1)} async-done(((f32[32,1,128]{2,1,0:T(1,128)}), f32[32,1,128]{2,1,0:T(1,128)S(1)}, u32[]{:S(2)}, u32[]{:S(2)}) %all-to-all-start) | async-done | bytes 16416 | tf_op jit(solution)/shard_map/all_to_all | solution.py:529
  18.7 2.3 %sum_and_refine.1 = f32[10,3,6144]{2,1,0:T(4,128)} custom-call(f32[30,72,128]{2,1,0:T(8,128)S(1)} %get-tuple-element.25.cur, f32[30,72,128]{2,1,0:T(8,128)S(1)} %get-tuple-element.26.rate_ref, f32[30,48,128]{2,1,0:T(8,128)S(1)} %get-tuple-element.27.twice_ref, bf16[120,96]{1,0:T(8,128)(2,1)S(1)} %get-tuple-element.28.weights, ...), custom_call_target="tpu_custom_call" | custom-call | tf_op jit(solution)/shard_map/sum_and_refine/pallas_call | solution.py:578
Async XLA Ops:
  1.7 11.7 %collective-permute-start = (f32[333,128]{1,0:T(8,128)S(1)}, f32[333,128]{1,0:T(8,128)S(1)}, u32[]{:S(2)}, u32[]{:S(2)}) collective-permute-start(f32[333,128]{1,0:T(8,128)S(1)} %get-tuple-element.23), channel_id=1, source_target_pairs={{1,2},{3,4},{5,6},{7,8},{9,10},{11,12},{13,14},{15,16},{17,18},{19... | collective-permute-start | bytes 511496 | tf_op jit(solution)/shard_map/ppermute | solution.py:527
  2.3 11.0 %collective-permute-start.1 = (f32[333,128]{1,0:T(8,128)S(1)}, f32[333,128]{1,0:T(8,128)S(1)}, u32[]{:S(2)}, u32[]{:S(2)}) collective-permute-start(f32[333,128]{1,0:T(8,128)S(1)} %get-tuple-element.24), channel_id=1, source_target_pairs={{0,1},{2,3},{4,5},{6,7},{8,9},{10,11},{12,13},{14,15},{16,17},{18,... | collective-permute-start | bytes 511496 | tf_op jit(solution)/shard_map/ppermute | solution.py:528
  6.8 11.9 %all-to-all-start = ((f32[32,1,128]{2,1,0:T(1,128)}), f32[32,1,128]{2,1,0:T(1,128)S(1)}, u32[]{:S(2)}, u32[]{:S(2)}) async-start(f32[32,1,128]{2,1,0:T(1,128)} %bitcast.7), calls=%async_computation | async-start | bytes 32768 | tf_op jit(solution)/shard_map/all_to_all | solution.py:529

commit v17 on v16

--- a/solution.py
+++ b/solution.py
@@ -469,14 +469,14 @@
         for sub in range(height):
             slot = begin_at + sub
             cut = slice(LANES * sub, LANES * (sub + 1))
-            tag = jnp.broadcast_to(index_ref[1, slot : slot + 1, :], (PACK, LANES))
-            value = jnp.where(
-                tag < 0.5,
-                children[2 * PACK :, cut],
-                jnp.where(tag < 1.5, children[:PACK, cut], children[PACK : 2 * PACK, cut]),
-            )
-            for node in range(10):
-                out_ref[node, :, LANES * slot : LANES * (slot + 1)] = value[4 * node : 4 * node + 3]
+            tag = jnp.broadcast_to(index_ref[1, slot : slot + 1, :], (8, LANES))
+            plain, earlier_child = tag < 0.5, tag < 1.5
+            for row in range(0, PACK, 8):
+                one, two, copied = [children[PACK * k + row : PACK * k + row + 8, cut] for k in range(3)]
+                value = jnp.where(plain, copied, jnp.where(earlier_child, one, two))
+                for half_row in range(2):
+                    node = row // 4 + half_row
+                    out_ref[node, :, LANES * slot : LANES * (slot + 1)] = value[4 * half_row : 4 * half_row + 3]
         result = pltpu.make_async_copy(out_ref.at[:, :, span], out_hbm.at[:, :, span], out_sems.at[part])
         result.start()
         results.append(result)

time: 21.3 us -> 21.3 us (level)
  no operation moved by 1% of the time
where the time goes in v17:
time: 21.3 us; the launch traced here: 21 us
  Pallas kernels  10.5 us (49%)
  starting transfers between devices  9.95 us (47%)
  waiting for transfers between devices  0.55 us (3%)
    all_to_all x1, starting transfers between devices, shards(): stats = lax.all_to_all(stats, AXES, 0, 0, tiled=True)  4.84 us
    pallas_call x1, Pallas kernels, shards(): pl.pallas_call(functools.partial(first_kernel, sizes), name='rates_twice'...  4.75 us
    ppermute x1, starting transfers between devices, shards(): even = lax.ppermute(even, AXES, swaps(0, count))  4.44 us
    pallas_call x1, Pallas kernels, shards(): pl.pallas_call(functools.partial(refine_kernel, sizes), name='sum_and_ref...  2.33 us
    pallas_call x1, Pallas kernels, shards(): pl.pallas_call(functools.partial(prep_kernel, sizes), name='lay_out', cos...  1.73 us
    pallas_call x1, Pallas kernels, shards(): pl.pallas_call(functools.partial(pack_kernel, sizes), name='pack', out_sh...  1.65 us
    ppermute x1, starting transfers between devices, shards(): odd = lax.ppermute(odd, AXES, swaps(1, count))  0.67 us
    all_to_all x1, waiting for transfers between devices, shards(): stats = lax.all_to_all(stats, AXES, 0, 0, tiled=True)  0.55 us
  transfers between devices with their start and end apart: 3, of which 1 were waited for; matrix products, arithmetic and copies ran while one was open for 0% of the time, Pallas kernels for 31%

profile of v17, /device:TPU:0, one launch (start us, length us, event | category | flops | bytes accessed | tf_op | source)
XLA Modules:
  0.0 21.0 jit_solution(6439687805393463237)
XLA Ops:
  0.0 1.7 %pack.1 = (f32[32,128]{1,0:T(8,128)}, f32[333,128]{1,0:T(8,128)S(1)}, f32[333,128]{1,0:T(8,128)S(1)}) custom-call(f32[10,3,4096]{2,1,0:T(4,128)} %bitcast.12, f32[32,128]{1,0:T(8,128)} %bitcast.14, f32[4,4096]{1,0:T(4,128)} %metric_hbm.3, s32[32,128]{1,0:T(8,128)} %bitcast.16, s32[32,128]{1,0:T(8,128)} %bitcast.18), custom_call_target="tpu_custom_call" | custom-call | tf_op jit(solution)/shard_map/pack/pallas_call | solution.py:510
  1.7 0.7 %collective-permute-start = (f32[333,128]{1,0:T(8,128)S(1)}, f32[333,128]{1,0:T(8,128)S(1)}, u32[]{:S(2)}, u32[]{:S(2)}) collective-permute-start(f32[333,128]{1,0:T(8,128)S(1)} %get-tuple-element.23), channel_id=1, source_target_pairs={{1,2},{3,4},{5,6},{7,8},{9,10},{11,12},{13,14},{15,16},{17,18},{19... | collective-permute-start | bytes 511496 | tf_op jit(solution)/shard_map/ppermute | solution.py:527
  2.3 4.4 %collective-permute-start.1 = (f32[333,128]{1,0:T(8,128)S(1)}, f32[333,128]{1,0:T(8,128)S(1)}, u32[]{:S(2)}, u32[]{:S(2)}) collective-permute-start(f32[333,128]{1,0:T(8,128)S(1)} %get-tuple-element.24), channel_id=1, source_target_pairs={{0,1},{2,3},{4,5},{6,7},{8,9},{10,11},{12,13},{14,15},{16,17},{18,... | collective-permute-start | bytes 511496 | tf_op jit(solution)/shard_map/ppermute | solution.py:528
  6.8 4.8 %all-to-all-start = ((f32[32,1,128]{2,1,0:T(1,128)}), f32[32,1,128]{2,1,0:T(1,128)S(1)}, u32[]{:S(2)}, u32[]{:S(2)}) async-start(f32[32,1,128]{2,1,0:T(1,128)} %bitcast.7), calls=%async_computation | async-start | bytes 32768 | tf_op jit(solution)/shard_map/all_to_all | solution.py:529
  11.6 1.7 %lay_out.1 = (f32[30,32,128]{2,1,0:T(8,128)S(1)}, f32[7,32,128]{2,1,0:T(8,128)S(1)}, bf16[120,96]{1,0:T(8,128)(2,1)S(1)}, f32[3,128]{1,0:T(4,128)S(1)}) custom-call(f32[10,3,4096]{2,1,0:T(4,128)} %bitcast.13, f32[32,128]{1,0:T(8,128)} %bitcast.15, f32[4,4096]{1,0:T(4,128)} %metric_hbm.3, s32[32,128]{1,0:T(8,128)} %bitcast.17, s32[32,128]{1,0:T(8,128)} %bitcast.19, ...), custom_call_target="tpu_custom_call" | custom-call | flops 16777216 | bytes 16777216 | tf_op jit(solution)/shard_map/lay_out/pallas_call | solution.py:531
  13.4 0.0 collective-permute-done.odd_ref
  13.4 0.0 collective-permute-done.1.even_ref
  13.4 4.8 %rates_twice.1 = (f32[30,72,128]{2,1,0:T(8,128)S(1)}, f32[30,72,128]{2,1,0:T(8,128)S(1)}, f32[30,48,128]{2,1,0:T(8,128)S(1)}, bf16[120,96]{1,0:T(8,128)(2,1)S(1)...) custom-call(f32[30,32,128]{2,1,0:T(8,128)S(1)} %get-tuple-element.19.cur_own, ...), custom_call_target="tpu_custom_call" | custom-call | flops 1024 | bytes 1024 | tf_op jit(solution)/shard_map/rates_twice/pallas_call | solution.py:555
  18.1 0.5 %all-to-all-done = f32[32,1,128]{2,1,0:T(1,128)S(1)} async-done(((f32[32,1,128]{2,1,0:T(1,128)}), f32[32,1,128]{2,1,0:T(1,128)S(1)}, u32[]{:S(2)}, u32[]{:S(2)}) %all-to-all-start) | async-done | bytes 16416 | tf_op jit(solution)/shard_map/all_to_all | solution.py:529
  18.7 2.3 %sum_and_refine.1 = f32[10,3,6144]{2,1,0:T(4,128)} custom-call(f32[30,72,128]{2,1,0:T(8,128)S(1)} %get-tuple-element.25.cur, f32[30,72,128]{2,1,0:T(8,128)S(1)} %get-tuple-element.26.rate_ref, f32[30,48,128]{2,1,0:T(8,128)S(1)} %get-tuple-element.27.twice_ref, bf16[120,96]{1,0:T(8,128)(2,1)S(1)} %get-tuple-element.28.weights, ...), custom_call_target="tpu_custom_call" | custom-call | tf_op jit(solution)/shard_map/sum_and_refine/pallas_call | solution.py:578
Async XLA Ops:
  1.7 11.7 %collective-permute-start = (f32[333,128]{1,0:T(8,128)S(1)}, f32[333,128]{1,0:T(8,128)S(1)}, u32[]{:S(2)}, u32[]{:S(2)}) collective-permute-start(f32[333,128]{1,0:T(8,128)S(1)} %get-tuple-element.23), channel_id=1, source_target_pairs={{1,2},{3,4},{5,6},{7,8},{9,10},{11,12},{13,14},{15,16},{17,18},{19... | collective-permute-start | bytes 511496 | tf_op jit(solution)/shard_map/ppermute | solution.py:527
  2.3 11.0 %collective-permute-start.1 = (f32[333,128]{1,0:T(8,128)S(1)}, f32[333,128]{1,0:T(8,128)S(1)}, u32[]{:S(2)}, u32[]{:S(2)}) collective-permute-start(f32[333,128]{1,0:T(8,128)S(1)} %get-tuple-element.24), channel_id=1, source_target_pairs={{0,1},{2,3},{4,5},{6,7},{8,9},{10,11},{12,13},{14,15},{16,17},{18,... | collective-permute-start | bytes 511496 | tf_op jit(solution)/shard_map/ppermute | solution.py:528
  6.8 11.9 %all-to-all-start = ((f32[32,1,128]{2,1,0:T(1,128)}), f32[32,1,128]{2,1,0:T(1,128)S(1)}, u32[]{:S(2)}, u32[]{:S(2)}) async-start(f32[32,1,128]{2,1,0:T(1,128)} %bitcast.7), calls=%async_computation | async-start | bytes 32768 | tf_op jit(solution)/shard_map/all_to_all | solution.py:529
